TPU v7x, 32 devices: a whole 2x2x4 slice. The times are simulated.
32 devices in a mesh: groups: 2 (over x), ep: 4 (over y, core), sub: 4 (over z).
Axes of the slice: x: 2, y: 2, z: 4, core: 2. Of those that a mesh axis runs over, the one named last changes fastest.
Arguments:
- tokens: bfloat16 [256, 7168], P(('groups', 'ep', 'sub')), parts along dimension 0, may hold values from -6 to 6
- routes: int32 [256, 2], P(('groups', 'ep', 'sub')), parts along dimension 0, may hold values from 0 to 3, all different within a row; in each aligned block of 8 rows (0 to 7, 8 to 15, ...) at most 4 rows name the same one
- gates: float32 [256, 2], P(('groups', 'ep', 'sub')), parts along dimension 0, may hold values from 0.05 to 1
- gate_weight: bfloat16 [4, 7168, 2048], P('ep', None, 'sub'), may hold values from -0.0625 to 0.0625
- up_weight: bfloat16 [4, 7168, 2048], P('ep', None, 'sub'), may hold values from -0.0625 to 0.0625
- down_weight: bfloat16 [4, 2048, 7168], P('ep', None, 'sub'), may hold values from -0.125 to 0.125
Outputs:
- combined: bfloat16 [256, 7168], P(('groups', 'ep', 'sub')), parts along dimension 0
There are 2 independent parts, one for each index of `groups`. A program takes and returns all parts, laid end to end along the dimension named above; an argument that names none is the same for every part. Nothing has to cross between parts.
Inputs may be any that keep to these rules, and one draw needn't show every extreme that they name: `routes`: each token names 2 different experts. Among the tokens of one device (aligned blocks of 8 rows) no expert is named more than 4 times, and in every draw some expert is named exactly 4 times in some such block.
All inputs are finite; a program needn't handle non-finite values.
Results may differ from a plain program's by a relative error of at most 0.0058.
Values may be sent and summed in bfloat16 or wider, within the bound.
No kernel may reach another device: no remote copies, remote signals or barrier semaphores. Data moves between devices by JAX's collectives and lax.ppermute only.
A program may use at most 128 MiB of HBM per device.

v0:
```python
import jax
import jax.numpy as jnp
from jax import lax
from jax.sharding import PartitionSpec as P


def body(tokens, routes, gates, gate_weight, up_weight, down_weight):
    experts = lax.axis_size("ep")
    groups = lax.axis_size("sub")
    count, width = tokens.shape
    chosen = routes.shape[1]
    slot_cap = count * chosen * 9 // (8 * experts)
    choose = (routes[:, :, None] == jnp.arange(experts, dtype=jnp.int32)[None, None, :]).astype(
        jnp.int32
    )
    present = jnp.sum(choose, axis=1)
    before = jnp.cumsum(present, axis=0) - present
    slots = jnp.sum(choose * before[:, None, :], axis=2)
    target = routes * slot_cap + slots
    select = (
        target[:, :, None] == jnp.arange(experts * slot_cap, dtype=jnp.int32)[None, None, :]
    ).astype(jnp.float32)
    placing = jnp.transpose(jnp.sum(select, axis=1)).astype(jnp.bfloat16)
    weighting = jnp.sum(select * gates[:, :, None], axis=1).reshape(count, experts, slot_cap)
    send_rows = jnp.dot(placing, tokens, preferred_element_type=jnp.float32).astype(jnp.bfloat16)
    send_rows = send_rows.reshape(experts, slot_cap, width)
    w_gate = gate_weight[0]
    w_up = up_weight[0]
    w_down = down_weight[0]
    wide_rows = jnp.broadcast_to(send_rows[:, None], (experts, groups, slot_cap, width))
    wide_rows = wide_rows.reshape(experts * groups, slot_cap, width)
    got_rows = lax.all_to_all(wide_rows, ("ep", "sub"), split_axis=0, concat_axis=0, tiled=True)
    rows = got_rows.reshape(-1, width)
    gate = jnp.dot(rows, w_gate, preferred_element_type=jnp.float32)
    up = jnp.dot(rows, w_up, preferred_element_type=jnp.float32)
    hidden = (jax.nn.silu(gate) * up).astype(jnp.bfloat16)
    out_cols = w_down.shape[1]
    result = jnp.dot(
        lax.all_gather(hidden, "sub", axis=1, tiled=True),
        w_down,
        preferred_element_type=jnp.float32,
    ).astype(jnp.bfloat16)
    returned = lax.all_to_all(
        result.reshape(experts * groups, slot_cap, out_cols),
        ("ep", "sub"),
        split_axis=0,
        concat_axis=2,
        tiled=True,
    )
    returned = returned.reshape(slot_cap, experts, width).astype(jnp.float32)
    combined = jnp.einsum("tec,ced->td", weighting, returned, precision=lax.Precision.HIGHEST)
    return combined.astype(jnp.bfloat16)


def solution(mesh):
    return jax.shard_map(
        body,
        mesh=mesh,
        in_specs=(
            P(("groups", "ep", "sub"), None),
            P(("groups", "ep", "sub"), None),
            P(("groups", "ep", "sub"), None),
            P("ep", None, "sub"),
            P("ep", None, "sub"),
            P("ep", None, "sub"),
        ),
        out_specs=P(("groups", "ep", "sub"), None),
        check_vma=False,
    )
```

profile of v0, /device:TPU:0, one launch (start us, length us, event | category | flops | bytes accessed | tf_op | source)
XLA Modules:
  0.0 74.2 jit_solution(4962411379704299218)
XLA Ops:
  0.0 0.0 copy-start
  0.0 0.7 convert_reduce_fusion.1
  0.7 0.2 reduce_window_sum.11
  0.9 0.7 select_reduce_fusion.1
  1.6 0.7 multiply_add_fusion
  2.3 0.8 %convert_reduce_fusion = (bf16[8,16]{1,0:T(8,128)(2,1)S(1)}, f32[8,16]{1,0:T(8,128)S(1)}) fusion(s32[8,2]{0,1:T(2,128)S(1)} %multiply_add_fusion, f32[8,2]{0,1:T(2,128)} %param.8), kind=kLoop, calls=%fused_computation.12 | loop fusion | flops 1024 | bytes 896 | tf_op jit(solution)/shard_map/reduce_sum | solution.py:23
  3.1 0.0 copy-done
  3.1 0.3 convolution_convert_fusion
  3.3 0.1 broadcast_in_dim.4
  3.4 0.2 broadcast_in_dim.5
  3.7 31.5 %all_to_all.20 = bf16[16,4,7168]{2,1,0:T(4,128)(2,1)} all-to-all(bf16[16,4,7168]{2,1,0:T(4,128)(2,1)S(1)} %bitcast.37), channel_id=1, replica_groups=mesh['groups'=2,'ep'=4,'sub'=4] {'ep','sub'}, dimensions={0} | all-to-all | bytes 1835008 | tf_op jit(solution)/shard_map/all_to_all | solution.py:32
  35.1 0.0 slice-start
  35.1 2.5 %reshape.31 = bf16[64,7168]{1,0:T(8,128)(2,1)} reshape(bf16[16,4,7168]{2,1,0:T(4,128)(2,1)} %all_to_all.20) | data formatting | bytes 1835008 | tf_op jit(solution)/shard_map/reshape | solution.py:33
  37.7 0.0 slice-start.1
  37.7 0.0 copy-start.1
  37.7 0.0 slice-start.2
  37.7 4.9 %fusion.5 = f32[64,512]{1,0:T(8,128)S(1)} fusion(bf16[64,7168]{1,0:T(8,128)(2,1)} %reshape.31, bf16[1,7168,512]{2,1,0:T(8,128)(2,1)} %param.9), kind=kOutput, calls=%fused_computation.7 | convolution fusion | flops 469762048 | bytes 8388608 | tf_op jit(solution)/shard_map/dot_general | solution.py:34
  42.6 0.0 slice-done
  42.6 0.0 slice-done.1
  42.6 0.0 copy-done.1
  42.6 0.0 slice-start.3
  42.6 1.4 %fusion.13 = bf16[64,512]{1,0:T(8,128)(2,1)S(1)} fusion(bf16[64,7168]{1,0:T(8,128)(2,1)S(1)} %copy-done.1, bf16[1,7168,512]{2,1,0:T(8,128)(2,1)S(1)} %bitcast.34, f32[64,512]{1,0:T(8,128)S(1)} %fusion.5), kind=kOutput, calls=%fused_computation.11 | convolution fusion | flops 469958656 | bytes 8454144 | tf_op jit(solution)/shard_map/dot_general | solution.py:35
  44.0 14.5 %all_gather.3 = bf16[64,2048]{1,0:T(8,128)(2,1)S(1)} all-gather(bf16[64,512]{1,0:T(8,128)(2,1)S(1)} %fusion.13), channel_id=1, replica_groups=mesh['groups'=2,'ep'=4,'sub'=4] {'sub'}, dimensions={1}, use_global_device_ids=true | all-gather | bytes 327680 | tf_op jit(solution)/shard_map/all_gather | solution.py:39
  58.5 0.0 slice-done.2
  58.5 0.0 slice-done.3
  58.5 1.4 %fusion.7 = bf16[64,1792]{1,0:T(8,128)(2,1)S(1)} fusion(bf16[64,2048]{1,0:T(8,128)(2,1)S(1)} %all_gather.3, bf16[1,2048,1792]{2,1,0:T(8,128)(2,1)S(1)} %bitcast.36), kind=kOutput, calls=%fused_computation.9 | convolution fusion | flops 469876736 | bytes 7831552 | tf_op jit(solution)/shard_map/dot_general | solution.py:38
  59.8 0.7 %reshape.32 = bf16[16,4,1792]{2,1,0:T(4,128)(2,1)} reshape(bf16[64,1792]{1,0:T(8,128)(2,1)S(1)} %fusion.7) | data formatting | bytes 458752 | tf_op jit(solution)/shard_map/reshape | solution.py:44
  60.6 3.5 %all-to-all-start.1 = ((bf16[16,4,1792]{2,1,0:T(4,128)(2,1)}), bf16[16,4,1792]{2,1,0:T(4,128)(2,1)S(1)}, u32[]{:S(2)}, u32[]{:S(2)}) async-start(bf16[16,4,1792]{2,1,0:T(4,128)(2,1)} %reshape.32), calls=%async_computation.1 | async-start | bytes 458752 | tf_op jit(solution)/shard_map/all_to_all | solution.py:43
  64.1 0.1 copy.12
  64.2 8.9 %all-to-all-done.1 = bf16[16,4,1792]{2,1,0:T(4,128)(2,1)S(1)} async-done(((bf16[16,4,1792]{2,1,0:T(4,128)(2,1)}), bf16[16,4,1792]{2,1,0:T(4,128)(2,1)S(1)}, u32[]{:S(2)}, u32[]{:S(2)}) %all-to-all-start.1) | async-done | bytes 229408 | tf_op jit(solution)/shard_map/all_to_all | solution.py:43
  73.1 1.1 %fusion = bf16[8,7168]{1,0:T(8,128)(2,1)} fusion(f32[8,4,4]{0,2,1:T(4,128)S(1)} %bitcast.39, bf16[4,4,7168]{2,0,1:T(4,128)(2,1)S(1)} %bitcast.38), kind=kOutput, calls=%fused_computation.2 | convolution fusion | flops 11067392 | bytes 344576 | tf_op jit(solution)/shard_map/tec,ced->td/dot_general | solution.py:51
  (3 shorter events, 0.0 us)
Async XLA Ops:
  0.0 3.1 %copy-start = (bf16[8,7168]{1,0:T(8,128)(2,1)S(1)}, bf16[8,7168]{1,0:T(8,128)(2,1)}, u32[]{:S(2)}) copy-start(bf16[8,7168]{1,0:T(8,128)(2,1)} %param.6) | copy-start | bytes 344068
  35.1 7.4 %slice-start = ((s8[7340032]{0:T(1024)(128)(4,1)}), s8[3145728]{0:T(1024)(128)(4,1)S(1)}, s32[]{:S(2)}) async-start(s8[7340032]{0:T(1024)(128)(4,1)} %bitcast.33), calls=%async_computation.2 | async-start | bytes 6291456
  37.7 4.9 %slice-start.1 = ((s8[7340032]{0:T(1024)(128)(4,1)}), s8[4194304]{0:T(1024)(128)(4,1)S(1)}, s32[]{:S(2)}) async-start(s8[7340032]{0:T(1024)(128)(4,1)} %bitcast.33), calls=%async_computation.3 | async-start | bytes 8388608
  37.7 4.9 %copy-start.1 = (bf16[64,7168]{1,0:T(8,128)(2,1)S(1)}, bf16[64,7168]{1,0:T(8,128)(2,1)}, u32[]{:S(2)}) copy-start(bf16[64,7168]{1,0:T(8,128)(2,1)} %reshape.31) | copy-start | bytes 2752516
  37.7 20.8 %slice-start.2 = ((s8[7340032]{0:T(1024)(128)(4,1)}), s8[4194304]{0:T(1024)(128)(4,1)S(1)}, s32[]{:S(2)}) async-start(s8[7340032]{0:T(1024)(128)(4,1)} %bitcast.35), calls=%async_computation.4 | async-start | bytes 8388608
  42.6 15.9 %slice-start.3 = ((s8[7340032]{0:T(1024)(128)(4,1)}), s8[3145728]{0:T(1024)(128)(4,1)S(1)}, s32[]{:S(2)}) async-start(s8[7340032]{0:T(1024)(128)(4,1)} %bitcast.35), calls=%async_computation.5 | async-start | bytes 6291456
  60.6 12.5 %all-to-all-start.1 = ((bf16[16,4,1792]{2,1,0:T(4,128)(2,1)}), bf16[16,4,1792]{2,1,0:T(4,128)(2,1)S(1)}, u32[]{:S(2)}, u32[]{:S(2)}) async-start(bf16[16,4,1792]{2,1,0:T(4,128)(2,1)} %reshape.32), calls=%async_computation.1 | async-start | bytes 458752 | tf_op jit(solution)/shard_map/all_to_all | solution.py:43
where the time goes:
time: 74.5 us; the launch traced here: 74.2 us
  blocking collectives  45.9 us (62%)
  matrix products  8.95 us (12%)
  waiting for transfers between devices  8.94 us (12%)
  local copies, waits for them, and re-layouts  3.72 us (5%)
  starting transfers between devices  3.53 us (5%)
  other arithmetic  3.05 us (4%)
    all_to_all x1, blocking collectives, body(): lax.all_to_all(wide_rows, ('ep', 'sub'), split_axis=0, concat_axis=0, til...  31.5 us
    all_gather x1, blocking collectives, body(): lax.all_gather(hidden, 'sub', axis=1, tiled=True)  14.5 us
    all_to_all x1, waiting for transfers between devices, body(): lax.all_to_all(result.reshape(experts * groups, slot_cap, out_cols), ('ep...  8.94 us
    dot_general x1, matrix products, body(): gate = jnp.dot(rows, w_gate, preferred_element_type=jnp.float32)  4.88 us
    all_to_all x1, starting transfers between devices, body(): lax.all_to_all(result.reshape(experts * groups, slot_cap, out_cols), ('ep...  3.53 us
    reshape x1, local copies, waits for them, and re-layouts, body(): rows = got_rows.reshape(-1, width)  2.55 us
  transfers between devices with their start and end apart: 1, of which 1 were waited for; matrix products, arithmetic and copies ran while one was open for 0% of the time, Pallas kernels for 0%

commit v1 on v0

v1 whole, which is shorter than its diff:
```python
import functools

import jax
import jax.numpy as jnp
from jax import lax
from jax.experimental import pallas as pl
from jax.experimental.pallas import tpu as pltpu
from jax.sharding import PartitionSpec as P

LANES = 128


def swap(x, axis, size, k):
    return lax.ppermute(x, axis, [(i, i ^ k) for i in range(size)])


def pack_kernel(tokens, routes, out):
    count, width = tokens.shape
    chosen = routes.shape[0]
    out[:, :width] = tokens[...]
    diagonal = lax.broadcasted_iota(jnp.int32, (count, count), 0) == lax.broadcasted_iota(
        jnp.int32, (count, count), 1
    )
    lane = lax.broadcasted_iota(jnp.int32, (count, LANES), 1)
    meta = jnp.zeros((count, LANES), jnp.float32)
    for k in range(chosen):
        named = jnp.broadcast_to(routes[k:k + 1, :], (count, count)).astype(jnp.float32)
        named = jnp.sum(jnp.where(diagonal, named, 0.0), axis=1, keepdims=True)
        meta = jnp.where(lane == k, named, meta)
    out[:, width:] = meta.astype(jnp.bfloat16)


def up_kernel(count, chosen, cap, chunk, width, where, *refs):
    n = (len(refs) - 4)
    blocks, (w_gate, w_up, out, xs) = refs[:n], refs[n:]
    columns = out.shape[1]
    rows = count * chunk
    slots = cap * chunk
    expert, me = where[0], where[1]
    for b in range(0, n, 2):
        pair = jnp.concatenate([blocks[b][...], blocks[b + 1][...]], axis=0)
        xs[b * count:(b + 2) * count, :] = pair
    step = min(256, columns)

    def part(j, carry):
        at = pl.multiple_of(j * rows, rows)
        meta = jnp.transpose(xs[pl.ds(at, rows), width:width + LANES].astype(jnp.float32))
        row = lax.broadcasted_iota(jnp.int32, (LANES, rows), 0)
        named = (row < chosen) & (meta == expert.astype(jnp.float32))
        present = jnp.max(named.astype(jnp.float32), axis=0, keepdims=True)
        a = lax.broadcasted_iota(jnp.int32, (rows, rows), 0)
        b = lax.broadcasted_iota(jnp.int32, (rows, rows), 1)
        earlier = ((a // count == b // count) & (a < b)).astype(jnp.float32).astype(jnp.bfloat16)
        many = jnp.broadcast_to(present, (slots, rows))
        rank = jnp.dot(many.astype(jnp.bfloat16), earlier, preferred_element_type=jnp.float32)
        slot = lax.broadcasted_iota(jnp.int32, (slots, rows), 0)
        token = lax.broadcasted_iota(jnp.int32, (slots, rows), 1)
        owner = (token // count) ^ (me % chunk)
        pick = (slot // cap == owner) & ((slot % cap).astype(jnp.float32) == rank) & (many > 0.5)
        pick = pick.astype(jnp.float32).astype(jnp.bfloat16)
        to = pl.multiple_of((j ^ (me // chunk)) * slots, slots)
        for c in range(0, columns, step):
            x = xs[pl.ds(at, rows), :width]
            gate = jnp.dot(x, w_gate[0, :, c:c + step], preferred_element_type=jnp.float32)
            up = jnp.dot(x, w_up[0, :, c:c + step], preferred_element_type=jnp.float32)
            hidden = (gate / (1.0 + jnp.exp(-gate)) * up).astype(jnp.bfloat16)
            chosen_rows = jnp.dot(pick, hidden, preferred_element_type=jnp.float32)
            out[pl.ds(to, slots), c:c + step] = chosen_rows.astype(jnp.bfloat16)
        return carry

    lax.fori_loop(0, n // chunk, part, 0)


def down_kernel(where, *refs):
    n = len(refs) - 2
    parts, w_down, out = refs[:n], refs[n], refs[n + 1]
    depth = parts[0].shape[1]
    rows, columns = out.shape
    sub = where[0]
    step = 256 if columns % 256 == 0 else 128
    rstep = min(rows, 128)

    def part(j, carry):
        at = pl.multiple_of(j * rstep, rstep)
        for c in range(0, columns, step):
            total = None
            for k in range(n):
                d = pl.multiple_of((sub ^ k) * depth, depth)
                term = jnp.dot(
                    parts[k][pl.ds(at, rstep), :],
                    w_down[0, pl.ds(d, depth), c:c + step],
                    preferred_element_type=jnp.float32,
                )
                total = term if total is None else total + term
            out[pl.ds(at, rstep), c:c + step] = total.astype(jnp.bfloat16)
        return carry

    lax.fori_loop(0, rows // rstep, part, 0)


def body(tokens, routes, gates, gate_weight, up_weight, down_weight):
    experts = lax.axis_size("ep")
    groups = lax.axis_size("sub")
    ep, sub = lax.axis_index("ep"), lax.axis_index("sub")
    count, width = tokens.shape
    chosen = routes.shape[1]
    slot_cap = count * chosen * 9 // (8 * experts)
    devices = experts * groups

    vmem = pl.BlockSpec(memory_space=pltpu.VMEM)
    smem = pl.BlockSpec(memory_space=pltpu.SMEM)
    own = pl.pallas_call(
        pack_kernel,
        out_shape=jax.ShapeDtypeStruct((count, width + LANES), jnp.bfloat16),
        in_specs=[vmem, vmem],
        out_specs=vmem,
        cost_estimate=pl.CostEstimate(flops=20 * 10**9, bytes_accessed=0, transcendentals=0),
        compiler_params=pltpu.CompilerParams(vmem_limit_bytes=1 << 20),
        name="pack",
    )(tokens, routes.T)
    got = {(0, 0): own}
    for kz in sorted(range(1, groups), reverse=True):
        got[kz, 0] = swap(own, "sub", groups, kz)
    for kz in range(groups):
        for ky in range(2, experts, 2):
            got[kz, ky] = swap(got[kz, 0], "ep", experts, ky)
    for kz in range(groups):
        for ky in range(0, experts, 2):
            got[kz, ky + 1] = swap(got[kz, ky], "ep", experts, 1)
    blocks = [got[kz, ke] for ke in range(experts) for kz in range(groups)]

    columns = gate_weight.shape[2]
    chunk = min(16, devices)
    where = jnp.stack([ep, ep * groups + sub]).astype(jnp.int32)
    hidden = pl.pallas_call(
        functools.partial(up_kernel, count, chosen, slot_cap, chunk, width),
        out_shape=jax.ShapeDtypeStruct((devices * slot_cap, columns), jnp.bfloat16),
        in_specs=[smem] + [vmem] * (devices + 2),
        out_specs=vmem,
        scratch_shapes=[pltpu.VMEM((devices * count, width + LANES), jnp.bfloat16)],
        compiler_params=pltpu.CompilerParams(vmem_limit_bytes=(20 << 20) * (1 if devices <= 16 else 2)),
        name="gate_up",
    )(where, *blocks, gate_weight, up_weight)

    parts = [hidden] + [swap(hidden, "sub", groups, k) for k in range(1, groups)]
    out_cols = down_weight.shape[2]
    result = pl.pallas_call(
        down_kernel,
        out_shape=jax.ShapeDtypeStruct((devices * slot_cap, out_cols), jnp.bfloat16),
        in_specs=[smem] + [vmem] * (groups + 1),
        out_specs=vmem,
        compiler_params=pltpu.CompilerParams(vmem_limit_bytes=16 << 20),
        name="down",
    )(sub[None].astype(jnp.int32), *parts, down_weight)

    choose = (routes[:, :, None] == jnp.arange(experts, dtype=jnp.int32)[None, None, :]).astype(jnp.int32)
    present = jnp.sum(choose, axis=1)
    before = jnp.cumsum(present, axis=0) - present
    slots = jnp.sum(choose * before[:, None, :], axis=2)
    target = routes * slot_cap + slots
    select = (
        target[:, :, None] == jnp.arange(experts * slot_cap, dtype=jnp.int32)[None, None, :]
    ).astype(jnp.float32)
    weighting = jnp.sum(select * gates[:, :, None], axis=1).reshape(count, experts, slot_cap)
    returned = lax.all_to_all(
        result.reshape(devices, slot_cap, out_cols),
        ("ep", "sub"),
        split_axis=0,
        concat_axis=2,
        tiled=True,
    )
    returned = returned.reshape(slot_cap, experts, width).astype(jnp.float32)
    combined = jnp.einsum("tec,ced->td", weighting, returned, precision=lax.Precision.HIGHEST)
    return combined.astype(jnp.bfloat16)


def solution(mesh):
    return jax.shard_map(
        body,
        mesh=mesh,
        in_specs=(
            P(("groups", "ep", "sub"), None),
            P(("groups", "ep", "sub"), None),
            P(("groups", "ep", "sub"), None),
            P("ep", None, "sub"),
            P("ep", None, "sub"),
            P("ep", None, "sub"),
        ),
        out_specs=P(("groups", "ep", "sub"), None),
        check_vma=False,
    )
```

time: 74.5 us -> 63.5 us (0.85)
  blocking collectives: 45.9 us -> 0 us
  starting transfers between devices: 3.53 us -> 20.9 us
  waiting for transfers between devices: 8.94 us -> 24.3 us
  local copies, waits for them, and re-layouts: 3.72 us -> 11.7 us
  matrix products: 8.95 us -> 1.08 us
  Pallas kernels: 0 us -> 4.7 us
  other arithmetic: 3.05 us -> 0.38 us
    all_to_all x1 -> x0, blocking collectives: 31.5 us -> none  [body(): lax.all_to_all(wide_rows, ('ep', 'sub'), split_axis=0, concat_axis=0, til...]
    ppermute x0 -> x18, starting transfers between devices: none -> 16.7 us  [swap(): return lax.ppermute(x, axis, [(i, i ^ k) for i in range(size)])]
    ppermute x0 -> x18, waiting for transfers between devices: none -> 15.3 us  [swap(): return lax.ppermute(x, axis, [(i, i ^ k) for i in range(size)])]
    all_gather x1 -> x0, blocking collectives: 14.5 us -> none  [body(): lax.all_gather(hidden, 'sub', axis=1, tiled=True)]
    unnamed x12 -> x14, local copies, waits for them, and re-layouts: 0.03 us -> 10.8 us
    dot_general x4 -> x0, matrix products: 7.87 us -> none  [the longest x1 4.88 us: body(): gate = jnp.dot(rows, w_gate, preferred_element_type=jnp.float32)]
    pallas_call x0 -> x3, Pallas kernels: none -> 4.7 us  [the longest x1 3.23 us: body(): pl.pallas_call(functools.partial(up_kernel, count, chosen, slot_cap, chun...]
    reshape x2 -> x1, local copies, waits for them, and re-layouts: 3.29 us -> 0.74 us  [body(): result.reshape(devices, slot_cap, out_cols)]
  transfers between devices with their start and end apart: 1 -> 19, of which waited for: 1 -> 11; matrix products, arithmetic and copies ran while one was open for 0% -> 1% of each run, Pallas kernels for 0% -> 0%
where the time goes in v1:
time: 63.5 us; the launch traced here: 63.1 us
  waiting for transfers between devices  24.3 us (38%)
  starting transfers between devices  20.9 us (33%)
  local copies, waits for them, and re-layouts  11.7 us (18%)
  Pallas kernels  4.7 us (7%)
  matrix products  1.08 us (2%)
    ppermute x18, starting transfers between devices, swap(): return lax.ppermute(x, axis, [(i, i ^ k) for i in range(size)])  16.7 us
    ppermute x18, waiting for transfers between devices, swap(): return lax.ppermute(x, axis, [(i, i ^ k) for i in range(size)])  15.3 us
    unnamed x14, local copies, waits for them, and re-layouts  10.8 us
    all_to_all x1, waiting for transfers between devices, body(): lax.all_to_all(result.reshape(devices, slot_cap, out_cols), ('ep', 'sub')...  9.02 us
    all_to_all x1, starting transfers between devices, body(): lax.all_to_all(result.reshape(devices, slot_cap, out_cols), ('ep', 'sub')...  4.19 us
    pallas_call x1, Pallas kernels, body(): pl.pallas_call(functools.partial(up_kernel, count, chosen, slot_cap, chun...  3.23 us
    pallas_call x1, Pallas kernels, body(): pl.pallas_call(down_kernel, out_shape=jax.ShapeDtypeStruct((devices * slo...  1.38 us
  transfers between devices with their start and end apart: 19, of which 11 were waited for; matrix products, arithmetic and copies ran while one was open for 1% of the time, Pallas kernels for 0%

profile of v1, /device:TPU:0, one launch (start us, length us, event | category | flops | bytes accessed | tf_op | source)
XLA Modules:
  0.0 63.1 jit_solution(354335415499410651)
XLA Ops:
  0.0 0.0 copy-start.3
  0.0 0.7 %copy-done.3 = s32[8,2]{0,1:T(2,128)S(1)} copy-done((s32[8,2]{0,1:T(2,128)S(1)}, s32[8,2]{0,1:T(2,128)}, u32[]{:S(2)}) %copy-start.3) | copy-done | bytes 88
  0.7 0.0 copy-start.5
  0.7 0.9 %copy-done.5 = bf16[8,7168]{1,0:T(8,128)(2,1)S(1)} copy-done((bf16[8,7168]{1,0:T(8,128)(2,1)S(1)}, bf16[8,7168]{1,0:T(8,128)(2,1)}, u32[]{:S(2)}) %copy-start.5) | copy-done | bytes 114712
  1.6 0.1 pack.1.refs_0_
  1.7 3.0 %collective-permute-start = (bf16[8,7296]{1,0:T(8,128)(2,1)S(1)}, bf16[8,7296]{1,0:T(8,128)(2,1)S(1)}, u32[]{:S(2)}, u32[]{:S(2)}) collective-permute-start(bf16[8,7296]{1,0:T(8,128)(2,1)S(1)} %pack.1.refs_0_), channel_id=1, source_target_pairs={{0,1},{1,0},{2,3},{3,2},{4,5},{5,4},{6,7},{7,6},{8,9},{9,8},{10,11... | collective-permute-start | bytes 350216 | tf_op jit(solution)/shard_map/ppermute | solution.py:14
  4.7 2.6 %collective-permute-start.1 = (bf16[8,7296]{1,0:T(8,128)(2,1)S(1)}, bf16[8,7296]{1,0:T(8,128)(2,1)S(1)}, u32[]{:S(2)}, u32[]{:S(2)}) collective-permute-start(bf16[8,7296]{1,0:T(8,128)(2,1)S(1)} %pack.1.refs_0_), channel_id=1, source_target_pairs={{0,2},{1,3},{2,0},{3,1},{4,6},{5,7},{6,4},{7,5},{8,10},{9,11},{10,... | collective-permute-start | bytes 350216 | tf_op jit(solution)/shard_map/ppermute | solution.py:14
  7.3 0.0 collective-permute-start.2
  7.3 1.7 %collective-permute-start.7 = (bf16[8,7296]{1,0:T(8,128)(2,1)S(1)}, bf16[8,7296]{1,0:T(8,128)(2,1)S(1)}, u32[]{:S(2)}, u32[]{:S(2)}) collective-permute-start(bf16[8,7296]{1,0:T(8,128)(2,1)S(1)} %pack.1.refs_0_), channel_id=1, source_target_pairs={{0,8},{4,12},{8,0},{12,4},{1,9},{5,13},{9,1},{13,5},{2,10},{6,14},... | collective-permute-start | bytes 350216 | tf_op jit(solution)/shard_map/ppermute | solution.py:14
  9.0 0.0 collective-permute-start.3
  9.0 0.1 collective-permute-done.refs_1_
  9.1 1.7 %collective-permute-start.8 = (bf16[8,7296]{1,0:T(8,128)(2,1)S(1)}, bf16[8,7296]{1,0:T(8,128)(2,1)S(1)}, u32[]{:S(2)}, u32[]{:S(2)}) collective-permute-start(bf16[8,7296]{1,0:T(8,128)(2,1)S(1)} %collective-permute-done.refs_1_), channel_id=1, source_target_pairs={{0,8},{4,12},{8,0},{12,4},{1,9},{5,13},{9,1},{13,5},{2,10},{6,14},... | collective-permute-start | bytes 350216 | tf_op jit(solution)/shard_map/ppermute | solution.py:14
  10.8 5.7 %collective-permute-done.1.refs_2_ = bf16[8,7296]{1,0:T(8,128)(2,1)S(1)} collective-permute-done((bf16[8,7296]{1,0:T(8,128)(2,1)S(1)}, bf16[8,7296]{1,0:T(8,128)(2,1)S(1)}, u32[]{:S(2)}, u32[]{:S(2)}) %collective-permute-start.1) | collective-permute-done | bytes 116768 | tf_op jit(solution)/shard_map/ppermute | solution.py:14
  16.5 1.5 %collective-permute-start.9 = (bf16[8,7296]{1,0:T(8,128)(2,1)S(1)}, bf16[8,7296]{1,0:T(8,128)(2,1)S(1)}, u32[]{:S(2)}, u32[]{:S(2)}) collective-permute-start(bf16[8,7296]{1,0:T(8,128)(2,1)S(1)} %collective-permute-done.1.refs_2_), channel_id=1, source_target_pairs={{0,8},{4,12},{8,0},{12,4},{1,9},{5,13},{9,1},{13,5},{2,10},{6,14},... | collective-permute-start | bytes 350216 | tf_op jit(solution)/shard_map/ppermute | solution.py:14
  18.1 0.0 collective-permute-done.2.refs_3_
  18.1 0.5 collective-permute-start.10
  18.6 0.0 collective-permute-done.7.refs_8_
  18.6 0.0 collective-permute-start.4
  18.6 0.0 collective-permute-done.3.refs_4_
  18.6 0.5 collective-permute-start.5
  19.1 0.0 collective-permute-done.8.refs_9_
  19.1 0.1 collective-permute-start.6
  19.2 2.2 %collective-permute-done.9.refs_10_ = bf16[8,7296]{1,0:T(8,128)(2,1)S(1)} collective-permute-done((bf16[8,7296]{1,0:T(8,128)(2,1)S(1)}, bf16[8,7296]{1,0:T(8,128)(2,1)S(1)}, u32[]{:S(2)}, u32[]{:S(2)}) %collective-permute-start.9) | collective-permute-done | bytes 116768 | tf_op jit(solution)/shard_map/ppermute | solution.py:14
  21.4 0.0 collective-permute-start.11
  21.4 1.5 %collective-permute-done.10.refs_11_ = bf16[8,7296]{1,0:T(8,128)(2,1)S(1)} collective-permute-done((bf16[8,7296]{1,0:T(8,128)(2,1)S(1)}, bf16[8,7296]{1,0:T(8,128)(2,1)S(1)}, u32[]{:S(2)}, u32[]{:S(2)}) %collective-permute-start.10) | collective-permute-done | bytes 116768 | tf_op jit(solution)/shard_map/ppermute | solution.py:14
  22.9 0.0 collective-permute-start.12
  22.9 0.0 collective-permute-done.4.refs_5_
  22.9 0.5 collective-permute-start.13
  23.4 0.0 collective-permute-done.5.refs_6_
  23.4 0.1 collective-permute-start.14
  23.5 0.0 copy-start.4
  23.5 0.1 pad_add_fusion.where
  23.5 0.0 collective-permute-done.6.refs_7_
  23.5 0.0 collective-permute-done.11.refs_12_
  23.5 0.7 %collective-permute-done.12.refs_13_ = bf16[8,7296]{1,0:T(8,128)(2,1)S(1)} collective-permute-done((bf16[8,7296]{1,0:T(8,128)(2,1)S(1)}, bf16[8,7296]{1,0:T(8,128)(2,1)S(1)}, u32[]{:S(2)}, u32[]{:S(2)}) %collective-permute-start.12) | collective-permute-done | bytes 116768 | tf_op jit(solution)/shard_map/ppermute | solution.py:14
  24.2 0.2 collective-permute-done.13.refs_14_
  24.4 0.4 collective-permute-done.14.refs_15_
  24.7 0.0 copy-start
  24.7 3.1 %copy-done = bf16[1,7168,512]{2,1,0:T(8,128)(2,1)S(1)} copy-done((bf16[1,7168,512]{2,1,0:T(8,128)(2,1)S(1)}, bf16[1,7168,512]{2,1,0:T(8,128)(2,1)}, u32[]{:S(2)}) %copy-start) | copy-done | bytes 7340056
  27.8 0.0 copy-start.1
  27.8 3.1 %copy-done.1 = bf16[1,7168,512]{2,1,0:T(8,128)(2,1)S(1)} copy-done((bf16[1,7168,512]{2,1,0:T(8,128)(2,1)S(1)}, bf16[1,7168,512]{2,1,0:T(8,128)(2,1)}, u32[]{:S(2)}) %copy-start.1) | copy-done | bytes 7340056
  30.9 3.2 %gate_up.1.refs_0_ = bf16[64,512]{1,0:T(8,128)(2,1)S(1)} custom-call(s32[2]{0:T(128)S(1)} %pad_add_fusion.where, bf16[8,7296]{1,0:T(8,128)(2,1)S(1)} %pack.1.refs_0_, bf16[8,7296]{1,0:T(8,128)(2,1)S(1)} %collective-permute-done.refs_1_, bf16[8,7296]{1,0:T(8,128)(2,1)S(1)} %collective-permute-done.1.refs_2_, ...), custom_call_target="tpu_custom_call" | custom-call | tf_op jit(solution)/shard_map/gate_up/pallas_call | solution.py:135
  34.1 0.0 copy-start.6
  34.1 0.4 collective-permute-start.15
  34.5 2.7 %collective-permute-start.16 = (bf16[64,512]{1,0:T(8,128)(2,1)S(1)}, bf16[64,512]{1,0:T(8,128)(2,1)S(1)}, u32[]{:S(2)}, u32[]{:S(2)}) collective-permute-start(bf16[64,512]{1,0:T(8,128)(2,1)S(1)} %gate_up.1.refs_0_), channel_id=1, source_target_pairs={{0,2},{1,3},{2,0},{3,1},{4,6},{5,7},{6,4},{7,5},{8,10},{9,11},{10,... | collective-permute-start | bytes 196616 | tf_op jit(solution)/shard_map/ppermute | solution.py:14
  37.2 1.4 %collective-permute-start.17 = (bf16[64,512]{1,0:T(8,128)(2,1)S(1)}, bf16[64,512]{1,0:T(8,128)(2,1)S(1)}, u32[]{:S(2)}, u32[]{:S(2)}) collective-permute-start(bf16[64,512]{1,0:T(8,128)(2,1)S(1)} %gate_up.1.refs_0_), channel_id=1, source_target_pairs={{0,3},{1,2},{2,1},{3,0},{4,7},{5,6},{6,5},{7,4},{8,11},{9,10},{10,... | collective-permute-start | bytes 196616 | tf_op jit(solution)/shard_map/ppermute | solution.py:14
  38.6 0.0 copy-done.4
  38.6 0.2 reduce_window_sum.11
  38.8 0.5 collective-permute-done.15.refs_1_
  39.3 3.0 %collective-permute-done.16.refs_2_ = bf16[64,512]{1,0:T(8,128)(2,1)S(1)} collective-permute-done((bf16[64,512]{1,0:T(8,128)(2,1)S(1)}, bf16[64,512]{1,0:T(8,128)(2,1)S(1)}, u32[]{:S(2)}, u32[]{:S(2)}) %collective-permute-start.16) | collective-permute-done | bytes 65568 | tf_op jit(solution)/shard_map/ppermute | solution.py:14
  42.4 1.0 %collective-permute-done.17.refs_3_ = bf16[64,512]{1,0:T(8,128)(2,1)S(1)} collective-permute-done((bf16[64,512]{1,0:T(8,128)(2,1)S(1)}, bf16[64,512]{1,0:T(8,128)(2,1)S(1)}, u32[]{:S(2)}, u32[]{:S(2)}) %collective-permute-start.17) | collective-permute-done | bytes 65568 | tf_op jit(solution)/shard_map/ppermute | solution.py:14
  43.4 0.0 copy-start.2
  43.4 3.1 %copy-done.2 = bf16[1,2048,1792]{2,1,0:T(8,128)(2,1)S(1)} copy-done((bf16[1,2048,1792]{2,1,0:T(8,128)(2,1)S(1)}, bf16[1,2048,1792]{2,1,0:T(8,128)(2,1)}, u32[]{:S(2)}) %copy-start.2) | copy-done | bytes 7340056
  46.5 1.4 %down.1 = bf16[64,1792]{1,0:T(8,128)(2,1)S(1)} custom-call(s32[1]{0:T(128)} %bitcast.1.where, bf16[64,512]{1,0:T(8,128)(2,1)S(1)} %gate_up.1.refs_0_, bf16[64,512]{1,0:T(8,128)(2,1)S(1)} %collective-permute-done.15.refs_1_, bf16[64,512]{1,0:T(8,128)(2,1)S(1)} %collective-permute-done.16.refs_2_, bf16[64,512]{1,0:T(8,128)(2,1)S(1)} %collective-permute-done.17.refs_3_, ...), custom_call_target="tpu_custom_call" | custom-call | tf_op jit(solution)/shard_map/down/pallas_call | solution.py:147
  47.9 0.7 %reshape.23 = bf16[16,4,1792]{2,1,0:T(4,128)(2,1)} reshape(bf16[64,1792]{1,0:T(8,128)(2,1)S(1)} %down.1) | data formatting | bytes 458752 | tf_op jit(solution)/shard_map/reshape | solution.py:166
  48.6 4.2 %all-to-all-start = ((bf16[16,4,1792]{2,1,0:T(4,128)(2,1)}), bf16[16,4,1792]{2,1,0:T(4,128)(2,1)S(1)}, u32[]{:S(2)}, u32[]{:S(2)}) async-start(bf16[16,4,1792]{2,1,0:T(4,128)(2,1)} %reshape.23), calls=%async_computation | async-start | bytes 458752 | tf_op jit(solution)/shard_map/all_to_all | solution.py:165
  52.9 0.0 copy-done.6
  52.9 0.1 select_reduce_fusion
  52.9 0.1 copy.12
  53.0 9.0 %all-to-all-done = bf16[16,4,1792]{2,1,0:T(4,128)(2,1)S(1)} async-done(((bf16[16,4,1792]{2,1,0:T(4,128)(2,1)}), bf16[16,4,1792]{2,1,0:T(4,128)(2,1)S(1)}, u32[]{:S(2)}, u32[]{:S(2)}) %all-to-all-start) | async-done | bytes 229408 | tf_op jit(solution)/shard_map/all_to_all | solution.py:165
  62.0 1.1 %fusion = bf16[8,7168]{1,0:T(8,128)(2,1)} fusion(f32[8,4,4]{0,2,1:T(4,128)S(1)} %bitcast.18, bf16[4,4,7168]{2,0,1:T(4,128)(2,1)S(1)} %bitcast.17), kind=kOutput, calls=%fused_computation.1 | convolution fusion | flops 11067392 | bytes 344576 | tf_op jit(solution)/shard_map/tec,ced->td/dot_general | solution.py:173
  (4 shorter events, 0.0 us)
Async XLA Ops:
  0.0 0.7 %copy-start.3 = (s32[8,2]{0,1:T(2,128)S(1)}, s32[8,2]{0,1:T(2,128)}, u32[]{:S(2)}) copy-start(s32[8,2]{0,1:T(2,128)} %param.7) | copy-start | bytes 196
  0.7 0.9 %copy-start.5 = (bf16[8,7168]{1,0:T(8,128)(2,1)S(1)}, bf16[8,7168]{1,0:T(8,128)(2,1)}, u32[]{:S(2)}) copy-start(bf16[8,7168]{1,0:T(8,128)(2,1)} %tokens.1) | copy-start | bytes 344068
  1.7 7.4 %collective-permute-start = (bf16[8,7296]{1,0:T(8,128)(2,1)S(1)}, bf16[8,7296]{1,0:T(8,128)(2,1)S(1)}, u32[]{:S(2)}, u32[]{:S(2)}) collective-permute-start(bf16[8,7296]{1,0:T(8,128)(2,1)S(1)} %pack.1.refs_0_), channel_id=1, source_target_pairs={{0,1},{1,0},{2,3},{3,2},{4,5},{5,4},{6,7},{7,6},{8,9},{9,8},{10,11... | collective-permute-start | bytes 350216 | tf_op jit(solution)/shard_map/ppermute | solution.py:14
  4.7 11.8 %collective-permute-start.1 = (bf16[8,7296]{1,0:T(8,128)(2,1)S(1)}, bf16[8,7296]{1,0:T(8,128)(2,1)S(1)}, u32[]{:S(2)}, u32[]{:S(2)}) collective-permute-start(bf16[8,7296]{1,0:T(8,128)(2,1)S(1)} %pack.1.refs_0_), channel_id=1, source_target_pairs={{0,2},{1,3},{2,0},{3,1},{4,6},{5,7},{6,4},{7,5},{8,10},{9,11},{10,... | collective-permute-start | bytes 350216 | tf_op jit(solution)/shard_map/ppermute | solution.py:14
  7.3 10.8 %collective-permute-start.2 = (bf16[8,7296]{1,0:T(8,128)(2,1)S(1)}, bf16[8,7296]{1,0:T(8,128)(2,1)S(1)}, u32[]{:S(2)}, u32[]{:S(2)}) collective-permute-start(bf16[8,7296]{1,0:T(8,128)(2,1)S(1)} %pack.1.refs_0_), channel_id=1, source_target_pairs={{0,3},{1,2},{2,1},{3,0},{4,7},{5,6},{6,5},{7,4},{8,11},{9,10},{10,... | collective-permute-start | bytes 350216 | tf_op jit(solution)/shard_map/ppermute | solution.py:14
  7.3 11.3 %collective-permute-start.7 = (bf16[8,7296]{1,0:T(8,128)(2,1)S(1)}, bf16[8,7296]{1,0:T(8,128)(2,1)S(1)}, u32[]{:S(2)}, u32[]{:S(2)}) collective-permute-start(bf16[8,7296]{1,0:T(8,128)(2,1)S(1)} %pack.1.refs_0_), channel_id=1, source_target_pairs={{0,8},{4,12},{8,0},{12,4},{1,9},{5,13},{9,1},{13,5},{2,10},{6,14},... | collective-permute-start | bytes 350216 | tf_op jit(solution)/shard_map/ppermute | solution.py:14
  9.0 9.6 %collective-permute-start.3 = (bf16[8,7296]{1,0:T(8,128)(2,1)S(1)}, bf16[8,7296]{1,0:T(8,128)(2,1)S(1)}, u32[]{:S(2)}, u32[]{:S(2)}) collective-permute-start(bf16[8,7296]{1,0:T(8,128)(2,1)S(1)} %pack.1.refs_0_), channel_id=1, source_target_pairs={{0,4},{4,0},{8,12},{12,8},{1,5},{5,1},{9,13},{13,9},{2,6},{6,2},{1... | collective-permute-start | bytes 350216 | tf_op jit(solution)/shard_map/ppermute | solution.py:14
  9.1 10.0 %collective-permute-start.8 = (bf16[8,7296]{1,0:T(8,128)(2,1)S(1)}, bf16[8,7296]{1,0:T(8,128)(2,1)S(1)}, u32[]{:S(2)}, u32[]{:S(2)}) collective-permute-start(bf16[8,7296]{1,0:T(8,128)(2,1)S(1)} %collective-permute-done.refs_1_), channel_id=1, source_target_pairs={{0,8},{4,12},{8,0},{12,4},{1,9},{5,13},{9,1},{13,5},{2,10},{6,14},... | collective-permute-start | bytes 350216 | tf_op jit(solution)/shard_map/ppermute | solution.py:14
  16.5 4.8 %collective-permute-start.9 = (bf16[8,7296]{1,0:T(8,128)(2,1)S(1)}, bf16[8,7296]{1,0:T(8,128)(2,1)S(1)}, u32[]{:S(2)}, u32[]{:S(2)}) collective-permute-start(bf16[8,7296]{1,0:T(8,128)(2,1)S(1)} %collective-permute-done.1.refs_2_), channel_id=1, source_target_pairs={{0,8},{4,12},{8,0},{12,4},{1,9},{5,13},{9,1},{13,5},{2,10},{6,14},... | collective-permute-start | bytes 350216 | tf_op jit(solution)/shard_map/ppermute | solution.py:14
  18.1 4.8 %collective-permute-start.10 = (bf16[8,7296]{1,0:T(8,128)(2,1)S(1)}, bf16[8,7296]{1,0:T(8,128)(2,1)S(1)}, u32[]{:S(2)}, u32[]{:S(2)}) collective-permute-start(bf16[8,7296]{1,0:T(8,128)(2,1)S(1)} %collective-permute-done.2.refs_3_), channel_id=1, source_target_pairs={{0,8},{4,12},{8,0},{12,4},{1,9},{5,13},{9,1},{13,5},{2,10},{6,14},... | collective-permute-start | bytes 350216 | tf_op jit(solution)/shard_map/ppermute | solution.py:14
  18.6 4.3 %collective-permute-start.4 = (bf16[8,7296]{1,0:T(8,128)(2,1)S(1)}, bf16[8,7296]{1,0:T(8,128)(2,1)S(1)}, u32[]{:S(2)}, u32[]{:S(2)}) collective-permute-start(bf16[8,7296]{1,0:T(8,128)(2,1)S(1)} %collective-permute-done.refs_1_), channel_id=1, source_target_pairs={{0,4},{4,0},{8,12},{12,8},{1,5},{5,1},{9,13},{13,9},{2,6},{6,2},{1... | collective-permute-start | bytes 350216 | tf_op jit(solution)/shard_map/ppermute | solution.py:14
  18.6 4.8 %collective-permute-start.5 = (bf16[8,7296]{1,0:T(8,128)(2,1)S(1)}, bf16[8,7296]{1,0:T(8,128)(2,1)S(1)}, u32[]{:S(2)}, u32[]{:S(2)}) collective-permute-start(bf16[8,7296]{1,0:T(8,128)(2,1)S(1)} %collective-permute-done.1.refs_2_), channel_id=1, source_target_pairs={{0,4},{4,0},{8,12},{12,8},{1,5},{5,1},{9,13},{13,9},{2,6},{6,2},{1... | collective-permute-start | bytes 350216 | tf_op jit(solution)/shard_map/ppermute | solution.py:14
  19.1 4.5 %collective-permute-start.6 = (bf16[8,7296]{1,0:T(8,128)(2,1)S(1)}, bf16[8,7296]{1,0:T(8,128)(2,1)S(1)}, u32[]{:S(2)}, u32[]{:S(2)}) collective-permute-start(bf16[8,7296]{1,0:T(8,128)(2,1)S(1)} %collective-permute-done.2.refs_3_), channel_id=1, source_target_pairs={{0,4},{4,0},{8,12},{12,8},{1,5},{5,1},{9,13},{13,9},{2,6},{6,2},{1... | collective-permute-start | bytes 350216 | tf_op jit(solution)/shard_map/ppermute | solution.py:14
  21.4 2.2 %collective-permute-start.11 = (bf16[8,7296]{1,0:T(8,128)(2,1)S(1)}, bf16[8,7296]{1,0:T(8,128)(2,1)S(1)}, u32[]{:S(2)}, u32[]{:S(2)}) collective-permute-start(bf16[8,7296]{1,0:T(8,128)(2,1)S(1)} %collective-permute-done.7.refs_8_), channel_id=1, source_target_pairs={{0,4},{4,0},{8,12},{12,8},{1,5},{5,1},{9,13},{13,9},{2,6},{6,2},{1... | collective-permute-start | bytes 350216 | tf_op jit(solution)/shard_map/ppermute | solution.py:14
  22.9 1.3 %collective-permute-start.12 = (bf16[8,7296]{1,0:T(8,128)(2,1)S(1)}, bf16[8,7296]{1,0:T(8,128)(2,1)S(1)}, u32[]{:S(2)}, u32[]{:S(2)}) collective-permute-start(bf16[8,7296]{1,0:T(8,128)(2,1)S(1)} %collective-permute-done.8.refs_9_), channel_id=1, source_target_pairs={{0,4},{4,0},{8,12},{12,8},{1,5},{5,1},{9,13},{13,9},{2,6},{6,2},{1... | collective-permute-start | bytes 350216 | tf_op jit(solution)/shard_map/ppermute | solution.py:14
  22.9 1.5 %collective-permute-start.13 = (bf16[8,7296]{1,0:T(8,128)(2,1)S(1)}, bf16[8,7296]{1,0:T(8,128)(2,1)S(1)}, u32[]{:S(2)}, u32[]{:S(2)}) collective-permute-start(bf16[8,7296]{1,0:T(8,128)(2,1)S(1)} %collective-permute-done.9.refs_10_), channel_id=1, source_target_pairs={{0,4},{4,0},{8,12},{12,8},{1,5},{5,1},{9,13},{13,9},{2,6},{6,2},{1... | collective-permute-start | bytes 350216 | tf_op jit(solution)/shard_map/ppermute | solution.py:14
  23.4 1.3 %collective-permute-start.14 = (bf16[8,7296]{1,0:T(8,128)(2,1)S(1)}, bf16[8,7296]{1,0:T(8,128)(2,1)S(1)}, u32[]{:S(2)}, u32[]{:S(2)}) collective-permute-start(bf16[8,7296]{1,0:T(8,128)(2,1)S(1)} %collective-permute-done.10.refs_11_), channel_id=1, source_target_pairs={{0,4},{4,0},{8,12},{12,8},{1,5},{5,1},{9,13},{13,9},{2,6},{6,2},{1... | collective-permute-start | bytes 350216 | tf_op jit(solution)/shard_map/ppermute | solution.py:14
  23.5 15.1 %copy-start.4 = (s32[8,2]{0,1:T(2,128)S(1)}, s32[8,2]{0,1:T(2,128)}, u32[]{:S(2)}) copy-start(s32[8,2]{0,1:T(2,128)} %param.7) | copy-start | bytes 196
  24.7 3.1 %copy-start = (bf16[1,7168,512]{2,1,0:T(8,128)(2,1)S(1)}, bf16[1,7168,512]{2,1,0:T(8,128)(2,1)}, u32[]{:S(2)}) copy-start(bf16[1,7168,512]{2,1,0:T(8,128)(2,1)} %refs_16_.1) | copy-start | bytes 22020100
  27.8 3.1 %copy-start.1 = (bf16[1,7168,512]{2,1,0:T(8,128)(2,1)S(1)}, bf16[1,7168,512]{2,1,0:T(8,128)(2,1)}, u32[]{:S(2)}) copy-start(bf16[1,7168,512]{2,1,0:T(8,128)(2,1)} %refs_17_.1) | copy-start | bytes 22020100
  34.1 18.7 %copy-start.6 = (f32[8,2]{0,1:T(2,128)S(1)}, f32[8,2]{0,1:T(2,128)}, u32[]{:S(2)}) copy-start(f32[8,2]{0,1:T(2,128)} %param.8) | copy-start | bytes 196
  34.1 5.2 %collective-permute-start.15 = (bf16[64,512]{1,0:T(8,128)(2,1)S(1)}, bf16[64,512]{1,0:T(8,128)(2,1)S(1)}, u32[]{:S(2)}, u32[]{:S(2)}) collective-permute-start(bf16[64,512]{1,0:T(8,128)(2,1)S(1)} %gate_up.1.refs_0_), channel_id=1, source_target_pairs={{0,1},{1,0},{2,3},{3,2},{4,5},{5,4},{6,7},{7,6},{8,9},{9,8},{10,11... | collective-permute-start | bytes 196616 | tf_op jit(solution)/shard_map/ppermute | solution.py:14
  34.5 7.8 %collective-permute-start.16 = (bf16[64,512]{1,0:T(8,128)(2,1)S(1)}, bf16[64,512]{1,0:T(8,128)(2,1)S(1)}, u32[]{:S(2)}, u32[]{:S(2)}) collective-permute-start(bf16[64,512]{1,0:T(8,128)(2,1)S(1)} %gate_up.1.refs_0_), channel_id=1, source_target_pairs={{0,2},{1,3},{2,0},{3,1},{4,6},{5,7},{6,4},{7,5},{8,10},{9,11},{10,... | collective-permute-start | bytes 196616 | tf_op jit(solution)/shard_map/ppermute | solution.py:14
  37.2 6.2 %collective-permute-start.17 = (bf16[64,512]{1,0:T(8,128)(2,1)S(1)}, bf16[64,512]{1,0:T(8,128)(2,1)S(1)}, u32[]{:S(2)}, u32[]{:S(2)}) collective-permute-start(bf16[64,512]{1,0:T(8,128)(2,1)S(1)} %gate_up.1.refs_0_), channel_id=1, source_target_pairs={{0,3},{1,2},{2,1},{3,0},{4,7},{5,6},{6,5},{7,4},{8,11},{9,10},{10,... | collective-permute-start | bytes 196616 | tf_op jit(solution)/shard_map/ppermute | solution.py:14
  43.4 3.1 %copy-start.2 = (bf16[1,2048,1792]{2,1,0:T(8,128)(2,1)S(1)}, bf16[1,2048,1792]{2,1,0:T(8,128)(2,1)}, u32[]{:S(2)}) copy-start(bf16[1,2048,1792]{2,1,0:T(8,128)(2,1)} %refs_4_.1) | copy-start | bytes 22020100
  48.6 13.4 %all-to-all-start = ((bf16[16,4,1792]{2,1,0:T(4,128)(2,1)}), bf16[16,4,1792]{2,1,0:T(4,128)(2,1)S(1)}, u32[]{:S(2)}, u32[]{:S(2)}) async-start(bf16[16,4,1792]{2,1,0:T(4,128)(2,1)} %reshape.23), calls=%async_computation | async-start | bytes 458752 | tf_op jit(solution)/shard_map/all_to_all | solution.py:165

commit v2 on v1

v2 whole, which is shorter than its diff:
```python
import functools

import jax
import jax.numpy as jnp
from jax import lax
from jax.experimental import pallas as pl
from jax.experimental.pallas import tpu as pltpu
from jax.sharding import PartitionSpec as P

LANES = 128
PIECES = 3
VMEM = pl.BlockSpec(memory_space=pltpu.VMEM)
HBM = pl.BlockSpec(memory_space=pltpu.HBM)


def iota(shape, dim):
    return lax.broadcasted_iota(jnp.int32, shape, dim)


def as_bf16(mask):
    return mask.astype(jnp.float32).astype(jnp.bfloat16)


def swap(x, axis, size, k):
    return lax.ppermute(x, axis, [(i, i ^ k) for i in range(size)])


def pack_kernel(tokens, routes, gates, out, named, shares, sems):
    count, width = tokens.shape
    chosen = routes.shape[0]
    moves = [
        pltpu.make_async_copy(routes, named, sems.at[0]),
        pltpu.make_async_copy(gates, shares, sems.at[1]),
        pltpu.make_async_copy(tokens, out.at[:, pl.ds(0, width)], sems.at[2]),
    ]
    for move in moves:
        move.start()
    for move in moves[:2]:
        move.wait()
    diagonal = iota((count, count), 0) == iota((count, count), 1)
    lane = iota((count, LANES), 1)
    meta = jnp.zeros((count, LANES), jnp.float32)
    for k in range(chosen):
        columns = [named[k:k + 1, :].astype(jnp.float32)]
        rest = shares[k:k + 1, :]
        for _ in range(PIECES):
            piece = rest.astype(jnp.bfloat16).astype(jnp.float32)
            columns.append(piece)
            rest = rest - piece
        for p, value in enumerate(columns):
            value = jnp.where(diagonal, jnp.broadcast_to(value, (count, count)), 0.0)
            meta = jnp.where(lane == p * chosen + k, jnp.sum(value, axis=1, keepdims=True), meta)
    out[:, width:] = meta.astype(jnp.bfloat16)
    moves[2].wait()


def up_kernel(count, chosen, cap, chunk, width, *refs):
    n = len(refs) - 4
    blocks, (w_gate, w_up, out, xs) = refs[:n], refs[n:]
    columns = out.shape[1]
    rows = count * chunk
    slots = cap * chunk
    expert = lax.axis_index("ep")
    me = expert * lax.axis_size("sub") + lax.axis_index("sub")
    for b in range(0, n, 2):
        pair = jnp.concatenate([blocks[b][...], blocks[b + 1][...]], axis=0)
        xs[b * count:(b + 2) * count, :] = pair
    step = min(256, columns)

    def part(j, carry):
        at = pl.multiple_of(j * rows, rows)
        meta = jnp.transpose(xs[pl.ds(at, rows), width:width + LANES].astype(jnp.float32))
        named = (iota((LANES, rows), 0) < chosen) & (meta == expert.astype(jnp.float32))
        present = jnp.max(named.astype(jnp.float32), axis=0, keepdims=True)
        a, b = iota((rows, rows), 0), iota((rows, rows), 1)
        earlier = as_bf16((a // count == b // count) & (a < b))
        many = jnp.broadcast_to(present, (slots, rows))
        rank = jnp.dot(many.astype(jnp.bfloat16), earlier, preferred_element_type=jnp.float32)
        slot, token = iota((slots, rows), 0), iota((slots, rows), 1)
        owner = (token // count) ^ (me % chunk)
        pick = (slot // cap == owner) & ((slot % cap).astype(jnp.float32) == rank) & (many > 0.5)
        pick = as_bf16(pick)
        to = pl.multiple_of((j ^ (me // chunk)) * slots, slots)
        for c in range(0, columns, step):
            x = xs[pl.ds(at, rows), :width]
            gate = jnp.dot(x, w_gate[0, :, c:c + step], preferred_element_type=jnp.float32)
            up = jnp.dot(x, w_up[0, :, c:c + step], preferred_element_type=jnp.float32)
            hidden = (gate / (1.0 + jnp.exp(-gate)) * up).astype(jnp.bfloat16)
            picked = jnp.dot(pick, hidden, preferred_element_type=jnp.float32)
            out[pl.ds(to, slots), c:c + step] = picked.astype(jnp.bfloat16)
        return carry

    lax.fori_loop(0, n // chunk, part, 0)


def down_kernel(experts, groups, *refs):
    parts, w_down = refs[:groups], refs[groups]
    outs, rows = refs[groups + 1:groups + 1 + experts], refs[-1]
    depth = parts[0].shape[1]
    each, columns = outs[0].shape
    ep, sub = lax.axis_index("ep"), lax.axis_index("sub")
    for e in range(experts):
        at = pl.multiple_of((ep ^ e) * each, each)
        for k in range(groups):
            rows[e * each:(e + 1) * each, k * depth:(k + 1) * depth] = parts[k][pl.ds(at, each), :]
    step = 256 if columns % 256 == 0 else 128
    for c in range(0, columns, step):
        total = None
        for k in range(groups):
            d = pl.multiple_of((sub ^ k) * depth, depth)
            term = jnp.dot(
                rows[:, k * depth:(k + 1) * depth],
                w_down[0, pl.ds(d, depth), c:c + step],
                preferred_element_type=jnp.float32,
            )
            total = term if total is None else total + term
        total = total.astype(jnp.bfloat16)
        for e in range(experts):
            outs[e][:, c:c + step] = total[e * each:(e + 1) * each, :]


def combine_kernel(experts, groups, count, chosen, cap, width, *refs):
    blocks, got = refs[:groups], refs[groups:groups + experts]
    outs, rows = refs[groups + experts:-1], refs[-1]
    each = got[0].shape[0]
    tokens = groups * count
    ep, sub = lax.axis_index("ep"), lax.axis_index("sub")
    for e in range(experts):
        rows[e * each:(e + 1) * each, :] = got[e][...]
    meta = jnp.concatenate([b[:, width:width + LANES].astype(jnp.float32) for b in blocks], axis=0)
    a, b = iota((tokens, tokens), 0), iota((tokens, tokens), 1)
    earlier = as_bf16((a // count == b // count) & (b < a))
    lane = iota((tokens, LANES), 1)
    token, slot = iota((tokens, each), 0), iota((tokens, each), 1)
    mine = slot // cap == (token // count) ^ sub
    place = (slot % cap).astype(jnp.float32)
    weights = [[] for _ in range(PIECES)]
    for e in range(experts):
        named = ((lane < chosen) & (meta == (ep ^ e).astype(jnp.float32))).astype(jnp.float32)
        present = jnp.broadcast_to(jnp.max(named, axis=1, keepdims=True), (tokens, each))
        rank = jnp.dot(earlier, present.astype(jnp.bfloat16), preferred_element_type=jnp.float32)
        taken = mine & (place == rank) & (present > 0.5)
        for p in range(PIECES):
            share = 0.0
            for k in range(chosen):
                at = (p + 1) * chosen + k
                share = share + meta[:, at:at + 1] * named[:, k:k + 1]
            weights[p].append(jnp.where(taken, share, 0.0))
    weights = [jnp.concatenate(w, axis=1).astype(jnp.bfloat16) for w in weights]
    total = 0.0
    for w in weights[::-1]:
        total = total + jnp.dot(w, rows[...], preferred_element_type=jnp.float32)
    total = total.astype(jnp.bfloat16)
    for k in range(groups):
        outs[k][...] = total[k * count:(k + 1) * count, :]


def place_kernel(*refs):
    parts, out, sems = refs[:-2], refs[-2], refs[-1]
    columns = parts[0].shape[1]
    sub = lax.axis_index("sub")
    moves = []
    for k, part in enumerate(parts):
        at = pl.multiple_of((sub ^ k) * columns, columns)
        moves.append(pltpu.make_async_copy(part, out.at[:, pl.ds(at, columns)], sems.at[k]))
    for move in moves:
        move.start()
    for move in moves:
        move.wait()


def body(tokens, routes, gates, gate_weight, up_weight, down_weight):
    experts = lax.axis_size("ep")
    groups = lax.axis_size("sub")
    count, width = tokens.shape
    chosen = routes.shape[1]
    cap = count * chosen * 9 // (8 * experts)
    devices = experts * groups
    chunk = min(16, devices)

    def array(*shape):
        return jax.ShapeDtypeStruct(shape, jnp.bfloat16)

    def limit(mib):
        return pltpu.CompilerParams(vmem_limit_bytes=mib << 20)

    own = pl.pallas_call(
        pack_kernel,
        out_shape=array(count, width + LANES),
        in_specs=[HBM, HBM, HBM],
        out_specs=VMEM,
        scratch_shapes=[
            pltpu.VMEM((chosen, count), jnp.int32),
            pltpu.VMEM((chosen, count), jnp.float32),
            pltpu.SemaphoreType.DMA((3,)),
        ],
        compiler_params=limit(1),
        cost_estimate=pl.CostEstimate(flops=20000000000, bytes_accessed=0, transcendentals=0),
        name="pack",
    )(tokens, routes.T, gates.T)

    got = {(0, 0): own}
    single = [1 << b for b in range(groups.bit_length() - 1)]
    far = range(2, experts, 2)
    for kz in single[::-1]:
        got[kz, 0] = swap(own, "sub", groups, kz)
    for ky in far:
        got[0, ky] = swap(own, "ep", experts, ky)
    relayed = [kz for kz in range(1, groups) if kz not in single]
    for kz in relayed:
        for ky in far:
            got[kz, ky] = swap(got[0, ky], "sub", groups, kz)
    for kz in relayed:
        low = kz & -kz
        got[kz, 0] = swap(got[kz ^ low, 0], "sub", groups, low)
    for kz in single:
        for ky in far:
            got[kz, ky] = swap(got[kz, 0], "ep", experts, ky)
    for kz in range(groups):
        for ky in range(0, experts, 2):
            got[kz, ky + 1] = swap(got[kz, ky], "ep", experts, 1)
    blocks = [got[kz, ke] for ke in range(experts) for kz in range(groups)]

    columns = gate_weight.shape[2]
    hidden = pl.pallas_call(
        functools.partial(up_kernel, count, chosen, cap, chunk, width),
        out_shape=array(devices * cap, columns),
        in_specs=[VMEM] * (devices + 2),
        out_specs=VMEM,
        scratch_shapes=[pltpu.VMEM((devices * count, width + LANES), jnp.bfloat16)],
        compiler_params=limit(12 if devices <= 16 else 24),
        name="gate_up",
    )(*blocks, gate_weight, up_weight)

    parts = [hidden] + [swap(hidden, "sub", groups, k) for k in range(1, groups)]
    out_cols = down_weight.shape[2]
    sent = pl.pallas_call(
        functools.partial(down_kernel, experts, groups),
        out_shape=[array(groups * cap, out_cols)] * experts,
        in_specs=[VMEM] * (groups + 1),
        out_specs=[VMEM] * experts,
        scratch_shapes=[pltpu.VMEM((devices * cap, groups * columns), jnp.bfloat16)],
        compiler_params=limit(8 if devices <= 16 else 24),
        name="down",
    )(*parts, down_weight)

    came = [sent[0]] + [swap(sent[e], "ep", experts, e) for e in range(1, experts)]
    summed = pl.pallas_call(
        functools.partial(combine_kernel, experts, groups, count, chosen, cap, width),
        out_shape=[array(count, out_cols)] * groups,
        in_specs=[VMEM] * (groups + experts),
        out_specs=[VMEM] * groups,
        scratch_shapes=[pltpu.VMEM((devices * cap, out_cols), jnp.bfloat16)],
        compiler_params=limit(8 if devices <= 16 else 24),
        name="combine",
    )(*[got[k, 0] for k in range(groups)], *came)

    home = [summed[0]] + [swap(summed[k], "sub", groups, k) for k in range(1, groups)]
    return pl.pallas_call(
        place_kernel,
        out_shape=array(count, width),
        in_specs=[VMEM] * groups,
        out_specs=HBM,
        scratch_shapes=[pltpu.SemaphoreType.DMA((groups,))],
        compiler_params=limit(1),
        name="place",
    )(*home)


def solution(mesh):
    return jax.shard_map(
        body,
        mesh=mesh,
        in_specs=(
            P(("groups", "ep", "sub"), None),
            P(("groups", "ep", "sub"), None),
            P(("groups", "ep", "sub"), None),
            P("ep", None, "sub"),
            P("ep", None, "sub"),
            P("ep", None, "sub"),
        ),
        out_specs=P(("groups", "ep", "sub"), None),
        check_vma=False,
    )
```

time: 63.5 us -> 52.3 us (0.82)
  local copies, waits for them, and re-layouts: 11.7 us -> 2.68 us
  waiting for transfers between devices: 24.3 us -> 21.6 us
  starting transfers between devices: 20.9 us -> 22.3 us
  matrix products: 1.08 us -> 0 us
  Pallas kernels: 4.7 us -> 5.44 us
    all_to_all x1 -> x0, waiting for transfers between devices: 9.02 us -> none  [body(): lax.all_to_all(result.reshape(devices, slot_cap, out_cols), ('ep', 'sub')...]
    unnamed x14, local copies, waits for them, and re-layouts: 10.8 us -> 2.68 us
    ppermute x18 -> x24, waiting for transfers between devices: 15.3 us -> 21.6 us  [swap(): return lax.ppermute(x, axis, [(i, i ^ k) for i in range(size)])]
    ppermute x18 -> x24, starting transfers between devices: 16.7 us -> 22.3 us  [swap(): return lax.ppermute(x, axis, [(i, i ^ k) for i in range(size)])]
    all_to_all x1 -> x0, starting transfers between devices: 4.19 us -> none  [body(): lax.all_to_all(result.reshape(devices, slot_cap, out_cols), ('ep', 'sub')...]
    dot_general x1 -> x0, matrix products: 1.08 us -> none  [body(): jnp.einsum('tec,ced->td', weighting, returned, precision=lax.Precision.HI...]
    reshape x1 -> x0, local copies, waits for them, and re-layouts: 0.74 us -> none  [body(): result.reshape(devices, slot_cap, out_cols)]
    pallas_call x3 -> x5, Pallas kernels: 4.7 us -> 5.44 us  [the longest x1 2.5 us: body(): pl.pallas_call(functools.partial(up_kernel, count, chosen, cap, chunk, wi...]
  transfers between devices with their start and end apart: 19 -> 24, of which waited for: 11 -> 12; matrix products, arithmetic and copies ran while one was open for 1% -> 0% of each run, Pallas kernels for 0% -> 0%
where the time goes in v2:
time: 52.3 us; the launch traced here: 52.1 us
  starting transfers between devices  22.3 us (43%)
  waiting for transfers between devices  21.6 us (41%)
  Pallas kernels  5.44 us (10%)
  local copies, waits for them, and re-layouts  2.68 us (5%)
    ppermute x24, starting transfers between devices, swap(): return lax.ppermute(x, axis, [(i, i ^ k) for i in range(size)])  22.3 us
    ppermute x24, waiting for transfers between devices, swap(): return lax.ppermute(x, axis, [(i, i ^ k) for i in range(size)])  21.6 us
    unnamed x14, local copies, waits for them, and re-layouts  2.68 us
    pallas_call x1, Pallas kernels, body(): pl.pallas_call(functools.partial(up_kernel, count, chosen, cap, chunk, wi...  2.5 us
    pallas_call x1, Pallas kernels, body(): pl.pallas_call(functools.partial(down_kernel, experts, groups), out_shape...  1.39 us
  transfers between devices with their start and end apart: 24, of which 12 were waited for; matrix products, arithmetic and copies ran while one was open for 0% of the time, Pallas kernels for 0%

profile of v2, /device:TPU:0, one launch (start us, length us, event | category | flops | bytes accessed | tf_op | source)
XLA Modules:
  0.0 52.1 jit_solution(1057813140272513691)
XLA Ops:
  0.0 0.0 slice-start
  0.0 0.0 copy-start.2
  0.0 1.0 %copy-done.2 = bf16[8,7168]{1,0:T(8,128)(2,1)S(1)} copy-done((bf16[8,7168]{1,0:T(8,128)(2,1)S(1)}, bf16[8,7168]{1,0:T(8,128)(2,1)}, u32[]{:S(2)}) %copy-start.2) | copy-done | bytes 114712
  1.1 0.0 copy-start.3
  1.1 0.9 %copy-done.3 = s32[8,2]{0,1:T(2,128)S(1)} copy-done((s32[8,2]{0,1:T(2,128)S(1)}, s32[8,2]{0,1:T(2,128)}, u32[]{:S(2)}) %copy-start.3) | copy-done | bytes 88
  2.0 0.0 copy-start.4
  2.0 0.7 %copy-done.4 = f32[8,2]{0,1:T(2,128)S(1)} copy-done((f32[8,2]{0,1:T(2,128)S(1)}, f32[8,2]{0,1:T(2,128)}, u32[]{:S(2)}) %copy-start.4) | copy-done | bytes 88
  2.7 0.3 pack.1.refs_0_
  3.0 3.0 %collective-permute-start.7 = (bf16[8,7296]{1,0:T(8,128)(2,1)S(1)}, bf16[8,7296]{1,0:T(8,128)(2,1)S(1)}, u32[]{:S(2)}, u32[]{:S(2)}) collective-permute-start(bf16[8,7296]{1,0:T(8,128)(2,1)S(1)} %pack.1.refs_0_), channel_id=1, source_target_pairs={{0,8},{4,12},{8,0},{12,4},{1,9},{5,13},{9,1},{13,5},{2,10},{6,14},... | collective-permute-start | bytes 350216 | tf_op jit(solution)/shard_map/ppermute | solution.py:25
  6.0 2.6 %collective-permute-start.1 = (bf16[8,7296]{1,0:T(8,128)(2,1)S(1)}, bf16[8,7296]{1,0:T(8,128)(2,1)S(1)}, u32[]{:S(2)}, u32[]{:S(2)}) collective-permute-start(bf16[8,7296]{1,0:T(8,128)(2,1)S(1)} %pack.1.refs_0_), channel_id=1, source_target_pairs={{0,2},{1,3},{2,0},{3,1},{4,6},{5,7},{6,4},{7,5},{8,10},{9,11},{10,... | collective-permute-start | bytes 350216 | tf_op jit(solution)/shard_map/ppermute | solution.py:25
  8.6 0.0 collective-permute-start.3
  8.6 1.6 %collective-permute-start = (bf16[8,7296]{1,0:T(8,128)(2,1)S(1)}, bf16[8,7296]{1,0:T(8,128)(2,1)S(1)}, u32[]{:S(2)}, u32[]{:S(2)}) collective-permute-start(bf16[8,7296]{1,0:T(8,128)(2,1)S(1)} %pack.1.refs_0_), channel_id=1, source_target_pairs={{0,1},{1,0},{2,3},{3,2},{4,5},{5,4},{6,7},{7,6},{8,9},{9,8},{10,11... | collective-permute-start | bytes 350216 | tf_op jit(solution)/shard_map/ppermute | solution.py:25
  10.2 0.0 collective-permute-done.7.refs_8_
  10.2 0.2 collective-permute-start.11
  10.4 2.6 %collective-permute-start.10 = (bf16[8,7296]{1,0:T(8,128)(2,1)S(1)}, bf16[8,7296]{1,0:T(8,128)(2,1)S(1)}, u32[]{:S(2)}, u32[]{:S(2)}) collective-permute-start(bf16[8,7296]{1,0:T(8,128)(2,1)S(1)} %collective-permute-done.7.refs_8_), channel_id=1, source_target_pairs={{0,3},{1,2},{2,1},{3,0},{4,7},{5,6},{6,5},{7,4},{8,11},{9,10},{10,... | collective-permute-start | bytes 350216 | tf_op jit(solution)/shard_map/ppermute | solution.py:25
  13.0 1.3 %collective-permute-done.1.refs_2_ = bf16[8,7296]{1,0:T(8,128)(2,1)S(1)} collective-permute-done((bf16[8,7296]{1,0:T(8,128)(2,1)S(1)}, bf16[8,7296]{1,0:T(8,128)(2,1)S(1)}, u32[]{:S(2)}, u32[]{:S(2)}) %collective-permute-start.1) | collective-permute-done | bytes 116768 | tf_op jit(solution)/shard_map/ppermute | solution.py:25
  14.3 0.3 collective-permute-start.9
  14.6 0.0 collective-permute-done.3.refs_4_
  14.6 0.0 collective-permute-start.5
  14.6 3.3 %collective-permute-done.refs_1_ = bf16[8,7296]{1,0:T(8,128)(2,1)S(1)} collective-permute-done((bf16[8,7296]{1,0:T(8,128)(2,1)S(1)}, bf16[8,7296]{1,0:T(8,128)(2,1)S(1)}, u32[]{:S(2)}, u32[]{:S(2)}) %collective-permute-start) | collective-permute-done | bytes 116768 | tf_op jit(solution)/shard_map/ppermute | solution.py:25
  17.9 0.0 collective-permute-start.2
  17.9 0.0 collective-permute-done.11.refs_12_
  17.9 0.0 collective-permute-start.8
  17.9 0.0 collective-permute-done.10.refs_11_
  17.9 0.1 collective-permute-start.4
  18.0 2.0 %collective-permute-done.9.refs_10_ = bf16[8,7296]{1,0:T(8,128)(2,1)S(1)} collective-permute-done((bf16[8,7296]{1,0:T(8,128)(2,1)S(1)}, bf16[8,7296]{1,0:T(8,128)(2,1)S(1)}, u32[]{:S(2)}, u32[]{:S(2)}) %collective-permute-start.9) | collective-permute-done | bytes 116768 | tf_op jit(solution)/shard_map/ppermute | solution.py:25
  20.0 0.0 collective-permute-start.14
  20.0 0.0 collective-permute-done.5.refs_6_
  20.0 0.5 collective-permute-start.13
  20.5 2.2 %collective-permute-done.2.refs_3_ = bf16[8,7296]{1,0:T(8,128)(2,1)S(1)} collective-permute-done((bf16[8,7296]{1,0:T(8,128)(2,1)S(1)}, bf16[8,7296]{1,0:T(8,128)(2,1)S(1)}, u32[]{:S(2)}, u32[]{:S(2)}) %collective-permute-start.2) | collective-permute-done | bytes 116768 | tf_op jit(solution)/shard_map/ppermute | solution.py:25
  22.7 0.0 collective-permute-start.6
  22.7 0.0 collective-permute-done.8.refs_9_
  22.7 0.5 collective-permute-start.12
  23.2 0.0 collective-permute-done.4.refs_5_
  23.2 0.0 collective-permute-done.14.refs_15_
  23.2 0.0 collective-permute-done.13.refs_14_
  23.2 0.8 %collective-permute-done.6.refs_7_ = bf16[8,7296]{1,0:T(8,128)(2,1)S(1)} collective-permute-done((bf16[8,7296]{1,0:T(8,128)(2,1)S(1)}, bf16[8,7296]{1,0:T(8,128)(2,1)S(1)}, u32[]{:S(2)}, u32[]{:S(2)}) %collective-permute-start.6) | collective-permute-done | bytes 116768 | tf_op jit(solution)/shard_map/ppermute | solution.py:25
  24.0 0.2 collective-permute-done.12.refs_13_
  24.2 0.0 copy-done
  24.2 0.0 copy-done.1
  24.2 2.5 %gate_up.1.refs_0_ = bf16[64,512]{1,0:T(8,128)(2,1)S(1)} custom-call(bf16[8,7296]{1,0:T(8,128)(2,1)S(1)} %pack.1.refs_0_, bf16[8,7296]{1,0:T(8,128)(2,1)S(1)} %collective-permute-done.refs_1_, bf16[8,7296]{1,0:T(8,128)(2,1)S(1)} %collective-permute-done.1.refs_2_, bf16[8,7296]{1,0:T(8,128)(2,1)S(1)} %collective-permute-done.2.refs_3_, ...), custom_call_target="tpu_custom_call" | custom-call | tf_op jit(solution)/shard_map/gate_up/pallas_call | solution.py:225
  26.7 2.3 %collective-permute-start.17 = (bf16[64,512]{1,0:T(8,128)(2,1)S(1)}, bf16[64,512]{1,0:T(8,128)(2,1)S(1)}, u32[]{:S(2)}, u32[]{:S(2)}) collective-permute-start(bf16[64,512]{1,0:T(8,128)(2,1)S(1)} %gate_up.1.refs_0_), channel_id=1, source_target_pairs={{0,3},{1,2},{2,1},{3,0},{4,7},{5,6},{6,5},{7,4},{8,11},{9,10},{10,... | collective-permute-start | bytes 196616 | tf_op jit(solution)/shard_map/ppermute | solution.py:25
  29.0 1.1 %collective-permute-start.16 = (bf16[64,512]{1,0:T(8,128)(2,1)S(1)}, bf16[64,512]{1,0:T(8,128)(2,1)S(1)}, u32[]{:S(2)}, u32[]{:S(2)}) collective-permute-start(bf16[64,512]{1,0:T(8,128)(2,1)S(1)} %gate_up.1.refs_0_), channel_id=1, source_target_pairs={{0,2},{1,3},{2,0},{3,1},{4,6},{5,7},{6,4},{7,5},{8,10},{9,11},{10,... | collective-permute-start | bytes 196616 | tf_op jit(solution)/shard_map/ppermute | solution.py:25
  30.1 1.1 %collective-permute-start.15 = (bf16[64,512]{1,0:T(8,128)(2,1)S(1)}, bf16[64,512]{1,0:T(8,128)(2,1)S(1)}, u32[]{:S(2)}, u32[]{:S(2)}) collective-permute-start(bf16[64,512]{1,0:T(8,128)(2,1)S(1)} %gate_up.1.refs_0_), channel_id=1, source_target_pairs={{0,1},{1,0},{2,3},{3,2},{4,5},{5,4},{6,7},{7,6},{8,9},{9,8},{10,11... | collective-permute-start | bytes 196616 | tf_op jit(solution)/shard_map/ppermute | solution.py:25
  31.2 2.4 %collective-permute-done.17.refs_3_ = bf16[64,512]{1,0:T(8,128)(2,1)S(1)} collective-permute-done((bf16[64,512]{1,0:T(8,128)(2,1)S(1)}, bf16[64,512]{1,0:T(8,128)(2,1)S(1)}, u32[]{:S(2)}, u32[]{:S(2)}) %collective-permute-start.17) | collective-permute-done | bytes 65568 | tf_op jit(solution)/shard_map/ppermute | solution.py:25
  33.6 2.9 %collective-permute-done.16.refs_2_ = bf16[64,512]{1,0:T(8,128)(2,1)S(1)} collective-permute-done((bf16[64,512]{1,0:T(8,128)(2,1)S(1)}, bf16[64,512]{1,0:T(8,128)(2,1)S(1)}, u32[]{:S(2)}, u32[]{:S(2)}) %collective-permute-start.16) | collective-permute-done | bytes 65568 | tf_op jit(solution)/shard_map/ppermute | solution.py:25
  36.5 0.0 collective-permute-done.15.refs_1_
  36.5 0.0 slice-done
  36.5 0.0 slice-done.1
  36.5 1.4 %down.1 = (bf16[16,1792]{1,0:T(8,128)(2,1)S(1)}, bf16[16,1792]{1,0:T(8,128)(2,1)S(1)}, bf16[16,1792]{1,0:T(8,128)(2,1)S(1)}, bf16[16,1792]{1,0:T(8,128)(2,1)S(1)}) custom-call(bf16[64,512]{1,0:T(8,128)(2,1)S(1)} %gate_up.1.refs_0_, bf16[64,512]{1,0:T(8,128)(2,1)S(1)} %collective-permute-done.15.refs_1_, bf16[64,512]{1,0:T(8,128)(2,1)S(1)} %collective-permute-done.16.refs_2_, ...), custom_call_target="tpu_custom_call" | custom-call | tf_op jit(solution)/shard_map/down/pallas_call | solution.py:237
  37.9 0.1 collective-permute-start.18
  38.0 0.1 collective-permute-start.19
  38.0 1.8 %collective-permute-start.20 = (bf16[16,1792]{1,0:T(8,128)(2,1)S(1)}, bf16[16,1792]{1,0:T(8,128)(2,1)S(1)}, u32[]{:S(2)}, u32[]{:S(2)}) collective-permute-start(bf16[16,1792]{1,0:T(8,128)(2,1)S(1)} %get-tuple-element.16), channel_id=1, source_target_pairs={{0,12},{4,8},{8,4},{12,0},{1,13},{5,9},{9,5},{13,1},{2,14},{6,10},... | collective-permute-start | bytes 172040 | tf_op jit(solution)/shard_map/ppermute | solution.py:25
  39.8 0.0 collective-permute-done.18.refs_5_
  39.8 2.9 %collective-permute-done.19.refs_6_ = bf16[16,1792]{1,0:T(8,128)(2,1)S(1)} collective-permute-done((bf16[16,1792]{1,0:T(8,128)(2,1)S(1)}, bf16[16,1792]{1,0:T(8,128)(2,1)S(1)}, u32[]{:S(2)}, u32[]{:S(2)}) %collective-permute-start.19) | collective-permute-done | bytes 57376 | tf_op jit(solution)/shard_map/ppermute | solution.py:25
  42.7 0.3 collective-permute-done.20.refs_7_
  43.1 0.6 %combine.1 = (bf16[8,1792]{1,0:T(8,128)(2,1)S(1)}, bf16[8,1792]{1,0:T(8,128)(2,1)S(1)}, bf16[8,1792]{1,0:T(8,128)(2,1)S(1)}, bf16[8,1792]{1,0:T(8,128)(2,1)S(1)}) custom-call(bf16[8,7296]{1,0:T(8,128)(2,1)S(1)} %pack.1.refs_0_, bf16[8,7296]{1,0:T(8,128)(2,1)S(1)} %collective-permute-done.refs_1_, bf16[8,7296]{1,0:T(8,128)(2,1)S(1)} %collective-permute-done.1.refs_2_, ...), custom_call_target="tpu_custom_call" | custom-call | tf_op jit(solution)/shard_map/combine/pallas_call | solution.py:248
  43.7 0.1 collective-permute-start.21
  43.7 2.0 %collective-permute-start.22 = (bf16[8,1792]{1,0:T(8,128)(2,1)S(1)}, bf16[8,1792]{1,0:T(8,128)(2,1)S(1)}, u32[]{:S(2)}, u32[]{:S(2)}) collective-permute-start(bf16[8,1792]{1,0:T(8,128)(2,1)S(1)} %get-tuple-element.19), channel_id=1, source_target_pairs={{0,2},{1,3},{2,0},{3,1},{4,6},{5,7},{6,4},{7,5},{8,10},{9,11},{10,... | collective-permute-start | bytes 86024 | tf_op jit(solution)/shard_map/ppermute | solution.py:25
  45.8 2.4 %collective-permute-start.23 = (bf16[8,1792]{1,0:T(8,128)(2,1)S(1)}, bf16[8,1792]{1,0:T(8,128)(2,1)S(1)}, u32[]{:S(2)}, u32[]{:S(2)}) collective-permute-start(bf16[8,1792]{1,0:T(8,128)(2,1)S(1)} %get-tuple-element.20), channel_id=1, source_target_pairs={{0,3},{1,2},{2,1},{3,0},{4,7},{5,6},{6,5},{7,4},{8,11},{9,10},{10,... | collective-permute-start | bytes 86024 | tf_op jit(solution)/shard_map/ppermute | solution.py:25
  48.1 0.0 collective-permute-done.21.refs_1_
  48.1 0.5 collective-permute-done.22.refs_2_
  48.6 2.9 %collective-permute-done.23.refs_3_ = bf16[8,1792]{1,0:T(8,128)(2,1)S(1)} collective-permute-done((bf16[8,1792]{1,0:T(8,128)(2,1)S(1)}, bf16[8,1792]{1,0:T(8,128)(2,1)S(1)}, u32[]{:S(2)}, u32[]{:S(2)}) %collective-permute-start.23) | collective-permute-done | bytes 28704 | tf_op jit(solution)/shard_map/ppermute | solution.py:25
  51.4 0.7 %place.1 = bf16[8,7168]{1,0:T(8,128)(2,1)} custom-call(bf16[8,1792]{1,0:T(8,128)(2,1)S(1)} %get-tuple-element.17.refs_0_, bf16[8,1792]{1,0:T(8,128)(2,1)S(1)} %collective-permute-done.21.refs_1_, bf16[8,1792]{1,0:T(8,128)(2,1)S(1)} %collective-permute-done.22.refs_2_, bf16[8,1792]{1,0:T(8,128)(2,1)S(1)} %collective-permute-done.23.refs_3_), custom_call_target="tpu_custom_call" | custom-call | tf_op jit(solution)/shard_map/place/pallas_call | solution.py:259
  (4 shorter events, 0.0 us)
Async XLA Ops:
  0.0 36.5 %slice-start = ((s8[7340032]{0:T(1024)(128)(4,1)}), s8[4194304]{0:T(1024)(128)(4,1)S(1)}, s32[]{:S(2)}) async-start(s8[7340032]{0:T(1024)(128)(4,1)} %bitcast.2), calls=%async_computation | async-start | bytes 8388608
  0.0 1.0 %copy-start.2 = (bf16[8,7168]{1,0:T(8,128)(2,1)S(1)}, bf16[8,7168]{1,0:T(8,128)(2,1)}, u32[]{:S(2)}) copy-start(bf16[8,7168]{1,0:T(8,128)(2,1)} %tokens.1) | copy-start | bytes 344068
  1.1 0.9 %copy-start.3 = (s32[8,2]{0,1:T(2,128)S(1)}, s32[8,2]{0,1:T(2,128)}, u32[]{:S(2)}) copy-start(s32[8,2]{0,1:T(2,128)} %param.7) | copy-start | bytes 196
  2.0 0.7 %copy-start.4 = (f32[8,2]{0,1:T(2,128)S(1)}, f32[8,2]{0,1:T(2,128)}, u32[]{:S(2)}) copy-start(f32[8,2]{0,1:T(2,128)} %param.8) | copy-start | bytes 196
  2.7 21.5 %copy-start = (bf16[1,7168,512]{2,1,0:T(8,128)(2,1)S(1)}, bf16[1,7168,512]{2,1,0:T(8,128)(2,1)}, u32[]{:S(2)}) copy-start(bf16[1,7168,512]{2,1,0:T(8,128)(2,1)} %refs_16_.1) | copy-start | bytes 22020100
  2.7 21.5 %copy-start.1 = (bf16[1,7168,512]{2,1,0:T(8,128)(2,1)S(1)}, bf16[1,7168,512]{2,1,0:T(8,128)(2,1)}, u32[]{:S(2)}) copy-start(bf16[1,7168,512]{2,1,0:T(8,128)(2,1)} %refs_17_.1) | copy-start | bytes 22020100
  2.7 33.8 %slice-start.1 = ((s8[7340032]{0:T(1024)(128)(4,1)}), s8[3145728]{0:T(1024)(128)(4,1)S(1)}, s32[]{:S(2)}) async-start(s8[7340032]{0:T(1024)(128)(4,1)} %bitcast.2), calls=%async_computation.1 | async-start | bytes 6291456
  3.0 7.2 %collective-permute-start.7 = (bf16[8,7296]{1,0:T(8,128)(2,1)S(1)}, bf16[8,7296]{1,0:T(8,128)(2,1)S(1)}, u32[]{:S(2)}, u32[]{:S(2)}) collective-permute-start(bf16[8,7296]{1,0:T(8,128)(2,1)S(1)} %pack.1.refs_0_), channel_id=1, source_target_pairs={{0,8},{4,12},{8,0},{12,4},{1,9},{5,13},{9,1},{13,5},{2,10},{6,14},... | collective-permute-start | bytes 350216 | tf_op jit(solution)/shard_map/ppermute | solution.py:25
  6.0 8.3 %collective-permute-start.1 = (bf16[8,7296]{1,0:T(8,128)(2,1)S(1)}, bf16[8,7296]{1,0:T(8,128)(2,1)S(1)}, u32[]{:S(2)}, u32[]{:S(2)}) collective-permute-start(bf16[8,7296]{1,0:T(8,128)(2,1)S(1)} %pack.1.refs_0_), channel_id=1, source_target_pairs={{0,2},{1,3},{2,0},{3,1},{4,6},{5,7},{6,4},{7,5},{8,10},{9,11},{10,... | collective-permute-start | bytes 350216 | tf_op jit(solution)/shard_map/ppermute | solution.py:25
  8.6 6.0 %collective-permute-start.3 = (bf16[8,7296]{1,0:T(8,128)(2,1)S(1)}, bf16[8,7296]{1,0:T(8,128)(2,1)S(1)}, u32[]{:S(2)}, u32[]{:S(2)}) collective-permute-start(bf16[8,7296]{1,0:T(8,128)(2,1)S(1)} %pack.1.refs_0_), channel_id=1, source_target_pairs={{0,4},{4,0},{8,12},{12,8},{1,5},{5,1},{9,13},{13,9},{2,6},{6,2},{1... | collective-permute-start | bytes 350216 | tf_op jit(solution)/shard_map/ppermute | solution.py:25
  8.6 9.3 %collective-permute-start = (bf16[8,7296]{1,0:T(8,128)(2,1)S(1)}, bf16[8,7296]{1,0:T(8,128)(2,1)S(1)}, u32[]{:S(2)}, u32[]{:S(2)}) collective-permute-start(bf16[8,7296]{1,0:T(8,128)(2,1)S(1)} %pack.1.refs_0_), channel_id=1, source_target_pairs={{0,1},{1,0},{2,3},{3,2},{4,5},{5,4},{6,7},{7,6},{8,9},{9,8},{10,11... | collective-permute-start | bytes 350216 | tf_op jit(solution)/shard_map/ppermute | solution.py:25
  10.2 7.7 %collective-permute-start.11 = (bf16[8,7296]{1,0:T(8,128)(2,1)S(1)}, bf16[8,7296]{1,0:T(8,128)(2,1)S(1)}, u32[]{:S(2)}, u32[]{:S(2)}) collective-permute-start(bf16[8,7296]{1,0:T(8,128)(2,1)S(1)} %collective-permute-done.7.refs_8_), channel_id=1, source_target_pairs={{0,4},{4,0},{8,12},{12,8},{1,5},{5,1},{9,13},{13,9},{2,6},{6,2},{1... | collective-permute-start | bytes 350216 | tf_op jit(solution)/shard_map/ppermute | solution.py:25
  10.4 7.5 %collective-permute-start.10 = (bf16[8,7296]{1,0:T(8,128)(2,1)S(1)}, bf16[8,7296]{1,0:T(8,128)(2,1)S(1)}, u32[]{:S(2)}, u32[]{:S(2)}) collective-permute-start(bf16[8,7296]{1,0:T(8,128)(2,1)S(1)} %collective-permute-done.7.refs_8_), channel_id=1, source_target_pairs={{0,3},{1,2},{2,1},{3,0},{4,7},{5,6},{6,5},{7,4},{8,11},{9,10},{10,... | collective-permute-start | bytes 350216 | tf_op jit(solution)/shard_map/ppermute | solution.py:25
  14.3 5.7 %collective-permute-start.9 = (bf16[8,7296]{1,0:T(8,128)(2,1)S(1)}, bf16[8,7296]{1,0:T(8,128)(2,1)S(1)}, u32[]{:S(2)}, u32[]{:S(2)}) collective-permute-start(bf16[8,7296]{1,0:T(8,128)(2,1)S(1)} %collective-permute-done.1.refs_2_), channel_id=1, source_target_pairs={{0,8},{4,12},{8,0},{12,4},{1,9},{5,13},{9,1},{13,5},{2,10},{6,14},... | collective-permute-start | bytes 350216 | tf_op jit(solution)/shard_map/ppermute | solution.py:25
  14.6 5.4 %collective-permute-start.5 = (bf16[8,7296]{1,0:T(8,128)(2,1)S(1)}, bf16[8,7296]{1,0:T(8,128)(2,1)S(1)}, u32[]{:S(2)}, u32[]{:S(2)}) collective-permute-start(bf16[8,7296]{1,0:T(8,128)(2,1)S(1)} %collective-permute-done.1.refs_2_), channel_id=1, source_target_pairs={{0,4},{4,0},{8,12},{12,8},{1,5},{5,1},{9,13},{13,9},{2,6},{6,2},{1... | collective-permute-start | bytes 350216 | tf_op jit(solution)/shard_map/ppermute | solution.py:25
  17.9 4.8 %collective-permute-start.2 = (bf16[8,7296]{1,0:T(8,128)(2,1)S(1)}, bf16[8,7296]{1,0:T(8,128)(2,1)S(1)}, u32[]{:S(2)}, u32[]{:S(2)}) collective-permute-start(bf16[8,7296]{1,0:T(8,128)(2,1)S(1)} %collective-permute-done.1.refs_2_), channel_id=1, source_target_pairs={{0,1},{1,0},{2,3},{3,2},{4,5},{5,4},{6,7},{7,6},{8,9},{9,8},{10,11... | collective-permute-start | bytes 350216 | tf_op jit(solution)/shard_map/ppermute | solution.py:25
  17.9 4.8 %collective-permute-start.8 = (bf16[8,7296]{1,0:T(8,128)(2,1)S(1)}, bf16[8,7296]{1,0:T(8,128)(2,1)S(1)}, u32[]{:S(2)}, u32[]{:S(2)}) collective-permute-start(bf16[8,7296]{1,0:T(8,128)(2,1)S(1)} %collective-permute-done.refs_1_), channel_id=1, source_target_pairs={{0,8},{4,12},{8,0},{12,4},{1,9},{5,13},{9,1},{13,5},{2,10},{6,14},... | collective-permute-start | bytes 350216 | tf_op jit(solution)/shard_map/ppermute | solution.py:25
  17.9 5.3 %collective-permute-start.4 = (bf16[8,7296]{1,0:T(8,128)(2,1)S(1)}, bf16[8,7296]{1,0:T(8,128)(2,1)S(1)}, u32[]{:S(2)}, u32[]{:S(2)}) collective-permute-start(bf16[8,7296]{1,0:T(8,128)(2,1)S(1)} %collective-permute-done.refs_1_), channel_id=1, source_target_pairs={{0,4},{4,0},{8,12},{12,8},{1,5},{5,1},{9,13},{13,9},{2,6},{6,2},{1... | collective-permute-start | bytes 350216 | tf_op jit(solution)/shard_map/ppermute | solution.py:25
  20.0 3.2 %collective-permute-start.14 = (bf16[8,7296]{1,0:T(8,128)(2,1)S(1)}, bf16[8,7296]{1,0:T(8,128)(2,1)S(1)}, u32[]{:S(2)}, u32[]{:S(2)}) collective-permute-start(bf16[8,7296]{1,0:T(8,128)(2,1)S(1)} %collective-permute-done.10.refs_11_), channel_id=1, source_target_pairs={{0,4},{4,0},{8,12},{12,8},{1,5},{5,1},{9,13},{13,9},{2,6},{6,2},{1... | collective-permute-start | bytes 350216 | tf_op jit(solution)/shard_map/ppermute | solution.py:25
  20.0 3.2 %collective-permute-start.13 = (bf16[8,7296]{1,0:T(8,128)(2,1)S(1)}, bf16[8,7296]{1,0:T(8,128)(2,1)S(1)}, u32[]{:S(2)}, u32[]{:S(2)}) collective-permute-start(bf16[8,7296]{1,0:T(8,128)(2,1)S(1)} %collective-permute-done.9.refs_10_), channel_id=1, source_target_pairs={{0,4},{4,0},{8,12},{12,8},{1,5},{5,1},{9,13},{13,9},{2,6},{6,2},{1... | collective-permute-start | bytes 350216 | tf_op jit(solution)/shard_map/ppermute | solution.py:25
  22.7 1.3 %collective-permute-start.6 = (bf16[8,7296]{1,0:T(8,128)(2,1)S(1)}, bf16[8,7296]{1,0:T(8,128)(2,1)S(1)}, u32[]{:S(2)}, u32[]{:S(2)}) collective-permute-start(bf16[8,7296]{1,0:T(8,128)(2,1)S(1)} %collective-permute-done.2.refs_3_), channel_id=1, source_target_pairs={{0,4},{4,0},{8,12},{12,8},{1,5},{5,1},{9,13},{13,9},{2,6},{6,2},{1... | collective-permute-start | bytes 350216 | tf_op jit(solution)/shard_map/ppermute | solution.py:25
  22.7 1.5 %collective-permute-start.12 = (bf16[8,7296]{1,0:T(8,128)(2,1)S(1)}, bf16[8,7296]{1,0:T(8,128)(2,1)S(1)}, u32[]{:S(2)}, u32[]{:S(2)}) collective-permute-start(bf16[8,7296]{1,0:T(8,128)(2,1)S(1)} %collective-permute-done.8.refs_9_), channel_id=1, source_target_pairs={{0,4},{4,0},{8,12},{12,8},{1,5},{5,1},{9,13},{13,9},{2,6},{6,2},{1... | collective-permute-start | bytes 350216 | tf_op jit(solution)/shard_map/ppermute | solution.py:25
  26.7 6.9 %collective-permute-start.17 = (bf16[64,512]{1,0:T(8,128)(2,1)S(1)}, bf16[64,512]{1,0:T(8,128)(2,1)S(1)}, u32[]{:S(2)}, u32[]{:S(2)}) collective-permute-start(bf16[64,512]{1,0:T(8,128)(2,1)S(1)} %gate_up.1.refs_0_), channel_id=1, source_target_pairs={{0,3},{1,2},{2,1},{3,0},{4,7},{5,6},{6,5},{7,4},{8,11},{9,10},{10,... | collective-permute-start | bytes 196616 | tf_op jit(solution)/shard_map/ppermute | solution.py:25
  29.0 7.4 %collective-permute-start.16 = (bf16[64,512]{1,0:T(8,128)(2,1)S(1)}, bf16[64,512]{1,0:T(8,128)(2,1)S(1)}, u32[]{:S(2)}, u32[]{:S(2)}) collective-permute-start(bf16[64,512]{1,0:T(8,128)(2,1)S(1)} %gate_up.1.refs_0_), channel_id=1, source_target_pairs={{0,2},{1,3},{2,0},{3,1},{4,6},{5,7},{6,4},{7,5},{8,10},{9,11},{10,... | collective-permute-start | bytes 196616 | tf_op jit(solution)/shard_map/ppermute | solution.py:25
  30.1 6.3 %collective-permute-start.15 = (bf16[64,512]{1,0:T(8,128)(2,1)S(1)}, bf16[64,512]{1,0:T(8,128)(2,1)S(1)}, u32[]{:S(2)}, u32[]{:S(2)}) collective-permute-start(bf16[64,512]{1,0:T(8,128)(2,1)S(1)} %gate_up.1.refs_0_), channel_id=1, source_target_pairs={{0,1},{1,0},{2,3},{3,2},{4,5},{5,4},{6,7},{7,6},{8,9},{9,8},{10,11... | collective-permute-start | bytes 196616 | tf_op jit(solution)/shard_map/ppermute | solution.py:25
  37.9 1.9 %collective-permute-start.18 = (bf16[16,1792]{1,0:T(8,128)(2,1)S(1)}, bf16[16,1792]{1,0:T(8,128)(2,1)S(1)}, u32[]{:S(2)}, u32[]{:S(2)}) collective-permute-start(bf16[16,1792]{1,0:T(8,128)(2,1)S(1)} %get-tuple-element.14), channel_id=1, source_target_pairs={{0,4},{4,0},{8,12},{12,8},{1,5},{5,1},{9,13},{13,9},{2,6},{6,2},{1... | collective-permute-start | bytes 172040 | tf_op jit(solution)/shard_map/ppermute | solution.py:25
  38.0 4.8 %collective-permute-start.19 = (bf16[16,1792]{1,0:T(8,128)(2,1)S(1)}, bf16[16,1792]{1,0:T(8,128)(2,1)S(1)}, u32[]{:S(2)}, u32[]{:S(2)}) collective-permute-start(bf16[16,1792]{1,0:T(8,128)(2,1)S(1)} %get-tuple-element.15), channel_id=1, source_target_pairs={{0,8},{4,12},{8,0},{12,4},{1,9},{5,13},{9,1},{13,5},{2,10},{6,14},... | collective-permute-start | bytes 172040 | tf_op jit(solution)/shard_map/ppermute | solution.py:25
  38.0 5.0 %collective-permute-start.20 = (bf16[16,1792]{1,0:T(8,128)(2,1)S(1)}, bf16[16,1792]{1,0:T(8,128)(2,1)S(1)}, u32[]{:S(2)}, u32[]{:S(2)}) collective-permute-start(bf16[16,1792]{1,0:T(8,128)(2,1)S(1)} %get-tuple-element.16), channel_id=1, source_target_pairs={{0,12},{4,8},{8,4},{12,0},{1,13},{5,9},{9,5},{13,1},{2,14},{6,10},... | collective-permute-start | bytes 172040 | tf_op jit(solution)/shard_map/ppermute | solution.py:25
  43.7 4.5 %collective-permute-start.21 = (bf16[8,1792]{1,0:T(8,128)(2,1)S(1)}, bf16[8,1792]{1,0:T(8,128)(2,1)S(1)}, u32[]{:S(2)}, u32[]{:S(2)}) collective-permute-start(bf16[8,1792]{1,0:T(8,128)(2,1)S(1)} %get-tuple-element.18), channel_id=1, source_target_pairs={{0,1},{1,0},{2,3},{3,2},{4,5},{5,4},{6,7},{7,6},{8,9},{9,8},{10,11... | collective-permute-start | bytes 86024 | tf_op jit(solution)/shard_map/ppermute | solution.py:25
  43.7 4.8 %collective-permute-start.22 = (bf16[8,1792]{1,0:T(8,128)(2,1)S(1)}, bf16[8,1792]{1,0:T(8,128)(2,1)S(1)}, u32[]{:S(2)}, u32[]{:S(2)}) collective-permute-start(bf16[8,1792]{1,0:T(8,128)(2,1)S(1)} %get-tuple-element.19), channel_id=1, source_target_pairs={{0,2},{1,3},{2,0},{3,1},{4,6},{5,7},{6,4},{7,5},{8,10},{9,11},{10,... | collective-permute-start | bytes 86024 | tf_op jit(solution)/shard_map/ppermute | solution.py:25
  45.8 5.7 %collective-permute-start.23 = (bf16[8,1792]{1,0:T(8,128)(2,1)S(1)}, bf16[8,1792]{1,0:T(8,128)(2,1)S(1)}, u32[]{:S(2)}, u32[]{:S(2)}) collective-permute-start(bf16[8,1792]{1,0:T(8,128)(2,1)S(1)} %get-tuple-element.20), channel_id=1, source_target_pairs={{0,3},{1,2},{2,1},{3,0},{4,7},{5,6},{6,5},{7,4},{8,11},{9,10},{10,... | collective-permute-start | bytes 86024 | tf_op jit(solution)/shard_map/ppermute | solution.py:25

commit v3 on v2

--- a/solution.py
+++ b/solution.py
@@ -33,13 +33,15 @@
         pltpu.make_async_copy(gates, shares, sems.at[1]),
         pltpu.make_async_copy(tokens, out.at[:, pl.ds(0, width)], sems.at[2]),
     ]
-    for move in moves:
+    for move in moves[:3]:
         move.start()
     for move in moves[:2]:
         move.wait()
     diagonal = iota((count, count), 0) == iota((count, count), 1)
     lane = iota((count, LANES), 1)
-    meta = jnp.zeros((count, LANES), jnp.float32)
+    me = lax.axis_index("ep") * lax.axis_size("sub") + lax.axis_index("sub")
+    owner = (PIECES + 1) * chosen
+    meta = jnp.where(lane == owner, me.astype(jnp.float32), jnp.zeros((count, LANES), jnp.float32))
     for k in range(chosen):
         columns = [named[k:k + 1, :].astype(jnp.float32)]
         rest = shares[k:k + 1, :]
@@ -54,17 +56,32 @@
     moves[2].wait()
 
 
-def up_kernel(count, chosen, cap, chunk, width, *refs):
-    n = len(refs) - 4
-    blocks, (w_gate, w_up, out, xs) = refs[:n], refs[n:]
+def gather_rows(arrays, xs):
+    at, held = 0, None
+    for ref in arrays:
+        rows = ref.shape[0]
+        if rows % 16 == 0:
+            xs[at:at + rows, :] = ref[...]
+            at += rows
+        elif held is None:
+            held = ref
+        else:
+            xs[at:at + 2 * rows, :] = jnp.concatenate([held[...], ref[...]], axis=0)
+            at, held = at + 2 * rows, None
+
+
+def hold_kernel(x, out):
+    out[...] = x[...]
+
+
+def up_kernel(n, count, chosen, cap, chunk, width, *refs):
+    arrays, (w_gate, w_up, out, xs, total) = refs[:n], refs[n:]
     columns = out.shape[1]
+    slots = out.shape[0]
     rows = count * chunk
-    slots = cap * chunk
+    parts = xs.shape[0] // rows
     expert = lax.axis_index("ep")
-    me = expert * lax.axis_size("sub") + lax.axis_index("sub")
-    for b in range(0, n, 2):
-        pair = jnp.concatenate([blocks[b][...], blocks[b + 1][...]], axis=0)
-        xs[b * count:(b + 2) * count, :] = pair
+    gather_rows(arrays, xs)
     step = min(256, columns)
 
     def part(j, carry):
@@ -76,57 +93,66 @@
         earlier = as_bf16((a // count == b // count) & (a < b))
         many = jnp.broadcast_to(present, (slots, rows))
         rank = jnp.dot(many.astype(jnp.bfloat16), earlier, preferred_element_type=jnp.float32)
-        slot, token = iota((slots, rows), 0), iota((slots, rows), 1)
-        owner = (token // count) ^ (me % chunk)
-        pick = (slot // cap == owner) & ((slot % cap).astype(jnp.float32) == rank) & (many > 0.5)
-        pick = as_bf16(pick)
-        to = pl.multiple_of((j ^ (me // chunk)) * slots, slots)
+        slot = iota((slots, rows), 0)
+        lane = (PIECES + 1) * chosen
+        mine = (slot // cap).astype(jnp.float32) == meta[lane:lane + 1, :]
+        pick = as_bf16(mine & ((slot % cap).astype(jnp.float32) == rank) & (many > 0.5))
         for c in range(0, columns, step):
             x = xs[pl.ds(at, rows), :width]
             gate = jnp.dot(x, w_gate[0, :, c:c + step], preferred_element_type=jnp.float32)
             up = jnp.dot(x, w_up[0, :, c:c + step], preferred_element_type=jnp.float32)
             hidden = (gate / (1.0 + jnp.exp(-gate)) * up).astype(jnp.bfloat16)
             picked = jnp.dot(pick, hidden, preferred_element_type=jnp.float32)
-            out[pl.ds(to, slots), c:c + step] = picked.astype(jnp.bfloat16)
+            if parts == 1:
+                out[:, c:c + step] = picked.astype(jnp.bfloat16)
+            else:
+                total[:, c:c + step] += picked
         return carry
 
-    lax.fori_loop(0, n // chunk, part, 0)
-
-
-def down_kernel(experts, groups, *refs):
-    parts, w_down = refs[:groups], refs[groups]
-    outs, rows = refs[groups + 1:groups + 1 + experts], refs[-1]
-    depth = parts[0].shape[1]
-    each, columns = outs[0].shape
+    if parts == 1:
+        part(0, 0)
+    else:
+        total[...] = jnp.zeros_like(total)
+        lax.fori_loop(0, parts, part, 0)
+        out[...] = total[...].astype(jnp.bfloat16)
+
+
+def down_kernel(experts, first, n, last, *refs):
+    parts, w_down = refs[:n][::-1], refs[n]
+    before = None if first == 0 else refs[n + 1]
+    outs, rows = refs[n + 1 + (first > 0):-1], refs[-1]
+    count, depth = parts[0].shape
+    columns = w_down.shape[2]
+    each = count // experts
     ep, sub = lax.axis_index("ep"), lax.axis_index("sub")
     for e in range(experts):
         at = pl.multiple_of((ep ^ e) * each, each)
-        for k in range(groups):
+        for k in range(n):
             rows[e * each:(e + 1) * each, k * depth:(k + 1) * depth] = parts[k][pl.ds(at, each), :]
     step = 256 if columns % 256 == 0 else 128
     for c in range(0, columns, step):
-        total = None
-        for k in range(groups):
-            d = pl.multiple_of((sub ^ k) * depth, depth)
+        total = None if before is None else before[:, c:c + step]
+        for k in range(n):
+            d = pl.multiple_of((sub ^ (first + k)) * depth, depth)
             term = jnp.dot(
                 rows[:, k * depth:(k + 1) * depth],
                 w_down[0, pl.ds(d, depth), c:c + step],
                 preferred_element_type=jnp.float32,
             )
             total = term if total is None else total + term
+        if not last:
+            outs[0][:, c:c + step] = total
+            continue
         total = total.astype(jnp.bfloat16)
         for e in range(experts):
             outs[e][:, c:c + step] = total[e * each:(e + 1) * each, :]
 
 
-def combine_kernel(experts, groups, count, chosen, cap, width, *refs):
-    blocks, got = refs[:groups], refs[groups:groups + experts]
-    outs, rows = refs[groups + experts:-1], refs[-1]
-    each = got[0].shape[0]
+def share_kernel(experts, groups, count, chosen, cap, width, *refs):
+    blocks, outs = refs[:groups], refs[groups:]
+    each = groups * cap
     tokens = groups * count
     ep, sub = lax.axis_index("ep"), lax.axis_index("sub")
-    for e in range(experts):
-        rows[e * each:(e + 1) * each, :] = got[e][...]
     meta = jnp.concatenate([b[:, width:width + LANES].astype(jnp.float32) for b in blocks], axis=0)
     a, b = iota((tokens, tokens), 0), iota((tokens, tokens), 1)
     earlier = as_bf16((a // count == b // count) & (b < a))
@@ -146,17 +172,26 @@
                 at = (p + 1) * chosen + k
                 share = share + meta[:, at:at + 1] * named[:, k:k + 1]
             weights[p].append(jnp.where(taken, share, 0.0))
-    weights = [jnp.concatenate(w, axis=1).astype(jnp.bfloat16) for w in weights]
+    for p in range(PIECES):
+        outs[p][...] = jnp.concatenate(weights[p], axis=1).astype(jnp.bfloat16)
+
+
+def combine_kernel(experts, groups, count, *refs):
+    weights, got = refs[:PIECES], refs[PIECES:PIECES + experts]
+    outs, rows = refs[PIECES + experts:-1], refs[-1]
+    each = got[0].shape[0]
+    for e in range(experts):
+        rows[e * each:(e + 1) * each, :] = got[e][...]
     total = 0.0
     for w in weights[::-1]:
-        total = total + jnp.dot(w, rows[...], preferred_element_type=jnp.float32)
+        total = total + jnp.dot(w[...], rows[...], preferred_element_type=jnp.float32)
     total = total.astype(jnp.bfloat16)
     for k in range(groups):
         outs[k][...] = total[k * count:(k + 1) * count, :]
 
 
 def place_kernel(*refs):
-    parts, out, sems = refs[:-2], refs[-2], refs[-1]
+    parts, out, sems = refs[:-2][::-1], refs[-2], refs[-1]
     columns = parts[0].shape[1]
     sub = lax.axis_index("sub")
     moves = []
@@ -187,17 +222,27 @@
     own = pl.pallas_call(
         pack_kernel,
         out_shape=array(count, width + LANES),
-        in_specs=[HBM, HBM, HBM],
+        in_specs=[HBM] * 3,
         out_specs=VMEM,
         scratch_shapes=[
             pltpu.VMEM((chosen, count), jnp.int32),
             pltpu.VMEM((chosen, count), jnp.float32),
             pltpu.SemaphoreType.DMA((3,)),
         ],
-        compiler_params=limit(1),
-        cost_estimate=pl.CostEstimate(flops=20000000000, bytes_accessed=0, transcendentals=0),
+        compiler_params=pltpu.CompilerParams(vmem_limit_bytes=67_000_000),
         name="pack",
     )(tokens, routes.T, gates.T)
+
+    def hold(x):
+        return pl.pallas_call(
+            hold_kernel,
+            out_shape=array(*x.shape),
+            in_specs=[VMEM],
+            out_specs=VMEM,
+            cost_estimate=pl.CostEstimate(flops=3000000000, bytes_accessed=0, transcendentals=0),
+            compiler_params=limit(1),
+            name="hold",
+        )(x)
 
     got = {(0, 0): own}
     single = [1 << b for b in range(groups.bit_length() - 1)]
@@ -206,6 +251,8 @@
         got[kz, 0] = swap(own, "sub", groups, kz)
     for ky in far:
         got[0, ky] = swap(own, "ep", experts, ky)
+    got[0, 2] = hold(got[0, 2])
+    got[1, 0] = hold(got[1, 0])
     relayed = [kz for kz in range(1, groups) if kz not in single]
     for kz in relayed:
         for ky in far:
@@ -216,44 +263,68 @@
     for kz in single:
         for ky in far:
             got[kz, ky] = swap(got[kz, 0], "ep", experts, ky)
+    TIE = {(0, 0): (2, 2), (1, 0): (2, 2), (2, 0): (3, 2), (0, 2): (3, 2)}
     for kz in range(groups):
         for ky in range(0, experts, 2):
-            got[kz, ky + 1] = swap(got[kz, ky], "ep", experts, 1)
-    blocks = [got[kz, ke] for ke in range(experts) for kz in range(groups)]
+            block = got[kz, ky]
+            if (kz, ky) in TIE:
+                block = lax.optimization_barrier((block, got[TIE[kz, ky]]))[0]
+            got[kz, ky + 1] = swap(block, "ep", experts, 1)
+    arrays = [got[kz, ke] for ke in range(experts) for kz in range(groups)][::-1]
 
     columns = gate_weight.shape[2]
     hidden = pl.pallas_call(
-        functools.partial(up_kernel, count, chosen, cap, chunk, width),
+        functools.partial(up_kernel, len(arrays), count, chosen, cap, chunk, width),
         out_shape=array(devices * cap, columns),
-        in_specs=[VMEM] * (devices + 2),
+        in_specs=[VMEM] * (len(arrays) + 2),
         out_specs=VMEM,
-        scratch_shapes=[pltpu.VMEM((devices * count, width + LANES), jnp.bfloat16)],
+        scratch_shapes=[
+            pltpu.VMEM((devices * count, width + LANES), jnp.bfloat16),
+            pltpu.VMEM((devices * cap, columns), jnp.float32),
+        ],
         compiler_params=limit(12 if devices <= 16 else 24),
         name="gate_up",
-    )(*blocks, gate_weight, up_weight)
+    )(*arrays, gate_weight, up_weight)
 
     parts = [hidden] + [swap(hidden, "sub", groups, k) for k in range(1, groups)]
+    shares = pl.pallas_call(
+        functools.partial(share_kernel, experts, groups, count, chosen, cap, width),
+        out_shape=[array(groups * count, devices * cap)] * PIECES,
+        in_specs=[VMEM] * groups,
+        out_specs=[VMEM] * PIECES,
+        compiler_params=limit(8 if devices <= 16 else 24),
+        name="shares",
+    )(*[got[k, 0] for k in range(groups)])
     out_cols = down_weight.shape[2]
-    sent = pl.pallas_call(
-        functools.partial(down_kernel, experts, groups),
-        out_shape=[array(groups * cap, out_cols)] * experts,
-        in_specs=[VMEM] * (groups + 1),
-        out_specs=[VMEM] * experts,
-        scratch_shapes=[pltpu.VMEM((devices * cap, groups * columns), jnp.bfloat16)],
-        compiler_params=limit(8 if devices <= 16 else 24),
-        name="down",
-    )(*parts, down_weight)
+
+    def down(first, n, *more):
+        last = first + n == groups
+        out = [array(groups * cap, out_cols)] * experts
+        if not last:
+            out = [jax.ShapeDtypeStruct((devices * cap, out_cols), jnp.float32)]
+        return pl.pallas_call(
+            functools.partial(down_kernel, experts, first, n, last),
+            out_shape=out,
+            in_specs=[VMEM] * (n + 1 + (first > 0)),
+            out_specs=[VMEM] * len(out),
+            scratch_shapes=[pltpu.VMEM((devices * cap, n * columns), jnp.bfloat16)],
+            compiler_params=limit(8 if devices <= 16 else 24),
+            name=f"down_{first}",
+        )(*(parts[first:first + n][::-1] if first else more), down_weight, *(more if first else ()))
+
+    own_part, *shares = lax.optimization_barrier([parts[0]] + list(shares))
+    sent = down(1, groups - 1, *down(0, 1, own_part))
 
     came = [sent[0]] + [swap(sent[e], "ep", experts, e) for e in range(1, experts)]
     summed = pl.pallas_call(
-        functools.partial(combine_kernel, experts, groups, count, chosen, cap, width),
+        functools.partial(combine_kernel, experts, groups, count),
         out_shape=[array(count, out_cols)] * groups,
-        in_specs=[VMEM] * (groups + experts),
+        in_specs=[VMEM] * (PIECES + experts),
         out_specs=[VMEM] * groups,
         scratch_shapes=[pltpu.VMEM((devices * cap, out_cols), jnp.bfloat16)],
         compiler_params=limit(8 if devices <= 16 else 24),
         name="combine",
-    )(*[got[k, 0] for k in range(groups)], *came)
+    )(*shares, *came)
 
     home = [summed[0]] + [swap(summed[k], "sub", groups, k) for k in range(1, groups)]
     return pl.pallas_call(
@@ -264,7 +335,7 @@
         scratch_shapes=[pltpu.SemaphoreType.DMA((groups,))],
         compiler_params=limit(1),
         name="place",
-    )(*home)
+    )(*home[::-1])
 
 
 def solution(mesh):

time: 52.3 us -> 51.2 us (0.979)
  waiting for transfers between devices: 21.6 us -> 18.7 us
  starting transfers between devices: 22.3 us -> 25 us
  local copies, waits for them, and re-layouts: 2.68 us -> 0.04 us
  Pallas kernels: 5.44 us -> 7.17 us
    ppermute x24, waiting for transfers between devices: 21.6 us -> 18.7 us  [swap(): return lax.ppermute(x, axis, [(i, i ^ k) for i in range(size)])]
    ppermute x24, starting transfers between devices: 22.3 us -> 25 us  [swap(): return lax.ppermute(x, axis, [(i, i ^ k) for i in range(size)])]
    unnamed x14, local copies, waits for them, and re-layouts: 2.68 us -> 0.04 us
    pallas_call x1, Pallas kernels: 0.27 us -> 1.59 us  [body(): pl.pallas_call(pack_kernel, out_shape=array(count, width + LANES), in_spe...]
    pallas_call x3 -> x7, Pallas kernels: 4.5 us -> 4.91 us  [the longest x1 2.51 us: body(): pl.pallas_call(functools.partial(up_kernel, len(arrays), count, chosen, c...]
  transfers between devices with their start and end apart: 24 -> 24, of which waited for: 12 -> 14; matrix products, arithmetic and copies ran while one was open for 0% -> 0% of each run, Pallas kernels for 0% -> 2%
where the time goes in v3:
time: 51.2 us; the launch traced here: 51.1 us
  starting transfers between devices  25 us (49%)
  waiting for transfers between devices  18.7 us (37%)
  Pallas kernels  7.17 us (14%)
    ppermute x24, starting transfers between devices, swap(): return lax.ppermute(x, axis, [(i, i ^ k) for i in range(size)])  25 us
    ppermute x24, waiting for transfers between devices, swap(): return lax.ppermute(x, axis, [(i, i ^ k) for i in range(size)])  18.7 us
    pallas_call x1, Pallas kernels, body(): pl.pallas_call(functools.partial(up_kernel, len(arrays), count, chosen, c...  2.51 us
    pallas_call x1, Pallas kernels, body(): pl.pallas_call(pack_kernel, out_shape=array(count, width + LANES), in_spe...  1.59 us
    pallas_call x2, Pallas kernels, down(): pl.pallas_call(functools.partial(down_kernel, experts, first, n, last), o...  1.52 us
  transfers between devices with their start and end apart: 24, of which 14 were waited for; matrix products, arithmetic and copies ran while one was open for 0% of the time, Pallas kernels for 2%

profile of v3, /device:TPU:0, one launch (start us, length us, event | category | flops | bytes accessed | tf_op | source)
XLA Modules:
  0.0 51.1 jit_solution(6148418487542708399)
XLA Ops:
  0.0 1.6 %pack.1.refs_15_.refs_0_ = bf16[8,7296]{1,0:T(8,128)(2,1)} custom-call(bf16[8,7168]{1,0:T(8,128)(2,1)} %tokens.1, s32[2,8]{1,0:T(2,128)} %bitcast.8, f32[2,8]{1,0:T(2,128)} %bitcast.9), custom_call_target="tpu_custom_call" | custom-call | tf_op jit(solution)/shard_map/pack/pallas_call | solution.py:222
  1.6 3.0 %collective-permute-start = (bf16[8,7296]{1,0:T(8,128)(2,1)}, bf16[8,7296]{1,0:T(8,128)(2,1)S(1)}, u32[]{:S(2)}, u32[]{:S(2)}) collective-permute-start(bf16[8,7296]{1,0:T(8,128)(2,1)} %pack.1.refs_15_.refs_0_), channel_id=1, source_target_pairs={{0,8},{4,12},{8,0},{12,4},{1,9},{5,13},{9,1},{13,5},{2,10},{6,14},... | collective-permute-start | bytes 350216 | tf_op jit(solution)/shard_map/ppermute | solution.py:25
  4.6 2.6 %collective-permute-start.3 = (bf16[8,7296]{1,0:T(8,128)(2,1)}, bf16[8,7296]{1,0:T(8,128)(2,1)S(1)}, u32[]{:S(2)}, u32[]{:S(2)}) collective-permute-start(bf16[8,7296]{1,0:T(8,128)(2,1)} %pack.1.refs_15_.refs_0_), channel_id=1, source_target_pairs={{0,2},{1,3},{2,0},{3,1},{4,6},{5,7},{6,4},{7,5},{8,10},{9,11},{10,... | collective-permute-start | bytes 350216 | tf_op jit(solution)/shard_map/ppermute | solution.py:25
  7.2 1.6 %collective-permute-start.6 = (bf16[8,7296]{1,0:T(8,128)(2,1)}, bf16[8,7296]{1,0:T(8,128)(2,1)S(1)}, u32[]{:S(2)}, u32[]{:S(2)}) collective-permute-start(bf16[8,7296]{1,0:T(8,128)(2,1)} %pack.1.refs_15_.refs_0_), channel_id=1, source_target_pairs={{0,1},{1,0},{2,3},{3,2},{4,5},{5,4},{6,7},{7,6},{8,9},{9,8},{10,11... | collective-permute-start | bytes 350216 | tf_op jit(solution)/shard_map/ppermute | solution.py:25
  8.8 0.0 collective-permute-done.x
  8.8 0.0 copy-start
  8.8 0.0 slice-start.3
  8.8 0.0 slice-start.5
  8.9 3.1 %collective-permute-start.1 = (bf16[8,7296]{1,0:T(8,128)(2,1)S(1)}, bf16[8,7296]{1,0:T(8,128)(2,1)S(1)}, u32[]{:S(2)}, u32[]{:S(2)}) collective-permute-start(bf16[8,7296]{1,0:T(8,128)(2,1)S(1)} %hold.2.refs_7_), channel_id=1, source_target_pairs={{0,3},{1,2},{2,1},{3,0},{4,7},{5,6},{6,5},{7,4},{8,11},{9,10},{10,... | collective-permute-start | bytes 350216 | tf_op jit(solution)/shard_map/ppermute | solution.py:25
  12.0 3.2 %collective-permute-done.3.refs_13_.refs_2_ = bf16[8,7296]{1,0:T(8,128)(2,1)S(1)} collective-permute-done((bf16[8,7296]{1,0:T(8,128)(2,1)}, bf16[8,7296]{1,0:T(8,128)(2,1)S(1)}, u32[]{:S(2)}, u32[]{:S(2)}) %collective-permute-start.3) | collective-permute-done | bytes 116768 | tf_op jit(solution)/shard_map/ppermute | solution.py:25
  15.2 0.0 collective-permute-start.4
  15.2 0.0 collective-permute-done.6.x
  15.2 0.0 slice-start.1
  15.2 2.1 %collective-permute-start.7 = (bf16[8,7296]{1,0:T(8,128)(2,1)S(1)}, bf16[8,7296]{1,0:T(8,128)(2,1)S(1)}, u32[]{:S(2)}, u32[]{:S(2)}) collective-permute-start(bf16[8,7296]{1,0:T(8,128)(2,1)S(1)} %hold.3.refs_14_.refs_1_), channel_id=1, source_target_pairs={{0,8},{4,12},{8,0},{12,4},{1,9},{5,13},{9,1},{13,5},{2,10},{6,14},... | collective-permute-start | bytes 350216 | tf_op jit(solution)/shard_map/ppermute | solution.py:25
  17.3 0.0 collective-permute-start.10
  17.3 2.7 %collective-permute-done.4.refs_5_ = bf16[8,7296]{1,0:T(8,128)(2,1)S(1)} collective-permute-done((bf16[8,7296]{1,0:T(8,128)(2,1)S(1)}, bf16[8,7296]{1,0:T(8,128)(2,1)S(1)}, u32[]{:S(2)}, u32[]{:S(2)}) %collective-permute-start.4) | collective-permute-done | bytes 116768 | tf_op jit(solution)/shard_map/ppermute | solution.py:25
  20.0 0.0 collective-permute-start.13
  20.0 0.0 collective-permute-done.1.refs_4_
  20.0 0.5 collective-permute-start.12
  20.5 0.0 collective-permute-start.9
  20.5 1.6 %collective-permute-done.10.refs_12_.refs_3_ = bf16[8,7296]{1,0:T(8,128)(2,1)S(1)} collective-permute-done((bf16[8,7296]{1,0:T(8,128)(2,1)S(1)}, bf16[8,7296]{1,0:T(8,128)(2,1)S(1)}, u32[]{:S(2)}, u32[]{:S(2)}) %collective-permute-start.10) | collective-permute-done | bytes 116768 | tf_op jit(solution)/shard_map/ppermute | solution.py:25
  22.1 0.0 copy-done
  22.1 0.0 collective-permute-start.14
  22.1 0.0 collective-permute-done.7.refs_6_
  22.1 0.5 collective-permute-start.5
  22.6 0.0 collective-permute-done.13.refs_10_
  22.6 0.1 collective-permute-start.2
  22.7 0.0 collective-permute-done.12.refs_9_
  22.7 0.4 collective-permute-start.11
  23.1 0.0 collective-permute-done.9.refs_3_
  23.1 0.1 collective-permute-start.8
  23.2 0.2 collective-permute-done.14.refs_11_
  23.4 0.2 collective-permute-done.5.refs_1_
  23.6 0.5 %collective-permute-done.11.refs_8_ = bf16[8,7296]{1,0:T(8,128)(2,1)S(1)} collective-permute-done((bf16[8,7296]{1,0:T(8,128)(2,1)S(1)}, bf16[8,7296]{1,0:T(8,128)(2,1)S(1)}, u32[]{:S(2)}, u32[]{:S(2)}) %collective-permute-start.11) | collective-permute-done | bytes 116768 | tf_op jit(solution)/shard_map/ppermute | solution.py:25
  24.1 0.0 collective-permute-done.2.refs_0_
  24.1 0.3 collective-permute-done.8.refs_2_
  24.5 0.0 slice-done.2
  24.5 0.0 slice-done.4
  24.5 0.0 slice-done.3
  24.5 0.0 slice-done.5
  24.5 2.5 %gate_up.1.refs_0_ = bf16[64,512]{1,0:T(8,128)(2,1)S(1)} custom-call(bf16[8,7296]{1,0:T(8,128)(2,1)S(1)} %collective-permute-done.2.refs_0_, bf16[8,7296]{1,0:T(8,128)(2,1)S(1)} %collective-permute-done.5.refs_1_, bf16[8,7296]{1,0:T(8,128)(2,1)S(1)} %collective-permute-done.8.refs_2_, bf16[8,7296]{1,0:T(8,128)(2,1)S(1)} %collective-permute-done.9.refs_3_, ...), custom_call_target="tpu_custom_call" | custom-call | tf_op jit(solution)/shard_map/gate_up/pallas_call | solution.py:276
  27.0 4.0 %collective-permute-start.15 = (bf16[64,512]{1,0:T(8,128)(2,1)S(1)}, bf16[64,512]{1,0:T(8,128)(2,1)S(1)}, u32[]{:S(2)}, u32[]{:S(2)}) collective-permute-start(bf16[64,512]{1,0:T(8,128)(2,1)S(1)} %gate_up.1.refs_0_), channel_id=1, source_target_pairs={{0,3},{1,2},{2,1},{3,0},{4,7},{5,6},{6,5},{7,4},{8,11},{9,10},{10,... | collective-permute-start | bytes 196616 | tf_op jit(solution)/shard_map/ppermute | solution.py:25
  31.0 0.0 collective-permute-start.16
  31.0 0.6 %collective-permute-start.17 = (bf16[64,512]{1,0:T(8,128)(2,1)S(1)}, bf16[64,512]{1,0:T(8,128)(2,1)S(1)}, u32[]{:S(2)}, u32[]{:S(2)}) collective-permute-start(bf16[64,512]{1,0:T(8,128)(2,1)S(1)} %gate_up.1.refs_0_), channel_id=1, source_target_pairs={{0,1},{1,0},{2,3},{3,2},{4,5},{5,4},{6,7},{7,6},{8,9},{9,8},{10,11... | collective-permute-start | bytes 196616 | tf_op jit(solution)/shard_map/ppermute | solution.py:25
  31.7 0.6 %shares.1 = (bf16[32,64]{1,0:T(8,128)(2,1)S(1)}, bf16[32,64]{1,0:T(8,128)(2,1)S(1)}, bf16[32,64]{1,0:T(8,128)(2,1)S(1)}) custom-call(bf16[8,7296]{1,0:T(8,128)(2,1)S(1)} %copy-done, bf16[8,7296]{1,0:T(8,128)(2,1)S(1)} %hold.3.refs_14_.refs_1_, bf16[8,7296]{1,0:T(8,128)(2,1)S(1)} %collective-permute-done.3.refs_13_.refs_2_, ...), custom_call_target="tpu_custom_call" | custom-call | tf_op jit(solution)/shard_map/shares/pallas_call | solution.py:290
  32.3 0.4 down_0.1.refs_4_
  32.8 1.1 %collective-permute-done.15.refs_0_ = bf16[64,512]{1,0:T(8,128)(2,1)S(1)} collective-permute-done((bf16[64,512]{1,0:T(8,128)(2,1)S(1)}, bf16[64,512]{1,0:T(8,128)(2,1)S(1)}, u32[]{:S(2)}, u32[]{:S(2)}) %collective-permute-start.15) | collective-permute-done | bytes 65568 | tf_op jit(solution)/shard_map/ppermute | solution.py:25
  33.9 2.5 %collective-permute-done.16.refs_1_ = bf16[64,512]{1,0:T(8,128)(2,1)S(1)} collective-permute-done((bf16[64,512]{1,0:T(8,128)(2,1)S(1)}, bf16[64,512]{1,0:T(8,128)(2,1)S(1)}, u32[]{:S(2)}, u32[]{:S(2)}) %collective-permute-start.16) | collective-permute-done | bytes 65568 | tf_op jit(solution)/shard_map/ppermute | solution.py:25
  36.4 0.3 collective-permute-done.17.refs_2_
  36.7 1.1 %down_1.1 = (bf16[16,1792]{1,0:T(8,128)(2,1)S(1)}, bf16[16,1792]{1,0:T(8,128)(2,1)S(1)}, bf16[16,1792]{1,0:T(8,128)(2,1)S(1)}, bf16[16,1792]{1,0:T(8,128)(2,1)S(1)}) custom-call(bf16[64,512]{1,0:T(8,128)(2,1)S(1)} %collective-permute-done.15.refs_0_, bf16[64,512]{1,0:T(8,128)(2,1)S(1)} %collective-permute-done.16.refs_1_, ...), custom_call_target="tpu_custom_call" | custom-call | tf_op jit(solution)/shard_map/down_1/pallas_call | solution.py:305
  37.8 0.1 collective-permute-start.18
  37.8 0.1 collective-permute-start.19
  38.0 1.7 %collective-permute-start.20 = (bf16[16,1792]{1,0:T(8,128)(2,1)S(1)}, bf16[16,1792]{1,0:T(8,128)(2,1)S(1)}, u32[]{:S(2)}, u32[]{:S(2)}) collective-permute-start(bf16[16,1792]{1,0:T(8,128)(2,1)S(1)} %get-tuple-element.38), channel_id=1, source_target_pairs={{0,12},{4,8},{8,4},{12,0},{1,13},{5,9},{9,5},{13,1},{2,14},{6,10},... | collective-permute-start | bytes 172040 | tf_op jit(solution)/shard_map/ppermute | solution.py:25
  39.7 0.0 collective-permute-done.18.refs_4_
  39.7 2.9 %collective-permute-done.19.refs_5_ = bf16[16,1792]{1,0:T(8,128)(2,1)S(1)} collective-permute-done((bf16[16,1792]{1,0:T(8,128)(2,1)S(1)}, bf16[16,1792]{1,0:T(8,128)(2,1)S(1)}, u32[]{:S(2)}, u32[]{:S(2)}) %collective-permute-start.19) | collective-permute-done | bytes 57376 | tf_op jit(solution)/shard_map/ppermute | solution.py:25
  42.6 0.3 collective-permute-done.20.refs_6_
  42.9 0.2 combine.1
  43.2 2.5 %collective-permute-start.21 = (bf16[8,1792]{1,0:T(8,128)(2,1)S(1)}, bf16[8,1792]{1,0:T(8,128)(2,1)S(1)}, u32[]{:S(2)}, u32[]{:S(2)}) collective-permute-start(bf16[8,1792]{1,0:T(8,128)(2,1)S(1)} %get-tuple-element.39), channel_id=1, source_target_pairs={{0,3},{1,2},{2,1},{3,0},{4,7},{5,6},{6,5},{7,4},{8,11},{9,10},{10,... | collective-permute-start | bytes 86024 | tf_op jit(solution)/shard_map/ppermute | solution.py:25
  45.6 0.4 collective-permute-start.22
  46.1 1.6 %collective-permute-start.23 = (bf16[8,1792]{1,0:T(8,128)(2,1)S(1)}, bf16[8,1792]{1,0:T(8,128)(2,1)S(1)}, u32[]{:S(2)}, u32[]{:S(2)}) collective-permute-start(bf16[8,1792]{1,0:T(8,128)(2,1)S(1)} %get-tuple-element.41), channel_id=1, source_target_pairs={{0,1},{1,0},{2,3},{3,2},{4,5},{5,4},{6,7},{7,6},{8,9},{9,8},{10,11... | collective-permute-start | bytes 86024 | tf_op jit(solution)/shard_map/ppermute | solution.py:25
  47.6 1.4 %collective-permute-done.21.refs_0_ = bf16[8,1792]{1,0:T(8,128)(2,1)S(1)} collective-permute-done((bf16[8,1792]{1,0:T(8,128)(2,1)S(1)}, bf16[8,1792]{1,0:T(8,128)(2,1)S(1)}, u32[]{:S(2)}, u32[]{:S(2)}) %collective-permute-start.21) | collective-permute-done | bytes 28704 | tf_op jit(solution)/shard_map/ppermute | solution.py:25
  49.0 1.4 %collective-permute-done.22.refs_1_ = bf16[8,1792]{1,0:T(8,128)(2,1)S(1)} collective-permute-done((bf16[8,1792]{1,0:T(8,128)(2,1)S(1)}, bf16[8,1792]{1,0:T(8,128)(2,1)S(1)}, u32[]{:S(2)}, u32[]{:S(2)}) %collective-permute-start.22) | collective-permute-done | bytes 28704 | tf_op jit(solution)/shard_map/ppermute | solution.py:25
  50.4 0.0 collective-permute-done.23.refs_2_
  50.4 0.7 %place.1 = bf16[8,7168]{1,0:T(8,128)(2,1)} custom-call(bf16[8,1792]{1,0:T(8,128)(2,1)S(1)} %collective-permute-done.21.refs_0_, bf16[8,1792]{1,0:T(8,128)(2,1)S(1)} %collective-permute-done.22.refs_1_, bf16[8,1792]{1,0:T(8,128)(2,1)S(1)} %collective-permute-done.23.refs_2_, bf16[8,1792]{1,0:T(8,128)(2,1)S(1)} %get-tuple-element.42.refs_3_), custom_call_target="tpu_custom_call" | custom-call | tf_op jit(solution)/shard_map/place/pallas_call | solution.py:330
  (10 shorter events, 0.0 us)
Async XLA Ops:
  1.6 7.2 %collective-permute-start = (bf16[8,7296]{1,0:T(8,128)(2,1)}, bf16[8,7296]{1,0:T(8,128)(2,1)S(1)}, u32[]{:S(2)}, u32[]{:S(2)}) collective-permute-start(bf16[8,7296]{1,0:T(8,128)(2,1)} %pack.1.refs_15_.refs_0_), channel_id=1, source_target_pairs={{0,8},{4,12},{8,0},{12,4},{1,9},{5,13},{9,1},{13,5},{2,10},{6,14},... | collective-permute-start | bytes 350216 | tf_op jit(solution)/shard_map/ppermute | solution.py:25
  4.6 10.5 %collective-permute-start.3 = (bf16[8,7296]{1,0:T(8,128)(2,1)}, bf16[8,7296]{1,0:T(8,128)(2,1)S(1)}, u32[]{:S(2)}, u32[]{:S(2)}) collective-permute-start(bf16[8,7296]{1,0:T(8,128)(2,1)} %pack.1.refs_15_.refs_0_), channel_id=1, source_target_pairs={{0,2},{1,3},{2,0},{3,1},{4,6},{5,7},{6,4},{7,5},{8,10},{9,11},{10,... | collective-permute-start | bytes 350216 | tf_op jit(solution)/shard_map/ppermute | solution.py:25
  7.2 7.9 %collective-permute-start.6 = (bf16[8,7296]{1,0:T(8,128)(2,1)}, bf16[8,7296]{1,0:T(8,128)(2,1)S(1)}, u32[]{:S(2)}, u32[]{:S(2)}) collective-permute-start(bf16[8,7296]{1,0:T(8,128)(2,1)} %pack.1.refs_15_.refs_0_), channel_id=1, source_target_pairs={{0,1},{1,0},{2,3},{3,2},{4,5},{5,4},{6,7},{7,6},{8,9},{9,8},{10,11... | collective-permute-start | bytes 350216 | tf_op jit(solution)/shard_map/ppermute | solution.py:25
  8.8 15.7 %slice-start.2 = ((s8[7340032]{0:T(1024)(128)(4,1)}), s8[4194304]{0:T(1024)(128)(4,1)S(1)}, s32[]{:S(2)}) async-start(s8[7340032]{0:T(1024)(128)(4,1)} %bitcast.4), calls=%async_computation.2 | async-start | bytes 8388608
  8.8 15.7 %slice-start.4 = ((s8[7340032]{0:T(1024)(128)(4,1)}), s8[4194304]{0:T(1024)(128)(4,1)S(1)}, s32[]{:S(2)}) async-start(s8[7340032]{0:T(1024)(128)(4,1)} %bitcast.6), calls=%async_computation.4 | async-start | bytes 8388608
  8.8 13.3 %copy-start = (bf16[8,7296]{1,0:T(8,128)(2,1)S(1)}, bf16[8,7296]{1,0:T(8,128)(2,1)}, u32[]{:S(2)}) copy-start(bf16[8,7296]{1,0:T(8,128)(2,1)} %pack.1.refs_15_.refs_0_) | copy-start | bytes 350212
  8.8 15.6 %slice-start.3 = ((s8[7340032]{0:T(1024)(128)(4,1)}), s8[3145728]{0:T(1024)(128)(4,1)S(1)}, s32[]{:S(2)}) async-start(s8[7340032]{0:T(1024)(128)(4,1)} %bitcast.4), calls=%async_computation.3 | async-start | bytes 6291456
  8.8 15.6 %slice-start.5 = ((s8[7340032]{0:T(1024)(128)(4,1)}), s8[3145728]{0:T(1024)(128)(4,1)S(1)}, s32[]{:S(2)}) async-start(s8[7340032]{0:T(1024)(128)(4,1)} %bitcast.6), calls=%async_computation.5 | async-start | bytes 6291456
  8.9 11.1 %collective-permute-start.1 = (bf16[8,7296]{1,0:T(8,128)(2,1)S(1)}, bf16[8,7296]{1,0:T(8,128)(2,1)S(1)}, u32[]{:S(2)}, u32[]{:S(2)}) collective-permute-start(bf16[8,7296]{1,0:T(8,128)(2,1)S(1)} %hold.2.refs_7_), channel_id=1, source_target_pairs={{0,3},{1,2},{2,1},{3,0},{4,7},{5,6},{6,5},{7,4},{8,11},{9,10},{10,... | collective-permute-start | bytes 350216 | tf_op jit(solution)/shard_map/ppermute | solution.py:25
  15.2 4.8 %collective-permute-start.4 = (bf16[8,7296]{1,0:T(8,128)(2,1)S(1)}, bf16[8,7296]{1,0:T(8,128)(2,1)S(1)}, u32[]{:S(2)}, u32[]{:S(2)}) collective-permute-start(bf16[8,7296]{1,0:T(8,128)(2,1)S(1)} %collective-permute-done.3.refs_13_.refs_2_), channel_id=1, source_target_pairs={{0,8},{4,12},{8,0},{12,4},{1,9},{5,13},{9,1},{13,5},{2,10},{6,14},... | collective-permute-start | bytes 350216 | tf_op jit(solution)/shard_map/ppermute | solution.py:25
  15.2 17.1 %slice-start = ((s8[7340032]{0:T(1024)(128)(4,1)}), s8[4194304]{0:T(1024)(128)(4,1)S(1)}, s32[]{:S(2)}) async-start(s8[7340032]{0:T(1024)(128)(4,1)} %bitcast.2), calls=%async_computation | async-start | bytes 8388608
  15.2 17.1 %slice-start.1 = ((s8[7340032]{0:T(1024)(128)(4,1)}), s8[3145728]{0:T(1024)(128)(4,1)S(1)}, s32[]{:S(2)}) async-start(s8[7340032]{0:T(1024)(128)(4,1)} %bitcast.2), calls=%async_computation.1 | async-start | bytes 6291456
  15.2 6.9 %collective-permute-start.7 = (bf16[8,7296]{1,0:T(8,128)(2,1)S(1)}, bf16[8,7296]{1,0:T(8,128)(2,1)S(1)}, u32[]{:S(2)}, u32[]{:S(2)}) collective-permute-start(bf16[8,7296]{1,0:T(8,128)(2,1)S(1)} %hold.3.refs_14_.refs_1_), channel_id=1, source_target_pairs={{0,8},{4,12},{8,0},{12,4},{1,9},{5,13},{9,1},{13,5},{2,10},{6,14},... | collective-permute-start | bytes 350216 | tf_op jit(solution)/shard_map/ppermute | solution.py:25
  17.3 4.8 %collective-permute-start.10 = (bf16[8,7296]{1,0:T(8,128)(2,1)S(1)}, bf16[8,7296]{1,0:T(8,128)(2,1)S(1)}, u32[]{:S(2)}, u32[]{:S(2)}) collective-permute-start(bf16[8,7296]{1,0:T(8,128)(2,1)S(1)} %collective-permute-done.3.refs_13_.refs_2_), channel_id=1, source_target_pairs={{0,1},{1,0},{2,3},{3,2},{4,5},{5,4},{6,7},{7,6},{8,9},{9,8},{10,11... | collective-permute-start | bytes 350216 | tf_op jit(solution)/shard_map/ppermute | solution.py:25
  20.0 2.6 %collective-permute-start.13 = (bf16[8,7296]{1,0:T(8,128)(2,1)S(1)}, bf16[8,7296]{1,0:T(8,128)(2,1)S(1)}, u32[]{:S(2)}, u32[]{:S(2)}) collective-permute-start(bf16[8,7296]{1,0:T(8,128)(2,1)S(1)} %hold.3.refs_14_.refs_1_), channel_id=1, source_target_pairs={{0,4},{4,0},{8,12},{12,8},{1,5},{5,1},{9,13},{13,9},{2,6},{6,2},{1... | collective-permute-start | bytes 350216 | tf_op jit(solution)/shard_map/ppermute | solution.py:25
  20.0 2.7 %collective-permute-start.12 = (bf16[8,7296]{1,0:T(8,128)(2,1)S(1)}, bf16[8,7296]{1,0:T(8,128)(2,1)S(1)}, u32[]{:S(2)}, u32[]{:S(2)}) collective-permute-start(bf16[8,7296]{1,0:T(8,128)(2,1)S(1)} %collective-permute-done.3.refs_13_.refs_2_), channel_id=1, source_target_pairs={{0,4},{4,0},{8,12},{12,8},{1,5},{5,1},{9,13},{13,9},{2,6},{6,2},{1... | collective-permute-start | bytes 350216 | tf_op jit(solution)/shard_map/ppermute | solution.py:25
  20.5 2.6 %collective-permute-start.9 = (bf16[8,7296]{1,0:T(8,128)(2,1)S(1)}, bf16[8,7296]{1,0:T(8,128)(2,1)S(1)}, u32[]{:S(2)}, u32[]{:S(2)}) collective-permute-start(bf16[8,7296]{1,0:T(8,128)(2,1)S(1)} %hold.2.refs_7_), channel_id=1, source_target_pairs={{0,4},{4,0},{8,12},{12,8},{1,5},{5,1},{9,13},{13,9},{2,6},{6,2},{1... | collective-permute-start | bytes 350216 | tf_op jit(solution)/shard_map/ppermute | solution.py:25
  22.1 1.3 %collective-permute-start.14 = (bf16[8,7296]{1,0:T(8,128)(2,1)S(1)}, bf16[8,7296]{1,0:T(8,128)(2,1)S(1)}, u32[]{:S(2)}, u32[]{:S(2)}) collective-permute-start(bf16[8,7296]{1,0:T(8,128)(2,1)S(1)} %copy-done), channel_id=1, source_target_pairs={{0,4},{4,0},{8,12},{12,8},{1,5},{5,1},{9,13},{13,9},{2,6},{6,2},{1... | collective-permute-start | bytes 350216 | tf_op jit(solution)/shard_map/ppermute | solution.py:25
  22.1 1.5 %collective-permute-start.5 = (bf16[8,7296]{1,0:T(8,128)(2,1)S(1)}, bf16[8,7296]{1,0:T(8,128)(2,1)S(1)}, u32[]{:S(2)}, u32[]{:S(2)}) collective-permute-start(bf16[8,7296]{1,0:T(8,128)(2,1)S(1)} %collective-permute-done.4.refs_5_), channel_id=1, source_target_pairs={{0,4},{4,0},{8,12},{12,8},{1,5},{5,1},{9,13},{13,9},{2,6},{6,2},{1... | collective-permute-start | bytes 350216 | tf_op jit(solution)/shard_map/ppermute | solution.py:25
  22.6 1.5 %collective-permute-start.2 = (bf16[8,7296]{1,0:T(8,128)(2,1)S(1)}, bf16[8,7296]{1,0:T(8,128)(2,1)S(1)}, u32[]{:S(2)}, u32[]{:S(2)}) collective-permute-start(bf16[8,7296]{1,0:T(8,128)(2,1)S(1)} %collective-permute-done.1.refs_4_), channel_id=1, source_target_pairs={{0,4},{4,0},{8,12},{12,8},{1,5},{5,1},{9,13},{13,9},{2,6},{6,2},{1... | collective-permute-start | bytes 350216 | tf_op jit(solution)/shard_map/ppermute | solution.py:25
  22.7 1.4 %collective-permute-start.11 = (bf16[8,7296]{1,0:T(8,128)(2,1)S(1)}, bf16[8,7296]{1,0:T(8,128)(2,1)S(1)}, u32[]{:S(2)}, u32[]{:S(2)}) collective-permute-start(bf16[8,7296]{1,0:T(8,128)(2,1)S(1)} %collective-permute-done.10.refs_12_.refs_3_), channel_id=1, source_target_pairs={{0,4},{4,0},{8,12},{12,8},{1,5},{5,1},{9,13},{13,9},{2,6},{6,2},{1... | collective-permute-start | bytes 350216 | tf_op jit(solution)/shard_map/ppermute | solution.py:25
  23.1 1.3 %collective-permute-start.8 = (bf16[8,7296]{1,0:T(8,128)(2,1)S(1)}, bf16[8,7296]{1,0:T(8,128)(2,1)S(1)}, u32[]{:S(2)}, u32[]{:S(2)}) collective-permute-start(bf16[8,7296]{1,0:T(8,128)(2,1)S(1)} %collective-permute-done.7.refs_6_), channel_id=1, source_target_pairs={{0,4},{4,0},{8,12},{12,8},{1,5},{5,1},{9,13},{13,9},{2,6},{6,2},{1... | collective-permute-start | bytes 350216 | tf_op jit(solution)/shard_map/ppermute | solution.py:25
  27.0 6.9 %collective-permute-start.15 = (bf16[64,512]{1,0:T(8,128)(2,1)S(1)}, bf16[64,512]{1,0:T(8,128)(2,1)S(1)}, u32[]{:S(2)}, u32[]{:S(2)}) collective-permute-start(bf16[64,512]{1,0:T(8,128)(2,1)S(1)} %gate_up.1.refs_0_), channel_id=1, source_target_pairs={{0,3},{1,2},{2,1},{3,0},{4,7},{5,6},{6,5},{7,4},{8,11},{9,10},{10,... | collective-permute-start | bytes 196616 | tf_op jit(solution)/shard_map/ppermute | solution.py:25
  31.0 5.3 %collective-permute-start.16 = (bf16[64,512]{1,0:T(8,128)(2,1)S(1)}, bf16[64,512]{1,0:T(8,128)(2,1)S(1)}, u32[]{:S(2)}, u32[]{:S(2)}) collective-permute-start(bf16[64,512]{1,0:T(8,128)(2,1)S(1)} %gate_up.1.refs_0_), channel_id=1, source_target_pairs={{0,2},{1,3},{2,0},{3,1},{4,6},{5,7},{6,4},{7,5},{8,10},{9,11},{10,... | collective-permute-start | bytes 196616 | tf_op jit(solution)/shard_map/ppermute | solution.py:25
  31.0 5.7 %collective-permute-start.17 = (bf16[64,512]{1,0:T(8,128)(2,1)S(1)}, bf16[64,512]{1,0:T(8,128)(2,1)S(1)}, u32[]{:S(2)}, u32[]{:S(2)}) collective-permute-start(bf16[64,512]{1,0:T(8,128)(2,1)S(1)} %gate_up.1.refs_0_), channel_id=1, source_target_pairs={{0,1},{1,0},{2,3},{3,2},{4,5},{5,4},{6,7},{7,6},{8,9},{9,8},{10,11... | collective-permute-start | bytes 196616 | tf_op jit(solution)/shard_map/ppermute | solution.py:25
  37.8 1.9 %collective-permute-start.18 = (bf16[16,1792]{1,0:T(8,128)(2,1)S(1)}, bf16[16,1792]{1,0:T(8,128)(2,1)S(1)}, u32[]{:S(2)}, u32[]{:S(2)}) collective-permute-start(bf16[16,1792]{1,0:T(8,128)(2,1)S(1)} %get-tuple-element.36), channel_id=1, source_target_pairs={{0,4},{4,0},{8,12},{12,8},{1,5},{5,1},{9,13},{13,9},{2,6},{6,2},{1... | collective-permute-start | bytes 172040 | tf_op jit(solution)/shard_map/ppermute | solution.py:25
  37.8 4.8 %collective-permute-start.19 = (bf16[16,1792]{1,0:T(8,128)(2,1)S(1)}, bf16[16,1792]{1,0:T(8,128)(2,1)S(1)}, u32[]{:S(2)}, u32[]{:S(2)}) collective-permute-start(bf16[16,1792]{1,0:T(8,128)(2,1)S(1)} %get-tuple-element.37), channel_id=1, source_target_pairs={{0,8},{4,12},{8,0},{12,4},{1,9},{5,13},{9,1},{13,5},{2,10},{6,14},... | collective-permute-start | bytes 172040 | tf_op jit(solution)/shard_map/ppermute | solution.py:25
  38.0 5.0 %collective-permute-start.20 = (bf16[16,1792]{1,0:T(8,128)(2,1)S(1)}, bf16[16,1792]{1,0:T(8,128)(2,1)S(1)}, u32[]{:S(2)}, u32[]{:S(2)}) collective-permute-start(bf16[16,1792]{1,0:T(8,128)(2,1)S(1)} %get-tuple-element.38), channel_id=1, source_target_pairs={{0,12},{4,8},{8,4},{12,0},{1,13},{5,9},{9,5},{13,1},{2,14},{6,10},... | collective-permute-start | bytes 172040 | tf_op jit(solution)/shard_map/ppermute | solution.py:25
  43.2 5.8 %collective-permute-start.21 = (bf16[8,1792]{1,0:T(8,128)(2,1)S(1)}, bf16[8,1792]{1,0:T(8,128)(2,1)S(1)}, u32[]{:S(2)}, u32[]{:S(2)}) collective-permute-start(bf16[8,1792]{1,0:T(8,128)(2,1)S(1)} %get-tuple-element.39), channel_id=1, source_target_pairs={{0,3},{1,2},{2,1},{3,0},{4,7},{5,6},{6,5},{7,4},{8,11},{9,10},{10,... | collective-permute-start | bytes 86024 | tf_op jit(solution)/shard_map/ppermute | solution.py:25
  45.6 4.8 %collective-permute-start.22 = (bf16[8,1792]{1,0:T(8,128)(2,1)S(1)}, bf16[8,1792]{1,0:T(8,128)(2,1)S(1)}, u32[]{:S(2)}, u32[]{:S(2)}) collective-permute-start(bf16[8,1792]{1,0:T(8,128)(2,1)S(1)} %get-tuple-element.40), channel_id=1, source_target_pairs={{0,2},{1,3},{2,0},{3,1},{4,6},{5,7},{6,4},{7,5},{8,10},{9,11},{10,... | collective-permute-start | bytes 86024 | tf_op jit(solution)/shard_map/ppermute | solution.py:25
  46.1 4.3 %collective-permute-start.23 = (bf16[8,1792]{1,0:T(8,128)(2,1)S(1)}, bf16[8,1792]{1,0:T(8,128)(2,1)S(1)}, u32[]{:S(2)}, u32[]{:S(2)}) collective-permute-start(bf16[8,1792]{1,0:T(8,128)(2,1)S(1)} %get-tuple-element.41), channel_id=1, source_target_pairs={{0,1},{1,0},{2,3},{3,2},{4,5},{5,4},{6,7},{7,6},{8,9},{9,8},{10,11... | collective-permute-start | bytes 86024 | tf_op jit(solution)/shard_map/ppermute | solution.py:25

commit v4 on v3

--- a/solution.py
+++ b/solution.py
@@ -263,12 +263,12 @@
     for kz in single:
         for ky in far:
             got[kz, ky] = swap(got[kz, 0], "ep", experts, ky)
-    TIE = {(0, 0): (2, 2), (1, 0): (2, 2), (2, 0): (3, 2), (0, 2): (3, 2)}
+    later = {(0, 0): (1, 2), (1, 0): (1, 2), (2, 0): (1, 2), (0, 2): (1, 2)}
     for kz in range(groups):
         for ky in range(0, experts, 2):
             block = got[kz, ky]
-            if (kz, ky) in TIE:
-                block = lax.optimization_barrier((block, got[TIE[kz, ky]]))[0]
+            if (kz, ky) in later:
+                block = lax.optimization_barrier((block, got[later[kz, ky]]))[0]
             got[kz, ky + 1] = swap(block, "ep", experts, 1)
     arrays = [got[kz, ke] for ke in range(experts) for kz in range(groups)][::-1]
 

time: 51.2 us -> 48.8 us (0.953)
  waiting for transfers between devices: 18.7 us -> 15.7 us
  starting transfers between devices: 25 us -> 25.6 us
    ppermute x24, waiting for transfers between devices: 18.7 us -> 15.7 us  [swap(): return lax.ppermute(x, axis, [(i, i ^ k) for i in range(size)])]
    ppermute x24, starting transfers between devices: 25 us -> 25.6 us  [swap(): return lax.ppermute(x, axis, [(i, i ^ k) for i in range(size)])]
  transfers between devices with their start and end apart: 24 -> 24, of which waited for: 14 -> 15; matrix products, arithmetic and copies ran while one was open for 0% -> 0% of each run, Pallas kernels for 2% -> 2%
where the time goes in v4:
time: 48.8 us; the launch traced here: 48.7 us
  starting transfers between devices  25.6 us (52%)
  waiting for transfers between devices  15.7 us (32%)
  Pallas kernels  7.18 us (15%)
    ppermute x24, starting transfers between devices, swap(): return lax.ppermute(x, axis, [(i, i ^ k) for i in range(size)])  25.6 us
    ppermute x24, waiting for transfers between devices, swap(): return lax.ppermute(x, axis, [(i, i ^ k) for i in range(size)])  15.7 us
    pallas_call x1, Pallas kernels, body(): pl.pallas_call(functools.partial(up_kernel, len(arrays), count, chosen, c...  2.51 us
    pallas_call x1, Pallas kernels, body(): pl.pallas_call(pack_kernel, out_shape=array(count, width + LANES), in_spe...  1.59 us
    pallas_call x2, Pallas kernels, down(): pl.pallas_call(functools.partial(down_kernel, experts, first, n, last), o...  1.53 us
  transfers between devices with their start and end apart: 24, of which 15 were waited for; matrix products, arithmetic and copies ran while one was open for 0% of the time, Pallas kernels for 2%

profile of v4, /device:TPU:0, one launch (start us, length us, event | category | flops | bytes accessed | tf_op | source)
XLA Modules:
  0.0 48.7 jit_solution(16865804722262260005)
XLA Ops:
  0.0 1.6 %pack.1.refs_15_.refs_0_ = bf16[8,7296]{1,0:T(8,128)(2,1)} custom-call(bf16[8,7168]{1,0:T(8,128)(2,1)} %tokens.1, s32[2,8]{1,0:T(2,128)} %bitcast.8, f32[2,8]{1,0:T(2,128)} %bitcast.9), custom_call_target="tpu_custom_call" | custom-call | tf_op jit(solution)/shard_map/pack/pallas_call | solution.py:222
  1.6 3.1 %collective-permute-start.6 = (bf16[8,7296]{1,0:T(8,128)(2,1)}, bf16[8,7296]{1,0:T(8,128)(2,1)S(1)}, u32[]{:S(2)}, u32[]{:S(2)}) collective-permute-start(bf16[8,7296]{1,0:T(8,128)(2,1)} %pack.1.refs_15_.refs_0_), channel_id=1, source_target_pairs={{0,1},{1,0},{2,3},{3,2},{4,5},{5,4},{6,7},{7,6},{8,9},{9,8},{10,11... | collective-permute-start | bytes 350216 | tf_op jit(solution)/shard_map/ppermute | solution.py:25
  4.7 2.6 %collective-permute-start.3 = (bf16[8,7296]{1,0:T(8,128)(2,1)}, bf16[8,7296]{1,0:T(8,128)(2,1)S(1)}, u32[]{:S(2)}, u32[]{:S(2)}) collective-permute-start(bf16[8,7296]{1,0:T(8,128)(2,1)} %pack.1.refs_15_.refs_0_), channel_id=1, source_target_pairs={{0,2},{1,3},{2,0},{3,1},{4,6},{5,7},{6,4},{7,5},{8,10},{9,11},{10,... | collective-permute-start | bytes 350216 | tf_op jit(solution)/shard_map/ppermute | solution.py:25
  7.3 1.5 %collective-permute-start = (bf16[8,7296]{1,0:T(8,128)(2,1)}, bf16[8,7296]{1,0:T(8,128)(2,1)S(1)}, u32[]{:S(2)}, u32[]{:S(2)}) collective-permute-start(bf16[8,7296]{1,0:T(8,128)(2,1)} %pack.1.refs_15_.refs_0_), channel_id=1, source_target_pairs={{0,8},{4,12},{8,0},{12,4},{1,9},{5,13},{9,1},{13,5},{2,10},{6,14},... | collective-permute-start | bytes 350216 | tf_op jit(solution)/shard_map/ppermute | solution.py:25
  8.8 0.5 collective-permute-done.6.x
  9.3 0.0 copy-start
  9.3 0.0 slice-start.3
  9.3 0.0 slice-start.5
  9.3 1.9 %collective-permute-start.7 = (bf16[8,7296]{1,0:T(8,128)(2,1)S(1)}, bf16[8,7296]{1,0:T(8,128)(2,1)S(1)}, u32[]{:S(2)}, u32[]{:S(2)}) collective-permute-start(bf16[8,7296]{1,0:T(8,128)(2,1)S(1)} %hold.3.refs_14_.refs_1_), channel_id=1, source_target_pairs={{0,8},{4,12},{8,0},{12,4},{1,9},{5,13},{9,1},{13,5},{2,10},{6,14},... | collective-permute-start | bytes 350216 | tf_op jit(solution)/shard_map/ppermute | solution.py:25
  11.3 1.8 %collective-permute-done.3.refs_13_.refs_2_ = bf16[8,7296]{1,0:T(8,128)(2,1)S(1)} collective-permute-done((bf16[8,7296]{1,0:T(8,128)(2,1)}, bf16[8,7296]{1,0:T(8,128)(2,1)S(1)}, u32[]{:S(2)}, u32[]{:S(2)}) %collective-permute-start.3) | collective-permute-done | bytes 116768 | tf_op jit(solution)/shard_map/ppermute | solution.py:25
  13.0 0.4 collective-permute-start.10
  13.4 0.0 collective-permute-done.x
  13.5 0.0 slice-start.1
  13.5 2.1 %collective-permute-start.1 = (bf16[8,7296]{1,0:T(8,128)(2,1)S(1)}, bf16[8,7296]{1,0:T(8,128)(2,1)S(1)}, u32[]{:S(2)}, u32[]{:S(2)}) collective-permute-start(bf16[8,7296]{1,0:T(8,128)(2,1)S(1)} %hold.2.refs_7_), channel_id=1, source_target_pairs={{0,3},{1,2},{2,1},{3,0},{4,7},{5,6},{6,5},{7,4},{8,11},{9,10},{10,... | collective-permute-start | bytes 350216 | tf_op jit(solution)/shard_map/ppermute | solution.py:25
  15.6 1.6 %collective-permute-start.4 = (bf16[8,7296]{1,0:T(8,128)(2,1)S(1)}, bf16[8,7296]{1,0:T(8,128)(2,1)S(1)}, u32[]{:S(2)}, u32[]{:S(2)}) collective-permute-start(bf16[8,7296]{1,0:T(8,128)(2,1)S(1)} %collective-permute-done.3.refs_13_.refs_2_), channel_id=1, source_target_pairs={{0,8},{4,12},{8,0},{12,4},{1,9},{5,13},{9,1},{13,5},{2,10},{6,14},... | collective-permute-start | bytes 350216 | tf_op jit(solution)/shard_map/ppermute | solution.py:25
  17.1 0.0 collective-permute-done.7.refs_6_
  17.1 0.0 collective-permute-start.12
  17.1 0.5 %collective-permute-start.13 = (bf16[8,7296]{1,0:T(8,128)(2,1)S(1)}, bf16[8,7296]{1,0:T(8,128)(2,1)S(1)}, u32[]{:S(2)}, u32[]{:S(2)}) collective-permute-start(bf16[8,7296]{1,0:T(8,128)(2,1)S(1)} %hold.3.refs_14_.refs_1_), channel_id=1, source_target_pairs={{0,4},{4,0},{8,12},{12,8},{1,5},{5,1},{9,13},{13,9},{2,6},{6,2},{1... | collective-permute-start | bytes 350216 | tf_op jit(solution)/shard_map/ppermute | solution.py:25
  17.7 1.4 %collective-permute-done.10.refs_12_.refs_3_ = bf16[8,7296]{1,0:T(8,128)(2,1)S(1)} collective-permute-done((bf16[8,7296]{1,0:T(8,128)(2,1)S(1)}, bf16[8,7296]{1,0:T(8,128)(2,1)S(1)}, u32[]{:S(2)}, u32[]{:S(2)}) %collective-permute-start.10) | collective-permute-done | bytes 116768 | tf_op jit(solution)/shard_map/ppermute | solution.py:25
  19.0 0.0 collective-permute-start.9
  19.0 1.4 %collective-permute-done.4.refs_5_ = bf16[8,7296]{1,0:T(8,128)(2,1)S(1)} collective-permute-done((bf16[8,7296]{1,0:T(8,128)(2,1)S(1)}, bf16[8,7296]{1,0:T(8,128)(2,1)S(1)}, u32[]{:S(2)}, u32[]{:S(2)}) %collective-permute-start.4) | collective-permute-done | bytes 116768 | tf_op jit(solution)/shard_map/ppermute | solution.py:25
  20.4 0.0 copy-done
  20.4 0.0 collective-permute-start.14
  20.4 0.0 collective-permute-done.1.refs_4_
  20.4 0.5 %collective-permute-start.8 = (bf16[8,7296]{1,0:T(8,128)(2,1)S(1)}, bf16[8,7296]{1,0:T(8,128)(2,1)S(1)}, u32[]{:S(2)}, u32[]{:S(2)}) collective-permute-start(bf16[8,7296]{1,0:T(8,128)(2,1)S(1)} %collective-permute-done.7.refs_6_), channel_id=1, source_target_pairs={{0,4},{4,0},{8,12},{12,8},{1,5},{5,1},{9,13},{13,9},{2,6},{6,2},{1... | collective-permute-start | bytes 350216 | tf_op jit(solution)/shard_map/ppermute | solution.py:25
  20.9 0.0 collective-permute-done.12.refs_9_
  20.9 0.1 collective-permute-start.11
  21.0 0.0 collective-permute-done.13.refs_10_
  21.0 0.4 collective-permute-start.5
  21.4 0.0 collective-permute-done.9.refs_3_
  21.4 0.1 collective-permute-start.2
  21.5 0.2 collective-permute-done.14.refs_11_
  21.7 0.2 collective-permute-done.8.refs_2_
  21.9 0.4 collective-permute-done.11.refs_8_
  22.2 0.2 collective-permute-done.5.refs_1_
  22.4 0.4 collective-permute-done.2.refs_0_
  22.8 0.0 slice-done.2
  22.8 0.0 slice-done.4
  22.8 0.0 slice-done.3
  22.8 0.0 slice-done.5
  22.8 2.5 %gate_up.1.refs_0_ = bf16[64,512]{1,0:T(8,128)(2,1)S(1)} custom-call(bf16[8,7296]{1,0:T(8,128)(2,1)S(1)} %collective-permute-done.2.refs_0_, bf16[8,7296]{1,0:T(8,128)(2,1)S(1)} %collective-permute-done.5.refs_1_, bf16[8,7296]{1,0:T(8,128)(2,1)S(1)} %collective-permute-done.8.refs_2_, bf16[8,7296]{1,0:T(8,128)(2,1)S(1)} %collective-permute-done.9.refs_3_, ...), custom_call_target="tpu_custom_call" | custom-call | tf_op jit(solution)/shard_map/gate_up/pallas_call | solution.py:276
  25.3 1.8 %collective-permute-start.15 = (bf16[64,512]{1,0:T(8,128)(2,1)S(1)}, bf16[64,512]{1,0:T(8,128)(2,1)S(1)}, u32[]{:S(2)}, u32[]{:S(2)}) collective-permute-start(bf16[64,512]{1,0:T(8,128)(2,1)S(1)} %gate_up.1.refs_0_), channel_id=1, source_target_pairs={{0,3},{1,2},{2,1},{3,0},{4,7},{5,6},{6,5},{7,4},{8,11},{9,10},{10,... | collective-permute-start | bytes 196616 | tf_op jit(solution)/shard_map/ppermute | solution.py:25
  27.2 0.8 %collective-permute-start.16 = (bf16[64,512]{1,0:T(8,128)(2,1)S(1)}, bf16[64,512]{1,0:T(8,128)(2,1)S(1)}, u32[]{:S(2)}, u32[]{:S(2)}) collective-permute-start(bf16[64,512]{1,0:T(8,128)(2,1)S(1)} %gate_up.1.refs_0_), channel_id=1, source_target_pairs={{0,2},{1,3},{2,0},{3,1},{4,6},{5,7},{6,4},{7,5},{8,10},{9,11},{10,... | collective-permute-start | bytes 196616 | tf_op jit(solution)/shard_map/ppermute | solution.py:25
  28.0 1.8 %collective-permute-start.17 = (bf16[64,512]{1,0:T(8,128)(2,1)S(1)}, bf16[64,512]{1,0:T(8,128)(2,1)S(1)}, u32[]{:S(2)}, u32[]{:S(2)}) collective-permute-start(bf16[64,512]{1,0:T(8,128)(2,1)S(1)} %gate_up.1.refs_0_), channel_id=1, source_target_pairs={{0,1},{1,0},{2,3},{3,2},{4,5},{5,4},{6,7},{7,6},{8,9},{9,8},{10,11... | collective-permute-start | bytes 196616 | tf_op jit(solution)/shard_map/ppermute | solution.py:25
  29.8 0.6 %shares.1 = (bf16[32,64]{1,0:T(8,128)(2,1)S(1)}, bf16[32,64]{1,0:T(8,128)(2,1)S(1)}, bf16[32,64]{1,0:T(8,128)(2,1)S(1)}) custom-call(bf16[8,7296]{1,0:T(8,128)(2,1)S(1)} %copy-done, bf16[8,7296]{1,0:T(8,128)(2,1)S(1)} %hold.3.refs_14_.refs_1_, bf16[8,7296]{1,0:T(8,128)(2,1)S(1)} %collective-permute-done.3.refs_13_.refs_2_, ...), custom_call_target="tpu_custom_call" | custom-call | tf_op jit(solution)/shard_map/shares/pallas_call | solution.py:290
  30.4 0.5 down_0.1.refs_4_
  30.9 1.3 %collective-permute-done.15.refs_0_ = bf16[64,512]{1,0:T(8,128)(2,1)S(1)} collective-permute-done((bf16[64,512]{1,0:T(8,128)(2,1)S(1)}, bf16[64,512]{1,0:T(8,128)(2,1)S(1)}, u32[]{:S(2)}, u32[]{:S(2)}) %collective-permute-start.15) | collective-permute-done | bytes 65568 | tf_op jit(solution)/shard_map/ppermute | solution.py:25
  32.2 2.2 %collective-permute-done.16.refs_1_ = bf16[64,512]{1,0:T(8,128)(2,1)S(1)} collective-permute-done((bf16[64,512]{1,0:T(8,128)(2,1)S(1)}, bf16[64,512]{1,0:T(8,128)(2,1)S(1)}, u32[]{:S(2)}, u32[]{:S(2)}) %collective-permute-start.16) | collective-permute-done | bytes 65568 | tf_op jit(solution)/shard_map/ppermute | solution.py:25
  34.4 0.0 collective-permute-done.17.refs_2_
  34.4 1.1 %down_1.1 = (bf16[16,1792]{1,0:T(8,128)(2,1)S(1)}, bf16[16,1792]{1,0:T(8,128)(2,1)S(1)}, bf16[16,1792]{1,0:T(8,128)(2,1)S(1)}, bf16[16,1792]{1,0:T(8,128)(2,1)S(1)}) custom-call(bf16[64,512]{1,0:T(8,128)(2,1)S(1)} %collective-permute-done.15.refs_0_, bf16[64,512]{1,0:T(8,128)(2,1)S(1)} %collective-permute-done.16.refs_1_, ...), custom_call_target="tpu_custom_call" | custom-call | tf_op jit(solution)/shard_map/down_1/pallas_call | solution.py:305
  35.5 0.1 collective-permute-start.18
  35.6 1.6 %collective-permute-start.19 = (bf16[16,1792]{1,0:T(8,128)(2,1)S(1)}, bf16[16,1792]{1,0:T(8,128)(2,1)S(1)}, u32[]{:S(2)}, u32[]{:S(2)}) collective-permute-start(bf16[16,1792]{1,0:T(8,128)(2,1)S(1)} %get-tuple-element.37), channel_id=1, source_target_pairs={{0,8},{4,12},{8,0},{12,4},{1,9},{5,13},{9,1},{13,5},{2,10},{6,14},... | collective-permute-start | bytes 172040 | tf_op jit(solution)/shard_map/ppermute | solution.py:25
  37.2 0.2 collective-permute-start.20
  37.4 0.0 collective-permute-done.18.refs_4_
  37.4 2.5 %collective-permute-done.19.refs_5_ = bf16[16,1792]{1,0:T(8,128)(2,1)S(1)} collective-permute-done((bf16[16,1792]{1,0:T(8,128)(2,1)S(1)}, bf16[16,1792]{1,0:T(8,128)(2,1)S(1)}, u32[]{:S(2)}, u32[]{:S(2)}) %collective-permute-start.19) | collective-permute-done | bytes 57376 | tf_op jit(solution)/shard_map/ppermute | solution.py:25
  39.9 1.2 %collective-permute-done.20.refs_6_ = bf16[16,1792]{1,0:T(8,128)(2,1)S(1)} collective-permute-done((bf16[16,1792]{1,0:T(8,128)(2,1)S(1)}, bf16[16,1792]{1,0:T(8,128)(2,1)S(1)}, u32[]{:S(2)}, u32[]{:S(2)}) %collective-permute-start.20) | collective-permute-done | bytes 57376 | tf_op jit(solution)/shard_map/ppermute | solution.py:25
  41.1 0.2 combine.1
  41.3 1.9 %collective-permute-start.21 = (bf16[8,1792]{1,0:T(8,128)(2,1)S(1)}, bf16[8,1792]{1,0:T(8,128)(2,1)S(1)}, u32[]{:S(2)}, u32[]{:S(2)}) collective-permute-start(bf16[8,1792]{1,0:T(8,128)(2,1)S(1)} %get-tuple-element.39), channel_id=1, source_target_pairs={{0,3},{1,2},{2,1},{3,0},{4,7},{5,6},{6,5},{7,4},{8,11},{9,10},{10,... | collective-permute-start | bytes 86024 | tf_op jit(solution)/shard_map/ppermute | solution.py:25
  43.2 0.0 collective-permute-start.22
  43.2 2.5 %collective-permute-start.23 = (bf16[8,1792]{1,0:T(8,128)(2,1)S(1)}, bf16[8,1792]{1,0:T(8,128)(2,1)S(1)}, u32[]{:S(2)}, u32[]{:S(2)}) collective-permute-start(bf16[8,1792]{1,0:T(8,128)(2,1)S(1)} %get-tuple-element.41), channel_id=1, source_target_pairs={{0,1},{1,0},{2,3},{3,2},{4,5},{5,4},{6,7},{7,6},{8,9},{9,8},{10,11... | collective-permute-start | bytes 86024 | tf_op jit(solution)/shard_map/ppermute | solution.py:25
  45.8 1.4 %collective-permute-done.21.refs_0_ = bf16[8,1792]{1,0:T(8,128)(2,1)S(1)} collective-permute-done((bf16[8,1792]{1,0:T(8,128)(2,1)S(1)}, bf16[8,1792]{1,0:T(8,128)(2,1)S(1)}, u32[]{:S(2)}, u32[]{:S(2)}) %collective-permute-start.21) | collective-permute-done | bytes 28704 | tf_op jit(solution)/shard_map/ppermute | solution.py:25
  47.1 0.9 %collective-permute-done.22.refs_1_ = bf16[8,1792]{1,0:T(8,128)(2,1)S(1)} collective-permute-done((bf16[8,1792]{1,0:T(8,128)(2,1)S(1)}, bf16[8,1792]{1,0:T(8,128)(2,1)S(1)}, u32[]{:S(2)}, u32[]{:S(2)}) %collective-permute-start.22) | collective-permute-done | bytes 28704 | tf_op jit(solution)/shard_map/ppermute | solution.py:25
  48.0 0.0 collective-permute-done.23.refs_2_
  48.0 0.7 %place.1 = bf16[8,7168]{1,0:T(8,128)(2,1)} custom-call(bf16[8,1792]{1,0:T(8,128)(2,1)S(1)} %collective-permute-done.21.refs_0_, bf16[8,1792]{1,0:T(8,128)(2,1)S(1)} %collective-permute-done.22.refs_1_, bf16[8,1792]{1,0:T(8,128)(2,1)S(1)} %collective-permute-done.23.refs_2_, bf16[8,1792]{1,0:T(8,128)(2,1)S(1)} %get-tuple-element.42.refs_3_), custom_call_target="tpu_custom_call" | custom-call | tf_op jit(solution)/shard_map/place/pallas_call | solution.py:330
  (10 shorter events, 0.0 us)
Async XLA Ops:
  1.6 7.7 %collective-permute-start.6 = (bf16[8,7296]{1,0:T(8,128)(2,1)}, bf16[8,7296]{1,0:T(8,128)(2,1)S(1)}, u32[]{:S(2)}, u32[]{:S(2)}) collective-permute-start(bf16[8,7296]{1,0:T(8,128)(2,1)} %pack.1.refs_15_.refs_0_), channel_id=1, source_target_pairs={{0,1},{1,0},{2,3},{3,2},{4,5},{5,4},{6,7},{7,6},{8,9},{9,8},{10,11... | collective-permute-start | bytes 350216 | tf_op jit(solution)/shard_map/ppermute | solution.py:25
  4.7 8.3 %collective-permute-start.3 = (bf16[8,7296]{1,0:T(8,128)(2,1)}, bf16[8,7296]{1,0:T(8,128)(2,1)S(1)}, u32[]{:S(2)}, u32[]{:S(2)}) collective-permute-start(bf16[8,7296]{1,0:T(8,128)(2,1)} %pack.1.refs_15_.refs_0_), channel_id=1, source_target_pairs={{0,2},{1,3},{2,0},{3,1},{4,6},{5,7},{6,4},{7,5},{8,10},{9,11},{10,... | collective-permute-start | bytes 350216 | tf_op jit(solution)/shard_map/ppermute | solution.py:25
  7.3 6.2 %collective-permute-start = (bf16[8,7296]{1,0:T(8,128)(2,1)}, bf16[8,7296]{1,0:T(8,128)(2,1)S(1)}, u32[]{:S(2)}, u32[]{:S(2)}) collective-permute-start(bf16[8,7296]{1,0:T(8,128)(2,1)} %pack.1.refs_15_.refs_0_), channel_id=1, source_target_pairs={{0,8},{4,12},{8,0},{12,4},{1,9},{5,13},{9,1},{13,5},{2,10},{6,14},... | collective-permute-start | bytes 350216 | tf_op jit(solution)/shard_map/ppermute | solution.py:25
  9.3 13.5 %slice-start.2 = ((s8[7340032]{0:T(1024)(128)(4,1)}), s8[4194304]{0:T(1024)(128)(4,1)S(1)}, s32[]{:S(2)}) async-start(s8[7340032]{0:T(1024)(128)(4,1)} %bitcast.4), calls=%async_computation.2 | async-start | bytes 8388608
  9.3 13.5 %slice-start.4 = ((s8[7340032]{0:T(1024)(128)(4,1)}), s8[4194304]{0:T(1024)(128)(4,1)S(1)}, s32[]{:S(2)}) async-start(s8[7340032]{0:T(1024)(128)(4,1)} %bitcast.6), calls=%async_computation.4 | async-start | bytes 8388608
  9.3 11.1 %copy-start = (bf16[8,7296]{1,0:T(8,128)(2,1)S(1)}, bf16[8,7296]{1,0:T(8,128)(2,1)}, u32[]{:S(2)}) copy-start(bf16[8,7296]{1,0:T(8,128)(2,1)} %pack.1.refs_15_.refs_0_) | copy-start | bytes 350212
  9.3 13.5 %slice-start.3 = ((s8[7340032]{0:T(1024)(128)(4,1)}), s8[3145728]{0:T(1024)(128)(4,1)S(1)}, s32[]{:S(2)}) async-start(s8[7340032]{0:T(1024)(128)(4,1)} %bitcast.4), calls=%async_computation.3 | async-start | bytes 6291456
  9.3 13.4 %slice-start.5 = ((s8[7340032]{0:T(1024)(128)(4,1)}), s8[3145728]{0:T(1024)(128)(4,1)S(1)}, s32[]{:S(2)}) async-start(s8[7340032]{0:T(1024)(128)(4,1)} %bitcast.6), calls=%async_computation.5 | async-start | bytes 6291456
  9.3 7.8 %collective-permute-start.7 = (bf16[8,7296]{1,0:T(8,128)(2,1)S(1)}, bf16[8,7296]{1,0:T(8,128)(2,1)S(1)}, u32[]{:S(2)}, u32[]{:S(2)}) collective-permute-start(bf16[8,7296]{1,0:T(8,128)(2,1)S(1)} %hold.3.refs_14_.refs_1_), channel_id=1, source_target_pairs={{0,8},{4,12},{8,0},{12,4},{1,9},{5,13},{9,1},{13,5},{2,10},{6,14},... | collective-permute-start | bytes 350216 | tf_op jit(solution)/shard_map/ppermute | solution.py:25
  13.0 6.0 %collective-permute-start.10 = (bf16[8,7296]{1,0:T(8,128)(2,1)S(1)}, bf16[8,7296]{1,0:T(8,128)(2,1)S(1)}, u32[]{:S(2)}, u32[]{:S(2)}) collective-permute-start(bf16[8,7296]{1,0:T(8,128)(2,1)S(1)} %collective-permute-done.3.refs_13_.refs_2_), channel_id=1, source_target_pairs={{0,1},{1,0},{2,3},{3,2},{4,5},{5,4},{6,7},{7,6},{8,9},{9,8},{10,11... | collective-permute-start | bytes 350216 | tf_op jit(solution)/shard_map/ppermute | solution.py:25
  13.4 17.0 %slice-start = ((s8[7340032]{0:T(1024)(128)(4,1)}), s8[4194304]{0:T(1024)(128)(4,1)S(1)}, s32[]{:S(2)}) async-start(s8[7340032]{0:T(1024)(128)(4,1)} %bitcast.2), calls=%async_computation | async-start | bytes 8388608
  13.5 17.0 %slice-start.1 = ((s8[7340032]{0:T(1024)(128)(4,1)}), s8[3145728]{0:T(1024)(128)(4,1)S(1)}, s32[]{:S(2)}) async-start(s8[7340032]{0:T(1024)(128)(4,1)} %bitcast.2), calls=%async_computation.1 | async-start | bytes 6291456
  13.5 6.9 %collective-permute-start.1 = (bf16[8,7296]{1,0:T(8,128)(2,1)S(1)}, bf16[8,7296]{1,0:T(8,128)(2,1)S(1)}, u32[]{:S(2)}, u32[]{:S(2)}) collective-permute-start(bf16[8,7296]{1,0:T(8,128)(2,1)S(1)} %hold.2.refs_7_), channel_id=1, source_target_pairs={{0,3},{1,2},{2,1},{3,0},{4,7},{5,6},{6,5},{7,4},{8,11},{9,10},{10,... | collective-permute-start | bytes 350216 | tf_op jit(solution)/shard_map/ppermute | solution.py:25
  15.6 4.8 %collective-permute-start.4 = (bf16[8,7296]{1,0:T(8,128)(2,1)S(1)}, bf16[8,7296]{1,0:T(8,128)(2,1)S(1)}, u32[]{:S(2)}, u32[]{:S(2)}) collective-permute-start(bf16[8,7296]{1,0:T(8,128)(2,1)S(1)} %collective-permute-done.3.refs_13_.refs_2_), channel_id=1, source_target_pairs={{0,8},{4,12},{8,0},{12,4},{1,9},{5,13},{9,1},{13,5},{2,10},{6,14},... | collective-permute-start | bytes 350216 | tf_op jit(solution)/shard_map/ppermute | solution.py:25
  17.1 3.8 %collective-permute-start.12 = (bf16[8,7296]{1,0:T(8,128)(2,1)S(1)}, bf16[8,7296]{1,0:T(8,128)(2,1)S(1)}, u32[]{:S(2)}, u32[]{:S(2)}) collective-permute-start(bf16[8,7296]{1,0:T(8,128)(2,1)S(1)} %collective-permute-done.3.refs_13_.refs_2_), channel_id=1, source_target_pairs={{0,4},{4,0},{8,12},{12,8},{1,5},{5,1},{9,13},{13,9},{2,6},{6,2},{1... | collective-permute-start | bytes 350216 | tf_op jit(solution)/shard_map/ppermute | solution.py:25
  17.1 3.8 %collective-permute-start.13 = (bf16[8,7296]{1,0:T(8,128)(2,1)S(1)}, bf16[8,7296]{1,0:T(8,128)(2,1)S(1)}, u32[]{:S(2)}, u32[]{:S(2)}) collective-permute-start(bf16[8,7296]{1,0:T(8,128)(2,1)S(1)} %hold.3.refs_14_.refs_1_), channel_id=1, source_target_pairs={{0,4},{4,0},{8,12},{12,8},{1,5},{5,1},{9,13},{13,9},{2,6},{6,2},{1... | collective-permute-start | bytes 350216 | tf_op jit(solution)/shard_map/ppermute | solution.py:25
  19.0 2.4 %collective-permute-start.9 = (bf16[8,7296]{1,0:T(8,128)(2,1)S(1)}, bf16[8,7296]{1,0:T(8,128)(2,1)S(1)}, u32[]{:S(2)}, u32[]{:S(2)}) collective-permute-start(bf16[8,7296]{1,0:T(8,128)(2,1)S(1)} %hold.2.refs_7_), channel_id=1, source_target_pairs={{0,4},{4,0},{8,12},{12,8},{1,5},{5,1},{9,13},{13,9},{2,6},{6,2},{1... | collective-permute-start | bytes 350216 | tf_op jit(solution)/shard_map/ppermute | solution.py:25
  20.4 1.3 %collective-permute-start.14 = (bf16[8,7296]{1,0:T(8,128)(2,1)S(1)}, bf16[8,7296]{1,0:T(8,128)(2,1)S(1)}, u32[]{:S(2)}, u32[]{:S(2)}) collective-permute-start(bf16[8,7296]{1,0:T(8,128)(2,1)S(1)} %copy-done), channel_id=1, source_target_pairs={{0,4},{4,0},{8,12},{12,8},{1,5},{5,1},{9,13},{13,9},{2,6},{6,2},{1... | collective-permute-start | bytes 350216 | tf_op jit(solution)/shard_map/ppermute | solution.py:25
  20.4 1.5 %collective-permute-start.8 = (bf16[8,7296]{1,0:T(8,128)(2,1)S(1)}, bf16[8,7296]{1,0:T(8,128)(2,1)S(1)}, u32[]{:S(2)}, u32[]{:S(2)}) collective-permute-start(bf16[8,7296]{1,0:T(8,128)(2,1)S(1)} %collective-permute-done.7.refs_6_), channel_id=1, source_target_pairs={{0,4},{4,0},{8,12},{12,8},{1,5},{5,1},{9,13},{13,9},{2,6},{6,2},{1... | collective-permute-start | bytes 350216 | tf_op jit(solution)/shard_map/ppermute | solution.py:25
  20.9 1.3 %collective-permute-start.11 = (bf16[8,7296]{1,0:T(8,128)(2,1)S(1)}, bf16[8,7296]{1,0:T(8,128)(2,1)S(1)}, u32[]{:S(2)}, u32[]{:S(2)}) collective-permute-start(bf16[8,7296]{1,0:T(8,128)(2,1)S(1)} %collective-permute-done.10.refs_12_.refs_3_), channel_id=1, source_target_pairs={{0,4},{4,0},{8,12},{12,8},{1,5},{5,1},{9,13},{13,9},{2,6},{6,2},{1... | collective-permute-start | bytes 350216 | tf_op jit(solution)/shard_map/ppermute | solution.py:25
  21.0 1.4 %collective-permute-start.5 = (bf16[8,7296]{1,0:T(8,128)(2,1)S(1)}, bf16[8,7296]{1,0:T(8,128)(2,1)S(1)}, u32[]{:S(2)}, u32[]{:S(2)}) collective-permute-start(bf16[8,7296]{1,0:T(8,128)(2,1)S(1)} %collective-permute-done.4.refs_5_), channel_id=1, source_target_pairs={{0,4},{4,0},{8,12},{12,8},{1,5},{5,1},{9,13},{13,9},{2,6},{6,2},{1... | collective-permute-start | bytes 350216 | tf_op jit(solution)/shard_map/ppermute | solution.py:25
  21.4 1.3 %collective-permute-start.2 = (bf16[8,7296]{1,0:T(8,128)(2,1)S(1)}, bf16[8,7296]{1,0:T(8,128)(2,1)S(1)}, u32[]{:S(2)}, u32[]{:S(2)}) collective-permute-start(bf16[8,7296]{1,0:T(8,128)(2,1)S(1)} %collective-permute-done.1.refs_4_), channel_id=1, source_target_pairs={{0,4},{4,0},{8,12},{12,8},{1,5},{5,1},{9,13},{13,9},{2,6},{6,2},{1... | collective-permute-start | bytes 350216 | tf_op jit(solution)/shard_map/ppermute | solution.py:25
  25.3 6.9 %collective-permute-start.15 = (bf16[64,512]{1,0:T(8,128)(2,1)S(1)}, bf16[64,512]{1,0:T(8,128)(2,1)S(1)}, u32[]{:S(2)}, u32[]{:S(2)}) collective-permute-start(bf16[64,512]{1,0:T(8,128)(2,1)S(1)} %gate_up.1.refs_0_), channel_id=1, source_target_pairs={{0,3},{1,2},{2,1},{3,0},{4,7},{5,6},{6,5},{7,4},{8,11},{9,10},{10,... | collective-permute-start | bytes 196616 | tf_op jit(solution)/shard_map/ppermute | solution.py:25
  27.2 7.2 %collective-permute-start.16 = (bf16[64,512]{1,0:T(8,128)(2,1)S(1)}, bf16[64,512]{1,0:T(8,128)(2,1)S(1)}, u32[]{:S(2)}, u32[]{:S(2)}) collective-permute-start(bf16[64,512]{1,0:T(8,128)(2,1)S(1)} %gate_up.1.refs_0_), channel_id=1, source_target_pairs={{0,2},{1,3},{2,0},{3,1},{4,6},{5,7},{6,4},{7,5},{8,10},{9,11},{10,... | collective-permute-start | bytes 196616 | tf_op jit(solution)/shard_map/ppermute | solution.py:25
  28.0 6.5 %collective-permute-start.17 = (bf16[64,512]{1,0:T(8,128)(2,1)S(1)}, bf16[64,512]{1,0:T(8,128)(2,1)S(1)}, u32[]{:S(2)}, u32[]{:S(2)}) collective-permute-start(bf16[64,512]{1,0:T(8,128)(2,1)S(1)} %gate_up.1.refs_0_), channel_id=1, source_target_pairs={{0,1},{1,0},{2,3},{3,2},{4,5},{5,4},{6,7},{7,6},{8,9},{9,8},{10,11... | collective-permute-start | bytes 196616 | tf_op jit(solution)/shard_map/ppermute | solution.py:25
  35.5 1.9 %collective-permute-start.18 = (bf16[16,1792]{1,0:T(8,128)(2,1)S(1)}, bf16[16,1792]{1,0:T(8,128)(2,1)S(1)}, u32[]{:S(2)}, u32[]{:S(2)}) collective-permute-start(bf16[16,1792]{1,0:T(8,128)(2,1)S(1)} %get-tuple-element.36), channel_id=1, source_target_pairs={{0,4},{4,0},{8,12},{12,8},{1,5},{5,1},{9,13},{13,9},{2,6},{6,2},{1... | collective-permute-start | bytes 172040 | tf_op jit(solution)/shard_map/ppermute | solution.py:25
  35.6 4.3 %collective-permute-start.19 = (bf16[16,1792]{1,0:T(8,128)(2,1)S(1)}, bf16[16,1792]{1,0:T(8,128)(2,1)S(1)}, u32[]{:S(2)}, u32[]{:S(2)}) collective-permute-start(bf16[16,1792]{1,0:T(8,128)(2,1)S(1)} %get-tuple-element.37), channel_id=1, source_target_pairs={{0,8},{4,12},{8,0},{12,4},{1,9},{5,13},{9,1},{13,5},{2,10},{6,14},... | collective-permute-start | bytes 172040 | tf_op jit(solution)/shard_map/ppermute | solution.py:25
  37.2 3.9 %collective-permute-start.20 = (bf16[16,1792]{1,0:T(8,128)(2,1)S(1)}, bf16[16,1792]{1,0:T(8,128)(2,1)S(1)}, u32[]{:S(2)}, u32[]{:S(2)}) collective-permute-start(bf16[16,1792]{1,0:T(8,128)(2,1)S(1)} %get-tuple-element.38), channel_id=1, source_target_pairs={{0,12},{4,8},{8,4},{12,0},{1,13},{5,9},{9,5},{13,1},{2,14},{6,10},... | collective-permute-start | bytes 172040 | tf_op jit(solution)/shard_map/ppermute | solution.py:25
  41.3 5.8 %collective-permute-start.21 = (bf16[8,1792]{1,0:T(8,128)(2,1)S(1)}, bf16[8,1792]{1,0:T(8,128)(2,1)S(1)}, u32[]{:S(2)}, u32[]{:S(2)}) collective-permute-start(bf16[8,1792]{1,0:T(8,128)(2,1)S(1)} %get-tuple-element.39), channel_id=1, source_target_pairs={{0,3},{1,2},{2,1},{3,0},{4,7},{5,6},{6,5},{7,4},{8,11},{9,10},{10,... | collective-permute-start | bytes 86024 | tf_op jit(solution)/shard_map/ppermute | solution.py:25
  43.2 4.8 %collective-permute-start.22 = (bf16[8,1792]{1,0:T(8,128)(2,1)S(1)}, bf16[8,1792]{1,0:T(8,128)(2,1)S(1)}, u32[]{:S(2)}, u32[]{:S(2)}) collective-permute-start(bf16[8,1792]{1,0:T(8,128)(2,1)S(1)} %get-tuple-element.40), channel_id=1, source_target_pairs={{0,2},{1,3},{2,0},{3,1},{4,6},{5,7},{6,4},{7,5},{8,10},{9,11},{10,... | collective-permute-start | bytes 86024 | tf_op jit(solution)/shard_map/ppermute | solution.py:25
  43.2 4.8 %collective-permute-start.23 = (bf16[8,1792]{1,0:T(8,128)(2,1)S(1)}, bf16[8,1792]{1,0:T(8,128)(2,1)S(1)}, u32[]{:S(2)}, u32[]{:S(2)}) collective-permute-start(bf16[8,1792]{1,0:T(8,128)(2,1)S(1)} %get-tuple-element.41), channel_id=1, source_target_pairs={{0,1},{1,0},{2,3},{3,2},{4,5},{5,4},{6,7},{7,6},{8,9},{9,8},{10,11... | collective-permute-start | bytes 86024 | tf_op jit(solution)/shard_map/ppermute | solution.py:25

commit v5 on v4

--- a/solution.py
+++ b/solution.py
@@ -117,10 +117,11 @@
         out[...] = total[...].astype(jnp.bfloat16)
 
 
-def down_kernel(experts, first, n, last, *refs):
-    parts, w_down = refs[:n][::-1], refs[n]
-    before = None if first == 0 else refs[n + 1]
-    outs, rows = refs[n + 1 + (first > 0):-1], refs[-1]
+def down_kernel(experts, which, last, *refs):
+    n = len(which)
+    parts, w_down = refs[:n], refs[n]
+    before = None if which[0] == 0 else refs[n + 1]
+    outs, rows = refs[n + 1 + (which[0] > 0):-1], refs[-1]
     count, depth = parts[0].shape
     columns = w_down.shape[2]
     each = count // experts
@@ -133,7 +134,7 @@
     for c in range(0, columns, step):
         total = None if before is None else before[:, c:c + step]
         for k in range(n):
-            d = pl.multiple_of((sub ^ (first + k)) * depth, depth)
+            d = pl.multiple_of((sub ^ which[k]) * depth, depth)
             term = jnp.dot(
                 rows[:, k * depth:(k + 1) * depth],
                 w_down[0, pl.ds(d, depth), c:c + step],
@@ -297,23 +298,24 @@
     )(*[got[k, 0] for k in range(groups)])
     out_cols = down_weight.shape[2]
 
-    def down(first, n, *more):
-        last = first + n == groups
+    def down(which, last, *before):
         out = [array(groups * cap, out_cols)] * experts
         if not last:
             out = [jax.ShapeDtypeStruct((devices * cap, out_cols), jnp.float32)]
         return pl.pallas_call(
-            functools.partial(down_kernel, experts, first, n, last),
+            functools.partial(down_kernel, experts, which, last),
             out_shape=out,
-            in_specs=[VMEM] * (n + 1 + (first > 0)),
+            in_specs=[VMEM] * (len(which) + 1 + len(before)),
             out_specs=[VMEM] * len(out),
-            scratch_shapes=[pltpu.VMEM((devices * cap, n * columns), jnp.bfloat16)],
+            scratch_shapes=[pltpu.VMEM((devices * cap, len(which) * columns), jnp.bfloat16)],
             compiler_params=limit(8 if devices <= 16 else 24),
-            name=f"down_{first}",
-        )(*(parts[first:first + n][::-1] if first else more), down_weight, *(more if first else ()))
-
-    own_part, *shares = lax.optimization_barrier([parts[0]] + list(shares))
-    sent = down(1, groups - 1, *down(0, 1, own_part))
+            name=f"down_{which[0]}",
+        )(*[parts[k] for k in which], down_weight, *before)
+
+    parts[0], *shares = lax.optimization_barrier([parts[0]] + list(shares))
+    total = down((0,), False)
+    total = down((groups - 1, 1), False, *total)
+    sent = down(tuple(range(groups - 2, 1, -1)), True, *total)
 
     came = [sent[0]] + [swap(sent[e], "ep", experts, e) for e in range(1, experts)]
     summed = pl.pallas_call(

time: 48.8 us -> 48.2 us (0.988)
  waiting for transfers between devices: 15.7 us -> 14.9 us
    ppermute x24, waiting for transfers between devices: 15.7 us -> 14.9 us  [swap(): return lax.ppermute(x, axis, [(i, i ^ k) for i in range(size)])]
    pallas_call x2 -> x3, Pallas kernels: 1.53 us -> 1.64 us  [down(): pl.pallas_call(functools.partial(down_kernel, experts, which, last), out_...]
  transfers between devices with their start and end apart: 24 -> 24, of which waited for: 15 -> 16; matrix products, arithmetic and copies ran while one was open for 0% -> 0% of each run, Pallas kernels for 2% -> 4%
where the time goes in v5:
time: 48.2 us; the launch traced here: 48.1 us
  starting transfers between devices  25.6 us (53%)
  waiting for transfers between devices  14.9 us (31%)
  Pallas kernels  7.3 us (15%)
    ppermute x24, starting transfers between devices, swap(): return lax.ppermute(x, axis, [(i, i ^ k) for i in range(size)])  25.6 us
    ppermute x24, waiting for transfers between devices, swap(): return lax.ppermute(x, axis, [(i, i ^ k) for i in range(size)])  14.9 us
    pallas_call x1, Pallas kernels, body(): pl.pallas_call(functools.partial(up_kernel, len(arrays), count, chosen, c...  2.51 us
    pallas_call x3, Pallas kernels, down(): pl.pallas_call(functools.partial(down_kernel, experts, which, last), out_...  1.64 us
    pallas_call x1, Pallas kernels, body(): pl.pallas_call(pack_kernel, out_shape=array(count, width + LANES), in_spe...  1.59 us
  transfers between devices with their start and end apart: 24, of which 16 were waited for; matrix products, arithmetic and copies ran while one was open for 0% of the time, Pallas kernels for 4%

profile of v5, /device:TPU:0, one launch (start us, length us, event | category | flops | bytes accessed | tf_op | source)
XLA Modules:
  0.0 48.1 jit_solution(9999031341535143916)
XLA Ops:
  0.0 1.6 %pack.1.refs_15_.refs_0_ = bf16[8,7296]{1,0:T(8,128)(2,1)} custom-call(bf16[8,7168]{1,0:T(8,128)(2,1)} %tokens.1, s32[2,8]{1,0:T(2,128)} %bitcast.8, f32[2,8]{1,0:T(2,128)} %bitcast.9), custom_call_target="tpu_custom_call" | custom-call | tf_op jit(solution)/shard_map/pack/pallas_call | solution.py:223
  1.6 3.1 %collective-permute-start.6 = (bf16[8,7296]{1,0:T(8,128)(2,1)}, bf16[8,7296]{1,0:T(8,128)(2,1)S(1)}, u32[]{:S(2)}, u32[]{:S(2)}) collective-permute-start(bf16[8,7296]{1,0:T(8,128)(2,1)} %pack.1.refs_15_.refs_0_), channel_id=1, source_target_pairs={{0,1},{1,0},{2,3},{3,2},{4,5},{5,4},{6,7},{7,6},{8,9},{9,8},{10,11... | collective-permute-start | bytes 350216 | tf_op jit(solution)/shard_map/ppermute | solution.py:25
  4.7 2.6 %collective-permute-start.3 = (bf16[8,7296]{1,0:T(8,128)(2,1)}, bf16[8,7296]{1,0:T(8,128)(2,1)S(1)}, u32[]{:S(2)}, u32[]{:S(2)}) collective-permute-start(bf16[8,7296]{1,0:T(8,128)(2,1)} %pack.1.refs_15_.refs_0_), channel_id=1, source_target_pairs={{0,2},{1,3},{2,0},{3,1},{4,6},{5,7},{6,4},{7,5},{8,10},{9,11},{10,... | collective-permute-start | bytes 350216 | tf_op jit(solution)/shard_map/ppermute | solution.py:25
  7.3 1.5 %collective-permute-start = (bf16[8,7296]{1,0:T(8,128)(2,1)}, bf16[8,7296]{1,0:T(8,128)(2,1)S(1)}, u32[]{:S(2)}, u32[]{:S(2)}) collective-permute-start(bf16[8,7296]{1,0:T(8,128)(2,1)} %pack.1.refs_15_.refs_0_), channel_id=1, source_target_pairs={{0,8},{4,12},{8,0},{12,4},{1,9},{5,13},{9,1},{13,5},{2,10},{6,14},... | collective-permute-start | bytes 350216 | tf_op jit(solution)/shard_map/ppermute | solution.py:25
  8.8 0.5 %collective-permute-done.6.x = bf16[8,7296]{1,0:T(8,128)(2,1)S(1)} collective-permute-done((bf16[8,7296]{1,0:T(8,128)(2,1)}, bf16[8,7296]{1,0:T(8,128)(2,1)S(1)}, u32[]{:S(2)}, u32[]{:S(2)}) %collective-permute-start.6) | collective-permute-done | bytes 116768 | tf_op jit(solution)/shard_map/ppermute | solution.py:25
  9.3 0.0 copy-start
  9.3 0.0 slice-start.3
  9.3 0.0 slice-start.5
  9.3 1.9 %collective-permute-start.7 = (bf16[8,7296]{1,0:T(8,128)(2,1)S(1)}, bf16[8,7296]{1,0:T(8,128)(2,1)S(1)}, u32[]{:S(2)}, u32[]{:S(2)}) collective-permute-start(bf16[8,7296]{1,0:T(8,128)(2,1)S(1)} %hold.3.refs_14_.refs_1_), channel_id=1, source_target_pairs={{0,8},{4,12},{8,0},{12,4},{1,9},{5,13},{9,1},{13,5},{2,10},{6,14},... | collective-permute-start | bytes 350216 | tf_op jit(solution)/shard_map/ppermute | solution.py:25
  11.3 1.8 %collective-permute-done.3.refs_13_.refs_2_ = bf16[8,7296]{1,0:T(8,128)(2,1)S(1)} collective-permute-done((bf16[8,7296]{1,0:T(8,128)(2,1)}, bf16[8,7296]{1,0:T(8,128)(2,1)S(1)}, u32[]{:S(2)}, u32[]{:S(2)}) %collective-permute-start.3) | collective-permute-done | bytes 116768 | tf_op jit(solution)/shard_map/ppermute | solution.py:25
  13.0 0.4 collective-permute-start.10
  13.4 0.0 collective-permute-done.x
  13.5 0.0 slice-start.1
  13.5 2.1 %collective-permute-start.1 = (bf16[8,7296]{1,0:T(8,128)(2,1)S(1)}, bf16[8,7296]{1,0:T(8,128)(2,1)S(1)}, u32[]{:S(2)}, u32[]{:S(2)}) collective-permute-start(bf16[8,7296]{1,0:T(8,128)(2,1)S(1)} %hold.2.refs_7_), channel_id=1, source_target_pairs={{0,3},{1,2},{2,1},{3,0},{4,7},{5,6},{6,5},{7,4},{8,11},{9,10},{10,... | collective-permute-start | bytes 350216 | tf_op jit(solution)/shard_map/ppermute | solution.py:25
  15.6 1.6 %collective-permute-start.4 = (bf16[8,7296]{1,0:T(8,128)(2,1)S(1)}, bf16[8,7296]{1,0:T(8,128)(2,1)S(1)}, u32[]{:S(2)}, u32[]{:S(2)}) collective-permute-start(bf16[8,7296]{1,0:T(8,128)(2,1)S(1)} %collective-permute-done.3.refs_13_.refs_2_), channel_id=1, source_target_pairs={{0,8},{4,12},{8,0},{12,4},{1,9},{5,13},{9,1},{13,5},{2,10},{6,14},... | collective-permute-start | bytes 350216 | tf_op jit(solution)/shard_map/ppermute | solution.py:25
  17.1 0.0 collective-permute-done.7.refs_6_
  17.1 0.0 collective-permute-start.12
  17.1 0.5 %collective-permute-start.13 = (bf16[8,7296]{1,0:T(8,128)(2,1)S(1)}, bf16[8,7296]{1,0:T(8,128)(2,1)S(1)}, u32[]{:S(2)}, u32[]{:S(2)}) collective-permute-start(bf16[8,7296]{1,0:T(8,128)(2,1)S(1)} %hold.3.refs_14_.refs_1_), channel_id=1, source_target_pairs={{0,4},{4,0},{8,12},{12,8},{1,5},{5,1},{9,13},{13,9},{2,6},{6,2},{1... | collective-permute-start | bytes 350216 | tf_op jit(solution)/shard_map/ppermute | solution.py:25
  17.7 1.4 %collective-permute-done.10.refs_12_.refs_3_ = bf16[8,7296]{1,0:T(8,128)(2,1)S(1)} collective-permute-done((bf16[8,7296]{1,0:T(8,128)(2,1)S(1)}, bf16[8,7296]{1,0:T(8,128)(2,1)S(1)}, u32[]{:S(2)}, u32[]{:S(2)}) %collective-permute-start.10) | collective-permute-done | bytes 116768 | tf_op jit(solution)/shard_map/ppermute | solution.py:25
  19.0 0.0 collective-permute-start.9
  19.0 1.4 %collective-permute-done.4.refs_5_ = bf16[8,7296]{1,0:T(8,128)(2,1)S(1)} collective-permute-done((bf16[8,7296]{1,0:T(8,128)(2,1)S(1)}, bf16[8,7296]{1,0:T(8,128)(2,1)S(1)}, u32[]{:S(2)}, u32[]{:S(2)}) %collective-permute-start.4) | collective-permute-done | bytes 116768 | tf_op jit(solution)/shard_map/ppermute | solution.py:25
  20.4 0.0 copy-done
  20.4 0.0 collective-permute-start.14
  20.4 0.0 collective-permute-done.1.refs_4_
  20.4 0.5 %collective-permute-start.8 = (bf16[8,7296]{1,0:T(8,128)(2,1)S(1)}, bf16[8,7296]{1,0:T(8,128)(2,1)S(1)}, u32[]{:S(2)}, u32[]{:S(2)}) collective-permute-start(bf16[8,7296]{1,0:T(8,128)(2,1)S(1)} %collective-permute-done.7.refs_6_), channel_id=1, source_target_pairs={{0,4},{4,0},{8,12},{12,8},{1,5},{5,1},{9,13},{13,9},{2,6},{6,2},{1... | collective-permute-start | bytes 350216 | tf_op jit(solution)/shard_map/ppermute | solution.py:25
  20.9 0.0 collective-permute-done.12.refs_9_
  20.9 0.1 collective-permute-start.11
  21.0 0.0 collective-permute-done.13.refs_10_
  21.0 0.4 collective-permute-start.5
  21.4 0.0 collective-permute-done.9.refs_3_
  21.4 0.1 collective-permute-start.2
  21.5 0.2 collective-permute-done.14.refs_11_
  21.7 0.2 collective-permute-done.8.refs_2_
  21.9 0.4 collective-permute-done.11.refs_8_
  22.2 0.2 collective-permute-done.5.refs_1_
  22.4 0.4 collective-permute-done.2.refs_0_
  22.8 0.0 slice-done.2
  22.8 0.0 slice-done.4
  22.8 0.0 slice-done.3
  22.8 2.5 %gate_up.1.refs_0_ = bf16[64,512]{1,0:T(8,128)(2,1)S(1)} custom-call(bf16[8,7296]{1,0:T(8,128)(2,1)S(1)} %collective-permute-done.2.refs_0_, bf16[8,7296]{1,0:T(8,128)(2,1)S(1)} %collective-permute-done.5.refs_1_, bf16[8,7296]{1,0:T(8,128)(2,1)S(1)} %collective-permute-done.8.refs_2_, bf16[8,7296]{1,0:T(8,128)(2,1)S(1)} %collective-permute-done.9.refs_3_, ...), custom_call_target="tpu_custom_call" | custom-call | tf_op jit(solution)/shard_map/gate_up/pallas_call | solution.py:277
  25.3 1.8 %collective-permute-start.16 = (bf16[64,512]{1,0:T(8,128)(2,1)S(1)}, bf16[64,512]{1,0:T(8,128)(2,1)S(1)}, u32[]{:S(2)}, u32[]{:S(2)}) collective-permute-start(bf16[64,512]{1,0:T(8,128)(2,1)S(1)} %gate_up.1.refs_0_), channel_id=1, source_target_pairs={{0,3},{1,2},{2,1},{3,0},{4,7},{5,6},{6,5},{7,4},{8,11},{9,10},{10,... | collective-permute-start | bytes 196616 | tf_op jit(solution)/shard_map/ppermute | solution.py:25
  27.2 0.2 collective-permute-start.17
  27.4 2.4 %collective-permute-start.15 = (bf16[64,512]{1,0:T(8,128)(2,1)S(1)}, bf16[64,512]{1,0:T(8,128)(2,1)S(1)}, u32[]{:S(2)}, u32[]{:S(2)}) collective-permute-start(bf16[64,512]{1,0:T(8,128)(2,1)S(1)} %gate_up.1.refs_0_), channel_id=1, source_target_pairs={{0,2},{1,3},{2,0},{3,1},{4,6},{5,7},{6,4},{7,5},{8,10},{9,11},{10,... | collective-permute-start | bytes 196616 | tf_op jit(solution)/shard_map/ppermute | solution.py:25
  29.8 0.6 %shares.1 = (bf16[32,64]{1,0:T(8,128)(2,1)S(1)}, bf16[32,64]{1,0:T(8,128)(2,1)S(1)}, bf16[32,64]{1,0:T(8,128)(2,1)S(1)}) custom-call(bf16[8,7296]{1,0:T(8,128)(2,1)S(1)} %copy-done, bf16[8,7296]{1,0:T(8,128)(2,1)S(1)} %hold.3.refs_14_.refs_1_, bf16[8,7296]{1,0:T(8,128)(2,1)S(1)} %collective-permute-done.3.refs_13_.refs_2_, ...), custom_call_target="tpu_custom_call" | custom-call | tf_op jit(solution)/shard_map/shares/pallas_call | solution.py:291
  30.4 0.5 down_0.1.refs_3_
  30.9 1.2 %collective-permute-done.16.refs_0_ = bf16[64,512]{1,0:T(8,128)(2,1)S(1)} collective-permute-done((bf16[64,512]{1,0:T(8,128)(2,1)S(1)}, bf16[64,512]{1,0:T(8,128)(2,1)S(1)}, u32[]{:S(2)}, u32[]{:S(2)}) %collective-permute-start.16) | collective-permute-done | bytes 65568 | tf_op jit(solution)/shard_map/ppermute | solution.py:25
  32.1 1.5 %collective-permute-done.17.refs_1_ = bf16[64,512]{1,0:T(8,128)(2,1)S(1)} collective-permute-done((bf16[64,512]{1,0:T(8,128)(2,1)S(1)}, bf16[64,512]{1,0:T(8,128)(2,1)S(1)}, u32[]{:S(2)}, u32[]{:S(2)}) %collective-permute-start.17) | collective-permute-done | bytes 65568 | tf_op jit(solution)/shard_map/ppermute | solution.py:25
  33.6 0.7 %down_3.1.refs_2_ = f32[64,1792]{1,0:T(8,128)S(1)} custom-call(bf16[64,512]{1,0:T(8,128)(2,1)S(1)} %collective-permute-done.16.refs_0_, bf16[64,512]{1,0:T(8,128)(2,1)S(1)} %collective-permute-done.17.refs_1_, bf16[1,2048,1792]{2,1,0:T(8,128)(2,1)S(1)} %bitcast.3, f32[64,1792]{1,0:T(8,128)S(1)} %down_0.1.refs_3_), custom_call_target="tpu_custom_call" | custom-call | tf_op jit(solution)/shard_map/down_3/pallas_call | solution.py:305
  34.4 0.1 collective-permute-done.15.refs_0_
  34.4 0.4 down_2.1
  34.9 0.1 collective-permute-start.18
  34.9 1.6 %collective-permute-start.19 = (bf16[16,1792]{1,0:T(8,128)(2,1)S(1)}, bf16[16,1792]{1,0:T(8,128)(2,1)S(1)}, u32[]{:S(2)}, u32[]{:S(2)}) collective-permute-start(bf16[16,1792]{1,0:T(8,128)(2,1)S(1)} %get-tuple-element.37), channel_id=1, source_target_pairs={{0,8},{4,12},{8,0},{12,4},{1,9},{5,13},{9,1},{13,5},{2,10},{6,14},... | collective-permute-start | bytes 172040 | tf_op jit(solution)/shard_map/ppermute | solution.py:25
  36.6 0.2 collective-permute-start.20
  36.8 0.0 collective-permute-done.18.refs_4_
  36.8 2.5 %collective-permute-done.19.refs_5_ = bf16[16,1792]{1,0:T(8,128)(2,1)S(1)} collective-permute-done((bf16[16,1792]{1,0:T(8,128)(2,1)S(1)}, bf16[16,1792]{1,0:T(8,128)(2,1)S(1)}, u32[]{:S(2)}, u32[]{:S(2)}) %collective-permute-start.19) | collective-permute-done | bytes 57376 | tf_op jit(solution)/shard_map/ppermute | solution.py:25
  39.3 1.2 %collective-permute-done.20.refs_6_ = bf16[16,1792]{1,0:T(8,128)(2,1)S(1)} collective-permute-done((bf16[16,1792]{1,0:T(8,128)(2,1)S(1)}, bf16[16,1792]{1,0:T(8,128)(2,1)S(1)}, u32[]{:S(2)}, u32[]{:S(2)}) %collective-permute-start.20) | collective-permute-done | bytes 57376 | tf_op jit(solution)/shard_map/ppermute | solution.py:25
  40.4 0.2 combine.1
  40.7 1.9 %collective-permute-start.21 = (bf16[8,1792]{1,0:T(8,128)(2,1)S(1)}, bf16[8,1792]{1,0:T(8,128)(2,1)S(1)}, u32[]{:S(2)}, u32[]{:S(2)}) collective-permute-start(bf16[8,1792]{1,0:T(8,128)(2,1)S(1)} %get-tuple-element.39), channel_id=1, source_target_pairs={{0,3},{1,2},{2,1},{3,0},{4,7},{5,6},{6,5},{7,4},{8,11},{9,10},{10,... | collective-permute-start | bytes 86024 | tf_op jit(solution)/shard_map/ppermute | solution.py:25
  42.6 0.0 collective-permute-start.22
  42.6 2.5 %collective-permute-start.23 = (bf16[8,1792]{1,0:T(8,128)(2,1)S(1)}, bf16[8,1792]{1,0:T(8,128)(2,1)S(1)}, u32[]{:S(2)}, u32[]{:S(2)}) collective-permute-start(bf16[8,1792]{1,0:T(8,128)(2,1)S(1)} %get-tuple-element.41), channel_id=1, source_target_pairs={{0,1},{1,0},{2,3},{3,2},{4,5},{5,4},{6,7},{7,6},{8,9},{9,8},{10,11... | collective-permute-start | bytes 86024 | tf_op jit(solution)/shard_map/ppermute | solution.py:25
  45.1 1.4 %collective-permute-done.21.refs_0_ = bf16[8,1792]{1,0:T(8,128)(2,1)S(1)} collective-permute-done((bf16[8,1792]{1,0:T(8,128)(2,1)S(1)}, bf16[8,1792]{1,0:T(8,128)(2,1)S(1)}, u32[]{:S(2)}, u32[]{:S(2)}) %collective-permute-start.21) | collective-permute-done | bytes 28704 | tf_op jit(solution)/shard_map/ppermute | solution.py:25
  46.5 0.9 %collective-permute-done.22.refs_1_ = bf16[8,1792]{1,0:T(8,128)(2,1)S(1)} collective-permute-done((bf16[8,1792]{1,0:T(8,128)(2,1)S(1)}, bf16[8,1792]{1,0:T(8,128)(2,1)S(1)}, u32[]{:S(2)}, u32[]{:S(2)}) %collective-permute-start.22) | collective-permute-done | bytes 28704 | tf_op jit(solution)/shard_map/ppermute | solution.py:25
  47.4 0.0 collective-permute-done.23.refs_2_
  47.4 0.7 %place.1 = bf16[8,7168]{1,0:T(8,128)(2,1)} custom-call(bf16[8,1792]{1,0:T(8,128)(2,1)S(1)} %collective-permute-done.21.refs_0_, bf16[8,1792]{1,0:T(8,128)(2,1)S(1)} %collective-permute-done.22.refs_1_, bf16[8,1792]{1,0:T(8,128)(2,1)S(1)} %collective-permute-done.23.refs_2_, bf16[8,1792]{1,0:T(8,128)(2,1)S(1)} %get-tuple-element.42.refs_3_), custom_call_target="tpu_custom_call" | custom-call | tf_op jit(solution)/shard_map/place/pallas_call | solution.py:332
  (11 shorter events, 0.0 us)
Async XLA Ops:
  1.6 7.7 %collective-permute-start.6 = (bf16[8,7296]{1,0:T(8,128)(2,1)}, bf16[8,7296]{1,0:T(8,128)(2,1)S(1)}, u32[]{:S(2)}, u32[]{:S(2)}) collective-permute-start(bf16[8,7296]{1,0:T(8,128)(2,1)} %pack.1.refs_15_.refs_0_), channel_id=1, source_target_pairs={{0,1},{1,0},{2,3},{3,2},{4,5},{5,4},{6,7},{7,6},{8,9},{9,8},{10,11... | collective-permute-start | bytes 350216 | tf_op jit(solution)/shard_map/ppermute | solution.py:25
  4.7 8.3 %collective-permute-start.3 = (bf16[8,7296]{1,0:T(8,128)(2,1)}, bf16[8,7296]{1,0:T(8,128)(2,1)S(1)}, u32[]{:S(2)}, u32[]{:S(2)}) collective-permute-start(bf16[8,7296]{1,0:T(8,128)(2,1)} %pack.1.refs_15_.refs_0_), channel_id=1, source_target_pairs={{0,2},{1,3},{2,0},{3,1},{4,6},{5,7},{6,4},{7,5},{8,10},{9,11},{10,... | collective-permute-start | bytes 350216 | tf_op jit(solution)/shard_map/ppermute | solution.py:25
  7.3 6.2 %collective-permute-start = (bf16[8,7296]{1,0:T(8,128)(2,1)}, bf16[8,7296]{1,0:T(8,128)(2,1)S(1)}, u32[]{:S(2)}, u32[]{:S(2)}) collective-permute-start(bf16[8,7296]{1,0:T(8,128)(2,1)} %pack.1.refs_15_.refs_0_), channel_id=1, source_target_pairs={{0,8},{4,12},{8,0},{12,4},{1,9},{5,13},{9,1},{13,5},{2,10},{6,14},... | collective-permute-start | bytes 350216 | tf_op jit(solution)/shard_map/ppermute | solution.py:25
  9.3 13.5 %slice-start.2 = ((s8[7340032]{0:T(1024)(128)(4,1)}), s8[4194304]{0:T(1024)(128)(4,1)S(1)}, s32[]{:S(2)}) async-start(s8[7340032]{0:T(1024)(128)(4,1)} %bitcast.4), calls=%async_computation.2 | async-start | bytes 8388608
  9.3 13.5 %slice-start.4 = ((s8[7340032]{0:T(1024)(128)(4,1)}), s8[4194304]{0:T(1024)(128)(4,1)S(1)}, s32[]{:S(2)}) async-start(s8[7340032]{0:T(1024)(128)(4,1)} %bitcast.6), calls=%async_computation.4 | async-start | bytes 8388608
  9.3 11.1 %copy-start = (bf16[8,7296]{1,0:T(8,128)(2,1)S(1)}, bf16[8,7296]{1,0:T(8,128)(2,1)}, u32[]{:S(2)}) copy-start(bf16[8,7296]{1,0:T(8,128)(2,1)} %pack.1.refs_15_.refs_0_) | copy-start | bytes 350212
  9.3 13.5 %slice-start.3 = ((s8[7340032]{0:T(1024)(128)(4,1)}), s8[3145728]{0:T(1024)(128)(4,1)S(1)}, s32[]{:S(2)}) async-start(s8[7340032]{0:T(1024)(128)(4,1)} %bitcast.4), calls=%async_computation.3 | async-start | bytes 6291456
  9.3 13.4 %slice-start.5 = ((s8[7340032]{0:T(1024)(128)(4,1)}), s8[3145728]{0:T(1024)(128)(4,1)S(1)}, s32[]{:S(2)}) async-start(s8[7340032]{0:T(1024)(128)(4,1)} %bitcast.6), calls=%async_computation.5 | async-start | bytes 6291456
  9.3 7.8 %collective-permute-start.7 = (bf16[8,7296]{1,0:T(8,128)(2,1)S(1)}, bf16[8,7296]{1,0:T(8,128)(2,1)S(1)}, u32[]{:S(2)}, u32[]{:S(2)}) collective-permute-start(bf16[8,7296]{1,0:T(8,128)(2,1)S(1)} %hold.3.refs_14_.refs_1_), channel_id=1, source_target_pairs={{0,8},{4,12},{8,0},{12,4},{1,9},{5,13},{9,1},{13,5},{2,10},{6,14},... | collective-permute-start | bytes 350216 | tf_op jit(solution)/shard_map/ppermute | solution.py:25
  13.0 6.0 %collective-permute-start.10 = (bf16[8,7296]{1,0:T(8,128)(2,1)S(1)}, bf16[8,7296]{1,0:T(8,128)(2,1)S(1)}, u32[]{:S(2)}, u32[]{:S(2)}) collective-permute-start(bf16[8,7296]{1,0:T(8,128)(2,1)S(1)} %collective-permute-done.3.refs_13_.refs_2_), channel_id=1, source_target_pairs={{0,1},{1,0},{2,3},{3,2},{4,5},{5,4},{6,7},{7,6},{8,9},{9,8},{10,11... | collective-permute-start | bytes 350216 | tf_op jit(solution)/shard_map/ppermute | solution.py:25
  13.4 17.0 %slice-start = ((s8[7340032]{0:T(1024)(128)(4,1)}), s8[4194304]{0:T(1024)(128)(4,1)S(1)}, s32[]{:S(2)}) async-start(s8[7340032]{0:T(1024)(128)(4,1)} %bitcast.2), calls=%async_computation | async-start | bytes 8388608
  13.5 17.0 %slice-start.1 = ((s8[7340032]{0:T(1024)(128)(4,1)}), s8[3145728]{0:T(1024)(128)(4,1)S(1)}, s32[]{:S(2)}) async-start(s8[7340032]{0:T(1024)(128)(4,1)} %bitcast.2), calls=%async_computation.1 | async-start | bytes 6291456
  13.5 6.9 %collective-permute-start.1 = (bf16[8,7296]{1,0:T(8,128)(2,1)S(1)}, bf16[8,7296]{1,0:T(8,128)(2,1)S(1)}, u32[]{:S(2)}, u32[]{:S(2)}) collective-permute-start(bf16[8,7296]{1,0:T(8,128)(2,1)S(1)} %hold.2.refs_7_), channel_id=1, source_target_pairs={{0,3},{1,2},{2,1},{3,0},{4,7},{5,6},{6,5},{7,4},{8,11},{9,10},{10,... | collective-permute-start | bytes 350216 | tf_op jit(solution)/shard_map/ppermute | solution.py:25
  15.6 4.8 %collective-permute-start.4 = (bf16[8,7296]{1,0:T(8,128)(2,1)S(1)}, bf16[8,7296]{1,0:T(8,128)(2,1)S(1)}, u32[]{:S(2)}, u32[]{:S(2)}) collective-permute-start(bf16[8,7296]{1,0:T(8,128)(2,1)S(1)} %collective-permute-done.3.refs_13_.refs_2_), channel_id=1, source_target_pairs={{0,8},{4,12},{8,0},{12,4},{1,9},{5,13},{9,1},{13,5},{2,10},{6,14},... | collective-permute-start | bytes 350216 | tf_op jit(solution)/shard_map/ppermute | solution.py:25
  17.1 3.8 %collective-permute-start.12 = (bf16[8,7296]{1,0:T(8,128)(2,1)S(1)}, bf16[8,7296]{1,0:T(8,128)(2,1)S(1)}, u32[]{:S(2)}, u32[]{:S(2)}) collective-permute-start(bf16[8,7296]{1,0:T(8,128)(2,1)S(1)} %collective-permute-done.3.refs_13_.refs_2_), channel_id=1, source_target_pairs={{0,4},{4,0},{8,12},{12,8},{1,5},{5,1},{9,13},{13,9},{2,6},{6,2},{1... | collective-permute-start | bytes 350216 | tf_op jit(solution)/shard_map/ppermute | solution.py:25
  17.1 3.8 %collective-permute-start.13 = (bf16[8,7296]{1,0:T(8,128)(2,1)S(1)}, bf16[8,7296]{1,0:T(8,128)(2,1)S(1)}, u32[]{:S(2)}, u32[]{:S(2)}) collective-permute-start(bf16[8,7296]{1,0:T(8,128)(2,1)S(1)} %hold.3.refs_14_.refs_1_), channel_id=1, source_target_pairs={{0,4},{4,0},{8,12},{12,8},{1,5},{5,1},{9,13},{13,9},{2,6},{6,2},{1... | collective-permute-start | bytes 350216 | tf_op jit(solution)/shard_map/ppermute | solution.py:25
  19.0 2.4 %collective-permute-start.9 = (bf16[8,7296]{1,0:T(8,128)(2,1)S(1)}, bf16[8,7296]{1,0:T(8,128)(2,1)S(1)}, u32[]{:S(2)}, u32[]{:S(2)}) collective-permute-start(bf16[8,7296]{1,0:T(8,128)(2,1)S(1)} %hold.2.refs_7_), channel_id=1, source_target_pairs={{0,4},{4,0},{8,12},{12,8},{1,5},{5,1},{9,13},{13,9},{2,6},{6,2},{1... | collective-permute-start | bytes 350216 | tf_op jit(solution)/shard_map/ppermute | solution.py:25
  20.4 1.3 %collective-permute-start.14 = (bf16[8,7296]{1,0:T(8,128)(2,1)S(1)}, bf16[8,7296]{1,0:T(8,128)(2,1)S(1)}, u32[]{:S(2)}, u32[]{:S(2)}) collective-permute-start(bf16[8,7296]{1,0:T(8,128)(2,1)S(1)} %copy-done), channel_id=1, source_target_pairs={{0,4},{4,0},{8,12},{12,8},{1,5},{5,1},{9,13},{13,9},{2,6},{6,2},{1... | collective-permute-start | bytes 350216 | tf_op jit(solution)/shard_map/ppermute | solution.py:25
  20.4 1.5 %collective-permute-start.8 = (bf16[8,7296]{1,0:T(8,128)(2,1)S(1)}, bf16[8,7296]{1,0:T(8,128)(2,1)S(1)}, u32[]{:S(2)}, u32[]{:S(2)}) collective-permute-start(bf16[8,7296]{1,0:T(8,128)(2,1)S(1)} %collective-permute-done.7.refs_6_), channel_id=1, source_target_pairs={{0,4},{4,0},{8,12},{12,8},{1,5},{5,1},{9,13},{13,9},{2,6},{6,2},{1... | collective-permute-start | bytes 350216 | tf_op jit(solution)/shard_map/ppermute | solution.py:25
  20.9 1.3 %collective-permute-start.11 = (bf16[8,7296]{1,0:T(8,128)(2,1)S(1)}, bf16[8,7296]{1,0:T(8,128)(2,1)S(1)}, u32[]{:S(2)}, u32[]{:S(2)}) collective-permute-start(bf16[8,7296]{1,0:T(8,128)(2,1)S(1)} %collective-permute-done.10.refs_12_.refs_3_), channel_id=1, source_target_pairs={{0,4},{4,0},{8,12},{12,8},{1,5},{5,1},{9,13},{13,9},{2,6},{6,2},{1... | collective-permute-start | bytes 350216 | tf_op jit(solution)/shard_map/ppermute | solution.py:25
  21.0 1.4 %collective-permute-start.5 = (bf16[8,7296]{1,0:T(8,128)(2,1)S(1)}, bf16[8,7296]{1,0:T(8,128)(2,1)S(1)}, u32[]{:S(2)}, u32[]{:S(2)}) collective-permute-start(bf16[8,7296]{1,0:T(8,128)(2,1)S(1)} %collective-permute-done.4.refs_5_), channel_id=1, source_target_pairs={{0,4},{4,0},{8,12},{12,8},{1,5},{5,1},{9,13},{13,9},{2,6},{6,2},{1... | collective-permute-start | bytes 350216 | tf_op jit(solution)/shard_map/ppermute | solution.py:25
  21.4 1.3 %collective-permute-start.2 = (bf16[8,7296]{1,0:T(8,128)(2,1)S(1)}, bf16[8,7296]{1,0:T(8,128)(2,1)S(1)}, u32[]{:S(2)}, u32[]{:S(2)}) collective-permute-start(bf16[8,7296]{1,0:T(8,128)(2,1)S(1)} %collective-permute-done.1.refs_4_), channel_id=1, source_target_pairs={{0,4},{4,0},{8,12},{12,8},{1,5},{5,1},{9,13},{13,9},{2,6},{6,2},{1... | collective-permute-start | bytes 350216 | tf_op jit(solution)/shard_map/ppermute | solution.py:25
  25.3 6.8 %collective-permute-start.16 = (bf16[64,512]{1,0:T(8,128)(2,1)S(1)}, bf16[64,512]{1,0:T(8,128)(2,1)S(1)}, u32[]{:S(2)}, u32[]{:S(2)}) collective-permute-start(bf16[64,512]{1,0:T(8,128)(2,1)S(1)} %gate_up.1.refs_0_), channel_id=1, source_target_pairs={{0,3},{1,2},{2,1},{3,0},{4,7},{5,6},{6,5},{7,4},{8,11},{9,10},{10,... | collective-permute-start | bytes 196616 | tf_op jit(solution)/shard_map/ppermute | solution.py:25
  27.2 6.4 %collective-permute-start.17 = (bf16[64,512]{1,0:T(8,128)(2,1)S(1)}, bf16[64,512]{1,0:T(8,128)(2,1)S(1)}, u32[]{:S(2)}, u32[]{:S(2)}) collective-permute-start(bf16[64,512]{1,0:T(8,128)(2,1)S(1)} %gate_up.1.refs_0_), channel_id=1, source_target_pairs={{0,1},{1,0},{2,3},{3,2},{4,5},{5,4},{6,7},{7,6},{8,9},{9,8},{10,11... | collective-permute-start | bytes 196616 | tf_op jit(solution)/shard_map/ppermute | solution.py:25
  27.4 7.0 %collective-permute-start.15 = (bf16[64,512]{1,0:T(8,128)(2,1)S(1)}, bf16[64,512]{1,0:T(8,128)(2,1)S(1)}, u32[]{:S(2)}, u32[]{:S(2)}) collective-permute-start(bf16[64,512]{1,0:T(8,128)(2,1)S(1)} %gate_up.1.refs_0_), channel_id=1, source_target_pairs={{0,2},{1,3},{2,0},{3,1},{4,6},{5,7},{6,4},{7,5},{8,10},{9,11},{10,... | collective-permute-start | bytes 196616 | tf_op jit(solution)/shard_map/ppermute | solution.py:25
  34.9 1.9 %collective-permute-start.18 = (bf16[16,1792]{1,0:T(8,128)(2,1)S(1)}, bf16[16,1792]{1,0:T(8,128)(2,1)S(1)}, u32[]{:S(2)}, u32[]{:S(2)}) collective-permute-start(bf16[16,1792]{1,0:T(8,128)(2,1)S(1)} %get-tuple-element.36), channel_id=1, source_target_pairs={{0,4},{4,0},{8,12},{12,8},{1,5},{5,1},{9,13},{13,9},{2,6},{6,2},{1... | collective-permute-start | bytes 172040 | tf_op jit(solution)/shard_map/ppermute | solution.py:25
  34.9 4.3 %collective-permute-start.19 = (bf16[16,1792]{1,0:T(8,128)(2,1)S(1)}, bf16[16,1792]{1,0:T(8,128)(2,1)S(1)}, u32[]{:S(2)}, u32[]{:S(2)}) collective-permute-start(bf16[16,1792]{1,0:T(8,128)(2,1)S(1)} %get-tuple-element.37), channel_id=1, source_target_pairs={{0,8},{4,12},{8,0},{12,4},{1,9},{5,13},{9,1},{13,5},{2,10},{6,14},... | collective-permute-start | bytes 172040 | tf_op jit(solution)/shard_map/ppermute | solution.py:25
  36.6 3.9 %collective-permute-start.20 = (bf16[16,1792]{1,0:T(8,128)(2,1)S(1)}, bf16[16,1792]{1,0:T(8,128)(2,1)S(1)}, u32[]{:S(2)}, u32[]{:S(2)}) collective-permute-start(bf16[16,1792]{1,0:T(8,128)(2,1)S(1)} %get-tuple-element.38), channel_id=1, source_target_pairs={{0,12},{4,8},{8,4},{12,0},{1,13},{5,9},{9,5},{13,1},{2,14},{6,10},... | collective-permute-start | bytes 172040 | tf_op jit(solution)/shard_map/ppermute | solution.py:25
  40.7 5.8 %collective-permute-start.21 = (bf16[8,1792]{1,0:T(8,128)(2,1)S(1)}, bf16[8,1792]{1,0:T(8,128)(2,1)S(1)}, u32[]{:S(2)}, u32[]{:S(2)}) collective-permute-start(bf16[8,1792]{1,0:T(8,128)(2,1)S(1)} %get-tuple-element.39), channel_id=1, source_target_pairs={{0,3},{1,2},{2,1},{3,0},{4,7},{5,6},{6,5},{7,4},{8,11},{9,10},{10,... | collective-permute-start | bytes 86024 | tf_op jit(solution)/shard_map/ppermute | solution.py:25
  42.6 4.8 %collective-permute-start.22 = (bf16[8,1792]{1,0:T(8,128)(2,1)S(1)}, bf16[8,1792]{1,0:T(8,128)(2,1)S(1)}, u32[]{:S(2)}, u32[]{:S(2)}) collective-permute-start(bf16[8,1792]{1,0:T(8,128)(2,1)S(1)} %get-tuple-element.40), channel_id=1, source_target_pairs={{0,2},{1,3},{2,0},{3,1},{4,6},{5,7},{6,4},{7,5},{8,10},{9,11},{10,... | collective-permute-start | bytes 86024 | tf_op jit(solution)/shard_map/ppermute | solution.py:25
  42.6 4.8 %collective-permute-start.23 = (bf16[8,1792]{1,0:T(8,128)(2,1)S(1)}, bf16[8,1792]{1,0:T(8,128)(2,1)S(1)}, u32[]{:S(2)}, u32[]{:S(2)}) collective-permute-start(bf16[8,1792]{1,0:T(8,128)(2,1)S(1)} %get-tuple-element.41), channel_id=1, source_target_pairs={{0,1},{1,0},{2,3},{3,2},{4,5},{5,4},{6,7},{7,6},{8,9},{9,8},{10,11... | collective-permute-start | bytes 86024 | tf_op jit(solution)/shard_map/ppermute | solution.py:25

commit v6 on v5

--- a/solution.py
+++ b/solution.py
@@ -82,7 +82,7 @@
     parts = xs.shape[0] // rows
     expert = lax.axis_index("ep")
     gather_rows(arrays, xs)
-    step = min(256, columns)
+    step = columns
 
     def part(j, carry):
         at = pl.multiple_of(j * rows, rows)
@@ -183,9 +183,12 @@
     each = got[0].shape[0]
     for e in range(experts):
         rows[e * each:(e + 1) * each, :] = got[e][...]
+    tall = jnp.concatenate([w[...] for w in weights[::-1]], axis=0)
+    terms = jnp.dot(tall, rows[...], preferred_element_type=jnp.float32)
+    tokens = weights[0].shape[0]
     total = 0.0
-    for w in weights[::-1]:
-        total = total + jnp.dot(w[...], rows[...], preferred_element_type=jnp.float32)
+    for p in range(PIECES):
+        total = total + terms[p * tokens:(p + 1) * tokens]
     total = total.astype(jnp.bfloat16)
     for k in range(groups):
         outs[k][...] = total[k * count:(k + 1) * count, :]

time: 48.2 us -> 47.9 us (level)
  no operation moved by 1% of the time
where the time goes in v6:
time: 47.9 us; the launch traced here: 47.8 us
  starting transfers between devices  25.6 us (53%)
  waiting for transfers between devices  14.9 us (31%)
  Pallas kernels  7.09 us (15%)
    ppermute x24, starting transfers between devices, swap(): return lax.ppermute(x, axis, [(i, i ^ k) for i in range(size)])  25.6 us
    ppermute x24, waiting for transfers between devices, swap(): return lax.ppermute(x, axis, [(i, i ^ k) for i in range(size)])  14.9 us
    pallas_call x1, Pallas kernels, body(): pl.pallas_call(functools.partial(up_kernel, len(arrays), count, chosen, c...  2.32 us
    pallas_call x3, Pallas kernels, down(): pl.pallas_call(functools.partial(down_kernel, experts, which, last), out_...  1.64 us
    pallas_call x1, Pallas kernels, body(): pl.pallas_call(pack_kernel, out_shape=array(count, width + LANES), in_spe...  1.59 us
  transfers between devices with their start and end apart: 24, of which 16 were waited for; matrix products, arithmetic and copies ran while one was open for 0% of the time, Pallas kernels for 4%

profile of v6, /device:TPU:0, one launch (start us, length us, event | category | flops | bytes accessed | tf_op | source)
XLA Modules:
  0.0 47.8 jit_solution(17873884785551924536)
XLA Ops:
  0.0 1.6 %pack.1.refs_15_.refs_0_ = bf16[8,7296]{1,0:T(8,128)(2,1)} custom-call(bf16[8,7168]{1,0:T(8,128)(2,1)} %tokens.1, s32[2,8]{1,0:T(2,128)} %bitcast.8, f32[2,8]{1,0:T(2,128)} %bitcast.9), custom_call_target="tpu_custom_call" | custom-call | tf_op jit(solution)/shard_map/pack/pallas_call | solution.py:226
  1.6 3.1 %collective-permute-start.6 = (bf16[8,7296]{1,0:T(8,128)(2,1)}, bf16[8,7296]{1,0:T(8,128)(2,1)S(1)}, u32[]{:S(2)}, u32[]{:S(2)}) collective-permute-start(bf16[8,7296]{1,0:T(8,128)(2,1)} %pack.1.refs_15_.refs_0_), channel_id=1, source_target_pairs={{0,1},{1,0},{2,3},{3,2},{4,5},{5,4},{6,7},{7,6},{8,9},{9,8},{10,11... | collective-permute-start | bytes 350216 | tf_op jit(solution)/shard_map/ppermute | solution.py:25
  4.7 2.6 %collective-permute-start.3 = (bf16[8,7296]{1,0:T(8,128)(2,1)}, bf16[8,7296]{1,0:T(8,128)(2,1)S(1)}, u32[]{:S(2)}, u32[]{:S(2)}) collective-permute-start(bf16[8,7296]{1,0:T(8,128)(2,1)} %pack.1.refs_15_.refs_0_), channel_id=1, source_target_pairs={{0,2},{1,3},{2,0},{3,1},{4,6},{5,7},{6,4},{7,5},{8,10},{9,11},{10,... | collective-permute-start | bytes 350216 | tf_op jit(solution)/shard_map/ppermute | solution.py:25
  7.3 1.5 %collective-permute-start = (bf16[8,7296]{1,0:T(8,128)(2,1)}, bf16[8,7296]{1,0:T(8,128)(2,1)S(1)}, u32[]{:S(2)}, u32[]{:S(2)}) collective-permute-start(bf16[8,7296]{1,0:T(8,128)(2,1)} %pack.1.refs_15_.refs_0_), channel_id=1, source_target_pairs={{0,8},{4,12},{8,0},{12,4},{1,9},{5,13},{9,1},{13,5},{2,10},{6,14},... | collective-permute-start | bytes 350216 | tf_op jit(solution)/shard_map/ppermute | solution.py:25
  8.8 0.5 %collective-permute-done.6.x = bf16[8,7296]{1,0:T(8,128)(2,1)S(1)} collective-permute-done((bf16[8,7296]{1,0:T(8,128)(2,1)}, bf16[8,7296]{1,0:T(8,128)(2,1)S(1)}, u32[]{:S(2)}, u32[]{:S(2)}) %collective-permute-start.6) | collective-permute-done | bytes 116768 | tf_op jit(solution)/shard_map/ppermute | solution.py:25
  9.3 0.0 copy-start
  9.3 0.0 slice-start.3
  9.3 0.0 slice-start.5
  9.3 1.9 %collective-permute-start.7 = (bf16[8,7296]{1,0:T(8,128)(2,1)S(1)}, bf16[8,7296]{1,0:T(8,128)(2,1)S(1)}, u32[]{:S(2)}, u32[]{:S(2)}) collective-permute-start(bf16[8,7296]{1,0:T(8,128)(2,1)S(1)} %hold.3.refs_14_.refs_1_), channel_id=1, source_target_pairs={{0,8},{4,12},{8,0},{12,4},{1,9},{5,13},{9,1},{13,5},{2,10},{6,14},... | collective-permute-start | bytes 350216 | tf_op jit(solution)/shard_map/ppermute | solution.py:25
  11.3 1.8 %collective-permute-done.3.refs_13_.refs_2_ = bf16[8,7296]{1,0:T(8,128)(2,1)S(1)} collective-permute-done((bf16[8,7296]{1,0:T(8,128)(2,1)}, bf16[8,7296]{1,0:T(8,128)(2,1)S(1)}, u32[]{:S(2)}, u32[]{:S(2)}) %collective-permute-start.3) | collective-permute-done | bytes 116768 | tf_op jit(solution)/shard_map/ppermute | solution.py:25
  13.0 0.4 collective-permute-start.10
  13.4 0.0 collective-permute-done.x
  13.5 0.0 slice-start.1
  13.5 2.1 %collective-permute-start.1 = (bf16[8,7296]{1,0:T(8,128)(2,1)S(1)}, bf16[8,7296]{1,0:T(8,128)(2,1)S(1)}, u32[]{:S(2)}, u32[]{:S(2)}) collective-permute-start(bf16[8,7296]{1,0:T(8,128)(2,1)S(1)} %hold.2.refs_7_), channel_id=1, source_target_pairs={{0,3},{1,2},{2,1},{3,0},{4,7},{5,6},{6,5},{7,4},{8,11},{9,10},{10,... | collective-permute-start | bytes 350216 | tf_op jit(solution)/shard_map/ppermute | solution.py:25
  15.6 1.6 %collective-permute-start.4 = (bf16[8,7296]{1,0:T(8,128)(2,1)S(1)}, bf16[8,7296]{1,0:T(8,128)(2,1)S(1)}, u32[]{:S(2)}, u32[]{:S(2)}) collective-permute-start(bf16[8,7296]{1,0:T(8,128)(2,1)S(1)} %collective-permute-done.3.refs_13_.refs_2_), channel_id=1, source_target_pairs={{0,8},{4,12},{8,0},{12,4},{1,9},{5,13},{9,1},{13,5},{2,10},{6,14},... | collective-permute-start | bytes 350216 | tf_op jit(solution)/shard_map/ppermute | solution.py:25
  17.1 0.0 collective-permute-done.7.refs_6_
  17.1 0.0 collective-permute-start.12
  17.1 0.5 %collective-permute-start.13 = (bf16[8,7296]{1,0:T(8,128)(2,1)S(1)}, bf16[8,7296]{1,0:T(8,128)(2,1)S(1)}, u32[]{:S(2)}, u32[]{:S(2)}) collective-permute-start(bf16[8,7296]{1,0:T(8,128)(2,1)S(1)} %hold.3.refs_14_.refs_1_), channel_id=1, source_target_pairs={{0,4},{4,0},{8,12},{12,8},{1,5},{5,1},{9,13},{13,9},{2,6},{6,2},{1... | collective-permute-start | bytes 350216 | tf_op jit(solution)/shard_map/ppermute | solution.py:25
  17.7 1.4 %collective-permute-done.10.refs_12_.refs_3_ = bf16[8,7296]{1,0:T(8,128)(2,1)S(1)} collective-permute-done((bf16[8,7296]{1,0:T(8,128)(2,1)S(1)}, bf16[8,7296]{1,0:T(8,128)(2,1)S(1)}, u32[]{:S(2)}, u32[]{:S(2)}) %collective-permute-start.10) | collective-permute-done | bytes 116768 | tf_op jit(solution)/shard_map/ppermute | solution.py:25
  19.0 0.0 collective-permute-start.9
  19.0 1.4 %collective-permute-done.4.refs_5_ = bf16[8,7296]{1,0:T(8,128)(2,1)S(1)} collective-permute-done((bf16[8,7296]{1,0:T(8,128)(2,1)S(1)}, bf16[8,7296]{1,0:T(8,128)(2,1)S(1)}, u32[]{:S(2)}, u32[]{:S(2)}) %collective-permute-start.4) | collective-permute-done | bytes 116768 | tf_op jit(solution)/shard_map/ppermute | solution.py:25
  20.4 0.0 copy-done
  20.4 0.0 collective-permute-start.14
  20.4 0.0 collective-permute-done.1.refs_4_
  20.4 0.5 %collective-permute-start.8 = (bf16[8,7296]{1,0:T(8,128)(2,1)S(1)}, bf16[8,7296]{1,0:T(8,128)(2,1)S(1)}, u32[]{:S(2)}, u32[]{:S(2)}) collective-permute-start(bf16[8,7296]{1,0:T(8,128)(2,1)S(1)} %collective-permute-done.7.refs_6_), channel_id=1, source_target_pairs={{0,4},{4,0},{8,12},{12,8},{1,5},{5,1},{9,13},{13,9},{2,6},{6,2},{1... | collective-permute-start | bytes 350216 | tf_op jit(solution)/shard_map/ppermute | solution.py:25
  20.9 0.0 collective-permute-done.12.refs_9_
  20.9 0.1 collective-permute-start.11
  21.0 0.0 collective-permute-done.13.refs_10_
  21.0 0.4 collective-permute-start.5
  21.4 0.0 collective-permute-done.9.refs_3_
  21.4 0.1 collective-permute-start.2
  21.5 0.2 collective-permute-done.14.refs_11_
  21.7 0.2 collective-permute-done.8.refs_2_
  21.9 0.4 collective-permute-done.11.refs_8_
  22.2 0.2 collective-permute-done.5.refs_1_
  22.4 0.4 collective-permute-done.2.refs_0_
  22.8 0.0 slice-done.2
  22.8 0.0 slice-done.4
  22.8 0.0 slice-done.5
  22.8 2.3 %gate_up.1.refs_0_ = bf16[64,512]{1,0:T(8,128)(2,1)S(1)} custom-call(bf16[8,7296]{1,0:T(8,128)(2,1)S(1)} %collective-permute-done.2.refs_0_, bf16[8,7296]{1,0:T(8,128)(2,1)S(1)} %collective-permute-done.5.refs_1_, bf16[8,7296]{1,0:T(8,128)(2,1)S(1)} %collective-permute-done.8.refs_2_, bf16[8,7296]{1,0:T(8,128)(2,1)S(1)} %collective-permute-done.9.refs_3_, ...), custom_call_target="tpu_custom_call" | custom-call | tf_op jit(solution)/shard_map/gate_up/pallas_call | solution.py:280
  25.1 1.8 %collective-permute-start.16 = (bf16[64,512]{1,0:T(8,128)(2,1)S(1)}, bf16[64,512]{1,0:T(8,128)(2,1)S(1)}, u32[]{:S(2)}, u32[]{:S(2)}) collective-permute-start(bf16[64,512]{1,0:T(8,128)(2,1)S(1)} %gate_up.1.refs_0_), channel_id=1, source_target_pairs={{0,3},{1,2},{2,1},{3,0},{4,7},{5,6},{6,5},{7,4},{8,11},{9,10},{10,... | collective-permute-start | bytes 196616 | tf_op jit(solution)/shard_map/ppermute | solution.py:25
  26.9 0.2 collective-permute-start.17
  27.1 2.4 %collective-permute-start.15 = (bf16[64,512]{1,0:T(8,128)(2,1)S(1)}, bf16[64,512]{1,0:T(8,128)(2,1)S(1)}, u32[]{:S(2)}, u32[]{:S(2)}) collective-permute-start(bf16[64,512]{1,0:T(8,128)(2,1)S(1)} %gate_up.1.refs_0_), channel_id=1, source_target_pairs={{0,2},{1,3},{2,0},{3,1},{4,6},{5,7},{6,4},{7,5},{8,10},{9,11},{10,... | collective-permute-start | bytes 196616 | tf_op jit(solution)/shard_map/ppermute | solution.py:25
  29.5 0.6 %shares.1 = (bf16[32,64]{1,0:T(8,128)(2,1)S(1)}, bf16[32,64]{1,0:T(8,128)(2,1)S(1)}, bf16[32,64]{1,0:T(8,128)(2,1)S(1)}) custom-call(bf16[8,7296]{1,0:T(8,128)(2,1)S(1)} %copy-done, bf16[8,7296]{1,0:T(8,128)(2,1)S(1)} %hold.3.refs_14_.refs_1_, bf16[8,7296]{1,0:T(8,128)(2,1)S(1)} %collective-permute-done.3.refs_13_.refs_2_, ...), custom_call_target="tpu_custom_call" | custom-call | tf_op jit(solution)/shard_map/shares/pallas_call | solution.py:294
  30.2 0.5 down_0.1.refs_3_
  30.6 1.2 %collective-permute-done.16.refs_0_ = bf16[64,512]{1,0:T(8,128)(2,1)S(1)} collective-permute-done((bf16[64,512]{1,0:T(8,128)(2,1)S(1)}, bf16[64,512]{1,0:T(8,128)(2,1)S(1)}, u32[]{:S(2)}, u32[]{:S(2)}) %collective-permute-start.16) | collective-permute-done | bytes 65568 | tf_op jit(solution)/shard_map/ppermute | solution.py:25
  31.9 1.5 %collective-permute-done.17.refs_1_ = bf16[64,512]{1,0:T(8,128)(2,1)S(1)} collective-permute-done((bf16[64,512]{1,0:T(8,128)(2,1)S(1)}, bf16[64,512]{1,0:T(8,128)(2,1)S(1)}, u32[]{:S(2)}, u32[]{:S(2)}) %collective-permute-start.17) | collective-permute-done | bytes 65568 | tf_op jit(solution)/shard_map/ppermute | solution.py:25
  33.3 0.7 %down_3.1.refs_2_ = f32[64,1792]{1,0:T(8,128)S(1)} custom-call(bf16[64,512]{1,0:T(8,128)(2,1)S(1)} %collective-permute-done.16.refs_0_, bf16[64,512]{1,0:T(8,128)(2,1)S(1)} %collective-permute-done.17.refs_1_, bf16[1,2048,1792]{2,1,0:T(8,128)(2,1)S(1)} %bitcast.3, f32[64,1792]{1,0:T(8,128)S(1)} %down_0.1.refs_3_), custom_call_target="tpu_custom_call" | custom-call | tf_op jit(solution)/shard_map/down_3/pallas_call | solution.py:308
  34.1 0.1 collective-permute-done.15.refs_0_
  34.2 0.4 down_2.1
  34.6 0.1 collective-permute-start.18
  34.7 1.6 %collective-permute-start.19 = (bf16[16,1792]{1,0:T(8,128)(2,1)S(1)}, bf16[16,1792]{1,0:T(8,128)(2,1)S(1)}, u32[]{:S(2)}, u32[]{:S(2)}) collective-permute-start(bf16[16,1792]{1,0:T(8,128)(2,1)S(1)} %get-tuple-element.37), channel_id=1, source_target_pairs={{0,8},{4,12},{8,0},{12,4},{1,9},{5,13},{9,1},{13,5},{2,10},{6,14},... | collective-permute-start | bytes 172040 | tf_op jit(solution)/shard_map/ppermute | solution.py:25
  36.3 0.2 collective-permute-start.20
  36.5 0.0 collective-permute-done.18.refs_4_
  36.5 2.5 %collective-permute-done.19.refs_5_ = bf16[16,1792]{1,0:T(8,128)(2,1)S(1)} collective-permute-done((bf16[16,1792]{1,0:T(8,128)(2,1)S(1)}, bf16[16,1792]{1,0:T(8,128)(2,1)S(1)}, u32[]{:S(2)}, u32[]{:S(2)}) %collective-permute-start.19) | collective-permute-done | bytes 57376 | tf_op jit(solution)/shard_map/ppermute | solution.py:25
  39.0 1.2 %collective-permute-done.20.refs_6_ = bf16[16,1792]{1,0:T(8,128)(2,1)S(1)} collective-permute-done((bf16[16,1792]{1,0:T(8,128)(2,1)S(1)}, bf16[16,1792]{1,0:T(8,128)(2,1)S(1)}, u32[]{:S(2)}, u32[]{:S(2)}) %collective-permute-start.20) | collective-permute-done | bytes 57376 | tf_op jit(solution)/shard_map/ppermute | solution.py:25
  40.2 0.2 combine.1
  40.4 1.9 %collective-permute-start.21 = (bf16[8,1792]{1,0:T(8,128)(2,1)S(1)}, bf16[8,1792]{1,0:T(8,128)(2,1)S(1)}, u32[]{:S(2)}, u32[]{:S(2)}) collective-permute-start(bf16[8,1792]{1,0:T(8,128)(2,1)S(1)} %get-tuple-element.39), channel_id=1, source_target_pairs={{0,3},{1,2},{2,1},{3,0},{4,7},{5,6},{6,5},{7,4},{8,11},{9,10},{10,... | collective-permute-start | bytes 86024 | tf_op jit(solution)/shard_map/ppermute | solution.py:25
  42.3 0.0 collective-permute-start.22
  42.3 2.5 %collective-permute-start.23 = (bf16[8,1792]{1,0:T(8,128)(2,1)S(1)}, bf16[8,1792]{1,0:T(8,128)(2,1)S(1)}, u32[]{:S(2)}, u32[]{:S(2)}) collective-permute-start(bf16[8,1792]{1,0:T(8,128)(2,1)S(1)} %get-tuple-element.41), channel_id=1, source_target_pairs={{0,1},{1,0},{2,3},{3,2},{4,5},{5,4},{6,7},{7,6},{8,9},{9,8},{10,11... | collective-permute-start | bytes 86024 | tf_op jit(solution)/shard_map/ppermute | solution.py:25
  44.9 1.4 %collective-permute-done.21.refs_0_ = bf16[8,1792]{1,0:T(8,128)(2,1)S(1)} collective-permute-done((bf16[8,1792]{1,0:T(8,128)(2,1)S(1)}, bf16[8,1792]{1,0:T(8,128)(2,1)S(1)}, u32[]{:S(2)}, u32[]{:S(2)}) %collective-permute-start.21) | collective-permute-done | bytes 28704 | tf_op jit(solution)/shard_map/ppermute | solution.py:25
  46.2 0.9 %collective-permute-done.22.refs_1_ = bf16[8,1792]{1,0:T(8,128)(2,1)S(1)} collective-permute-done((bf16[8,1792]{1,0:T(8,128)(2,1)S(1)}, bf16[8,1792]{1,0:T(8,128)(2,1)S(1)}, u32[]{:S(2)}, u32[]{:S(2)}) %collective-permute-start.22) | collective-permute-done | bytes 28704 | tf_op jit(solution)/shard_map/ppermute | solution.py:25
  47.1 0.0 collective-permute-done.23.refs_2_
  47.1 0.7 %place.1 = bf16[8,7168]{1,0:T(8,128)(2,1)} custom-call(bf16[8,1792]{1,0:T(8,128)(2,1)S(1)} %collective-permute-done.21.refs_0_, bf16[8,1792]{1,0:T(8,128)(2,1)S(1)} %collective-permute-done.22.refs_1_, bf16[8,1792]{1,0:T(8,128)(2,1)S(1)} %collective-permute-done.23.refs_2_, bf16[8,1792]{1,0:T(8,128)(2,1)S(1)} %get-tuple-element.42.refs_3_), custom_call_target="tpu_custom_call" | custom-call | tf_op jit(solution)/shard_map/place/pallas_call | solution.py:335
  (11 shorter events, 0.0 us)
Async XLA Ops:
  1.6 7.7 %collective-permute-start.6 = (bf16[8,7296]{1,0:T(8,128)(2,1)}, bf16[8,7296]{1,0:T(8,128)(2,1)S(1)}, u32[]{:S(2)}, u32[]{:S(2)}) collective-permute-start(bf16[8,7296]{1,0:T(8,128)(2,1)} %pack.1.refs_15_.refs_0_), channel_id=1, source_target_pairs={{0,1},{1,0},{2,3},{3,2},{4,5},{5,4},{6,7},{7,6},{8,9},{9,8},{10,11... | collective-permute-start | bytes 350216 | tf_op jit(solution)/shard_map/ppermute | solution.py:25
  4.7 8.3 %collective-permute-start.3 = (bf16[8,7296]{1,0:T(8,128)(2,1)}, bf16[8,7296]{1,0:T(8,128)(2,1)S(1)}, u32[]{:S(2)}, u32[]{:S(2)}) collective-permute-start(bf16[8,7296]{1,0:T(8,128)(2,1)} %pack.1.refs_15_.refs_0_), channel_id=1, source_target_pairs={{0,2},{1,3},{2,0},{3,1},{4,6},{5,7},{6,4},{7,5},{8,10},{9,11},{10,... | collective-permute-start | bytes 350216 | tf_op jit(solution)/shard_map/ppermute | solution.py:25
  7.3 6.2 %collective-permute-start = (bf16[8,7296]{1,0:T(8,128)(2,1)}, bf16[8,7296]{1,0:T(8,128)(2,1)S(1)}, u32[]{:S(2)}, u32[]{:S(2)}) collective-permute-start(bf16[8,7296]{1,0:T(8,128)(2,1)} %pack.1.refs_15_.refs_0_), channel_id=1, source_target_pairs={{0,8},{4,12},{8,0},{12,4},{1,9},{5,13},{9,1},{13,5},{2,10},{6,14},... | collective-permute-start | bytes 350216 | tf_op jit(solution)/shard_map/ppermute | solution.py:25
  9.3 13.5 %slice-start.2 = ((s8[7340032]{0:T(1024)(128)(4,1)}), s8[4194304]{0:T(1024)(128)(4,1)S(1)}, s32[]{:S(2)}) async-start(s8[7340032]{0:T(1024)(128)(4,1)} %bitcast.4), calls=%async_computation.2 | async-start | bytes 8388608
  9.3 13.5 %slice-start.4 = ((s8[7340032]{0:T(1024)(128)(4,1)}), s8[4194304]{0:T(1024)(128)(4,1)S(1)}, s32[]{:S(2)}) async-start(s8[7340032]{0:T(1024)(128)(4,1)} %bitcast.6), calls=%async_computation.4 | async-start | bytes 8388608
  9.3 11.1 %copy-start = (bf16[8,7296]{1,0:T(8,128)(2,1)S(1)}, bf16[8,7296]{1,0:T(8,128)(2,1)}, u32[]{:S(2)}) copy-start(bf16[8,7296]{1,0:T(8,128)(2,1)} %pack.1.refs_15_.refs_0_) | copy-start | bytes 350212
  9.3 13.5 %slice-start.3 = ((s8[7340032]{0:T(1024)(128)(4,1)}), s8[3145728]{0:T(1024)(128)(4,1)S(1)}, s32[]{:S(2)}) async-start(s8[7340032]{0:T(1024)(128)(4,1)} %bitcast.4), calls=%async_computation.3 | async-start | bytes 6291456
  9.3 13.4 %slice-start.5 = ((s8[7340032]{0:T(1024)(128)(4,1)}), s8[3145728]{0:T(1024)(128)(4,1)S(1)}, s32[]{:S(2)}) async-start(s8[7340032]{0:T(1024)(128)(4,1)} %bitcast.6), calls=%async_computation.5 | async-start | bytes 6291456
  9.3 7.8 %collective-permute-start.7 = (bf16[8,7296]{1,0:T(8,128)(2,1)S(1)}, bf16[8,7296]{1,0:T(8,128)(2,1)S(1)}, u32[]{:S(2)}, u32[]{:S(2)}) collective-permute-start(bf16[8,7296]{1,0:T(8,128)(2,1)S(1)} %hold.3.refs_14_.refs_1_), channel_id=1, source_target_pairs={{0,8},{4,12},{8,0},{12,4},{1,9},{5,13},{9,1},{13,5},{2,10},{6,14},... | collective-permute-start | bytes 350216 | tf_op jit(solution)/shard_map/ppermute | solution.py:25
  13.0 6.0 %collective-permute-start.10 = (bf16[8,7296]{1,0:T(8,128)(2,1)S(1)}, bf16[8,7296]{1,0:T(8,128)(2,1)S(1)}, u32[]{:S(2)}, u32[]{:S(2)}) collective-permute-start(bf16[8,7296]{1,0:T(8,128)(2,1)S(1)} %collective-permute-done.3.refs_13_.refs_2_), channel_id=1, source_target_pairs={{0,1},{1,0},{2,3},{3,2},{4,5},{5,4},{6,7},{7,6},{8,9},{9,8},{10,11... | collective-permute-start | bytes 350216 | tf_op jit(solution)/shard_map/ppermute | solution.py:25
  13.4 16.7 %slice-start = ((s8[7340032]{0:T(1024)(128)(4,1)}), s8[4194304]{0:T(1024)(128)(4,1)S(1)}, s32[]{:S(2)}) async-start(s8[7340032]{0:T(1024)(128)(4,1)} %bitcast.2), calls=%async_computation | async-start | bytes 8388608
  13.5 16.7 %slice-start.1 = ((s8[7340032]{0:T(1024)(128)(4,1)}), s8[3145728]{0:T(1024)(128)(4,1)S(1)}, s32[]{:S(2)}) async-start(s8[7340032]{0:T(1024)(128)(4,1)} %bitcast.2), calls=%async_computation.1 | async-start | bytes 6291456
  13.5 6.9 %collective-permute-start.1 = (bf16[8,7296]{1,0:T(8,128)(2,1)S(1)}, bf16[8,7296]{1,0:T(8,128)(2,1)S(1)}, u32[]{:S(2)}, u32[]{:S(2)}) collective-permute-start(bf16[8,7296]{1,0:T(8,128)(2,1)S(1)} %hold.2.refs_7_), channel_id=1, source_target_pairs={{0,3},{1,2},{2,1},{3,0},{4,7},{5,6},{6,5},{7,4},{8,11},{9,10},{10,... | collective-permute-start | bytes 350216 | tf_op jit(solution)/shard_map/ppermute | solution.py:25
  15.6 4.8 %collective-permute-start.4 = (bf16[8,7296]{1,0:T(8,128)(2,1)S(1)}, bf16[8,7296]{1,0:T(8,128)(2,1)S(1)}, u32[]{:S(2)}, u32[]{:S(2)}) collective-permute-start(bf16[8,7296]{1,0:T(8,128)(2,1)S(1)} %collective-permute-done.3.refs_13_.refs_2_), channel_id=1, source_target_pairs={{0,8},{4,12},{8,0},{12,4},{1,9},{5,13},{9,1},{13,5},{2,10},{6,14},... | collective-permute-start | bytes 350216 | tf_op jit(solution)/shard_map/ppermute | solution.py:25
  17.1 3.8 %collective-permute-start.12 = (bf16[8,7296]{1,0:T(8,128)(2,1)S(1)}, bf16[8,7296]{1,0:T(8,128)(2,1)S(1)}, u32[]{:S(2)}, u32[]{:S(2)}) collective-permute-start(bf16[8,7296]{1,0:T(8,128)(2,1)S(1)} %collective-permute-done.3.refs_13_.refs_2_), channel_id=1, source_target_pairs={{0,4},{4,0},{8,12},{12,8},{1,5},{5,1},{9,13},{13,9},{2,6},{6,2},{1... | collective-permute-start | bytes 350216 | tf_op jit(solution)/shard_map/ppermute | solution.py:25
  17.1 3.8 %collective-permute-start.13 = (bf16[8,7296]{1,0:T(8,128)(2,1)S(1)}, bf16[8,7296]{1,0:T(8,128)(2,1)S(1)}, u32[]{:S(2)}, u32[]{:S(2)}) collective-permute-start(bf16[8,7296]{1,0:T(8,128)(2,1)S(1)} %hold.3.refs_14_.refs_1_), channel_id=1, source_target_pairs={{0,4},{4,0},{8,12},{12,8},{1,5},{5,1},{9,13},{13,9},{2,6},{6,2},{1... | collective-permute-start | bytes 350216 | tf_op jit(solution)/shard_map/ppermute | solution.py:25
  19.0 2.4 %collective-permute-start.9 = (bf16[8,7296]{1,0:T(8,128)(2,1)S(1)}, bf16[8,7296]{1,0:T(8,128)(2,1)S(1)}, u32[]{:S(2)}, u32[]{:S(2)}) collective-permute-start(bf16[8,7296]{1,0:T(8,128)(2,1)S(1)} %hold.2.refs_7_), channel_id=1, source_target_pairs={{0,4},{4,0},{8,12},{12,8},{1,5},{5,1},{9,13},{13,9},{2,6},{6,2},{1... | collective-permute-start | bytes 350216 | tf_op jit(solution)/shard_map/ppermute | solution.py:25
  20.4 1.3 %collective-permute-start.14 = (bf16[8,7296]{1,0:T(8,128)(2,1)S(1)}, bf16[8,7296]{1,0:T(8,128)(2,1)S(1)}, u32[]{:S(2)}, u32[]{:S(2)}) collective-permute-start(bf16[8,7296]{1,0:T(8,128)(2,1)S(1)} %copy-done), channel_id=1, source_target_pairs={{0,4},{4,0},{8,12},{12,8},{1,5},{5,1},{9,13},{13,9},{2,6},{6,2},{1... | collective-permute-start | bytes 350216 | tf_op jit(solution)/shard_map/ppermute | solution.py:25
  20.4 1.5 %collective-permute-start.8 = (bf16[8,7296]{1,0:T(8,128)(2,1)S(1)}, bf16[8,7296]{1,0:T(8,128)(2,1)S(1)}, u32[]{:S(2)}, u32[]{:S(2)}) collective-permute-start(bf16[8,7296]{1,0:T(8,128)(2,1)S(1)} %collective-permute-done.7.refs_6_), channel_id=1, source_target_pairs={{0,4},{4,0},{8,12},{12,8},{1,5},{5,1},{9,13},{13,9},{2,6},{6,2},{1... | collective-permute-start | bytes 350216 | tf_op jit(solution)/shard_map/ppermute | solution.py:25
  20.9 1.3 %collective-permute-start.11 = (bf16[8,7296]{1,0:T(8,128)(2,1)S(1)}, bf16[8,7296]{1,0:T(8,128)(2,1)S(1)}, u32[]{:S(2)}, u32[]{:S(2)}) collective-permute-start(bf16[8,7296]{1,0:T(8,128)(2,1)S(1)} %collective-permute-done.10.refs_12_.refs_3_), channel_id=1, source_target_pairs={{0,4},{4,0},{8,12},{12,8},{1,5},{5,1},{9,13},{13,9},{2,6},{6,2},{1... | collective-permute-start | bytes 350216 | tf_op jit(solution)/shard_map/ppermute | solution.py:25
  21.0 1.4 %collective-permute-start.5 = (bf16[8,7296]{1,0:T(8,128)(2,1)S(1)}, bf16[8,7296]{1,0:T(8,128)(2,1)S(1)}, u32[]{:S(2)}, u32[]{:S(2)}) collective-permute-start(bf16[8,7296]{1,0:T(8,128)(2,1)S(1)} %collective-permute-done.4.refs_5_), channel_id=1, source_target_pairs={{0,4},{4,0},{8,12},{12,8},{1,5},{5,1},{9,13},{13,9},{2,6},{6,2},{1... | collective-permute-start | bytes 350216 | tf_op jit(solution)/shard_map/ppermute | solution.py:25
  21.4 1.3 %collective-permute-start.2 = (bf16[8,7296]{1,0:T(8,128)(2,1)S(1)}, bf16[8,7296]{1,0:T(8,128)(2,1)S(1)}, u32[]{:S(2)}, u32[]{:S(2)}) collective-permute-start(bf16[8,7296]{1,0:T(8,128)(2,1)S(1)} %collective-permute-done.1.refs_4_), channel_id=1, source_target_pairs={{0,4},{4,0},{8,12},{12,8},{1,5},{5,1},{9,13},{13,9},{2,6},{6,2},{1... | collective-permute-start | bytes 350216 | tf_op jit(solution)/shard_map/ppermute | solution.py:25
  25.1 6.7 %collective-permute-start.16 = (bf16[64,512]{1,0:T(8,128)(2,1)S(1)}, bf16[64,512]{1,0:T(8,128)(2,1)S(1)}, u32[]{:S(2)}, u32[]{:S(2)}) collective-permute-start(bf16[64,512]{1,0:T(8,128)(2,1)S(1)} %gate_up.1.refs_0_), channel_id=1, source_target_pairs={{0,3},{1,2},{2,1},{3,0},{4,7},{5,6},{6,5},{7,4},{8,11},{9,10},{10,... | collective-permute-start | bytes 196616 | tf_op jit(solution)/shard_map/ppermute | solution.py:25
  26.9 6.4 %collective-permute-start.17 = (bf16[64,512]{1,0:T(8,128)(2,1)S(1)}, bf16[64,512]{1,0:T(8,128)(2,1)S(1)}, u32[]{:S(2)}, u32[]{:S(2)}) collective-permute-start(bf16[64,512]{1,0:T(8,128)(2,1)S(1)} %gate_up.1.refs_0_), channel_id=1, source_target_pairs={{0,1},{1,0},{2,3},{3,2},{4,5},{5,4},{6,7},{7,6},{8,9},{9,8},{10,11... | collective-permute-start | bytes 196616 | tf_op jit(solution)/shard_map/ppermute | solution.py:25
  27.1 7.0 %collective-permute-start.15 = (bf16[64,512]{1,0:T(8,128)(2,1)S(1)}, bf16[64,512]{1,0:T(8,128)(2,1)S(1)}, u32[]{:S(2)}, u32[]{:S(2)}) collective-permute-start(bf16[64,512]{1,0:T(8,128)(2,1)S(1)} %gate_up.1.refs_0_), channel_id=1, source_target_pairs={{0,2},{1,3},{2,0},{3,1},{4,6},{5,7},{6,4},{7,5},{8,10},{9,11},{10,... | collective-permute-start | bytes 196616 | tf_op jit(solution)/shard_map/ppermute | solution.py:25
  34.6 1.9 %collective-permute-start.18 = (bf16[16,1792]{1,0:T(8,128)(2,1)S(1)}, bf16[16,1792]{1,0:T(8,128)(2,1)S(1)}, u32[]{:S(2)}, u32[]{:S(2)}) collective-permute-start(bf16[16,1792]{1,0:T(8,128)(2,1)S(1)} %get-tuple-element.36), channel_id=1, source_target_pairs={{0,4},{4,0},{8,12},{12,8},{1,5},{5,1},{9,13},{13,9},{2,6},{6,2},{1... | collective-permute-start | bytes 172040 | tf_op jit(solution)/shard_map/ppermute | solution.py:25
  34.7 4.3 %collective-permute-start.19 = (bf16[16,1792]{1,0:T(8,128)(2,1)S(1)}, bf16[16,1792]{1,0:T(8,128)(2,1)S(1)}, u32[]{:S(2)}, u32[]{:S(2)}) collective-permute-start(bf16[16,1792]{1,0:T(8,128)(2,1)S(1)} %get-tuple-element.37), channel_id=1, source_target_pairs={{0,8},{4,12},{8,0},{12,4},{1,9},{5,13},{9,1},{13,5},{2,10},{6,14},... | collective-permute-start | bytes 172040 | tf_op jit(solution)/shard_map/ppermute | solution.py:25
  36.3 3.9 %collective-permute-start.20 = (bf16[16,1792]{1,0:T(8,128)(2,1)S(1)}, bf16[16,1792]{1,0:T(8,128)(2,1)S(1)}, u32[]{:S(2)}, u32[]{:S(2)}) collective-permute-start(bf16[16,1792]{1,0:T(8,128)(2,1)S(1)} %get-tuple-element.38), channel_id=1, source_target_pairs={{0,12},{4,8},{8,4},{12,0},{1,13},{5,9},{9,5},{13,1},{2,14},{6,10},... | collective-permute-start | bytes 172040 | tf_op jit(solution)/shard_map/ppermute | solution.py:25
  40.4 5.8 %collective-permute-start.21 = (bf16[8,1792]{1,0:T(8,128)(2,1)S(1)}, bf16[8,1792]{1,0:T(8,128)(2,1)S(1)}, u32[]{:S(2)}, u32[]{:S(2)}) collective-permute-start(bf16[8,1792]{1,0:T(8,128)(2,1)S(1)} %get-tuple-element.39), channel_id=1, source_target_pairs={{0,3},{1,2},{2,1},{3,0},{4,7},{5,6},{6,5},{7,4},{8,11},{9,10},{10,... | collective-permute-start | bytes 86024 | tf_op jit(solution)/shard_map/ppermute | solution.py:25
  42.3 4.8 %collective-permute-start.22 = (bf16[8,1792]{1,0:T(8,128)(2,1)S(1)}, bf16[8,1792]{1,0:T(8,128)(2,1)S(1)}, u32[]{:S(2)}, u32[]{:S(2)}) collective-permute-start(bf16[8,1792]{1,0:T(8,128)(2,1)S(1)} %get-tuple-element.40), channel_id=1, source_target_pairs={{0,2},{1,3},{2,0},{3,1},{4,6},{5,7},{6,4},{7,5},{8,10},{9,11},{10,... | collective-permute-start | bytes 86024 | tf_op jit(solution)/shard_map/ppermute | solution.py:25
  42.3 4.8 %collective-permute-start.23 = (bf16[8,1792]{1,0:T(8,128)(2,1)S(1)}, bf16[8,1792]{1,0:T(8,128)(2,1)S(1)}, u32[]{:S(2)}, u32[]{:S(2)}) collective-permute-start(bf16[8,1792]{1,0:T(8,128)(2,1)S(1)} %get-tuple-element.41), channel_id=1, source_target_pairs={{0,1},{1,0},{2,3},{3,2},{4,5},{5,4},{6,7},{7,6},{8,9},{9,8},{10,11... | collective-permute-start | bytes 86024 | tf_op jit(solution)/shard_map/ppermute | solution.py:25

commit v7 on v6

--- a/solution.py
+++ b/solution.py
@@ -255,8 +255,8 @@
         got[kz, 0] = swap(own, "sub", groups, kz)
     for ky in far:
         got[0, ky] = swap(own, "ep", experts, ky)
+    got[1, 0] = hold(got[1, 0])
     got[0, 2] = hold(got[0, 2])
-    got[1, 0] = hold(got[1, 0])
     relayed = [kz for kz in range(1, groups) if kz not in single]
     for kz in relayed:
         for ky in far:

time: 47.9 us -> 47.9 us (level)
  no operation moved by 1% of the time
where the time goes in v7:
time: 47.9 us; the launch traced here: 47.8 us
  starting transfers between devices  25.6 us (53%)
  waiting for transfers between devices  14.9 us (31%)
  Pallas kernels  7.09 us (15%)
    ppermute x24, starting transfers between devices, swap(): return lax.ppermute(x, axis, [(i, i ^ k) for i in range(size)])  25.6 us
    ppermute x24, waiting for transfers between devices, swap(): return lax.ppermute(x, axis, [(i, i ^ k) for i in range(size)])  14.9 us
    pallas_call x1, Pallas kernels, body(): pl.pallas_call(functools.partial(up_kernel, len(arrays), count, chosen, c...  2.32 us
    pallas_call x3, Pallas kernels, down(): pl.pallas_call(functools.partial(down_kernel, experts, which, last), out_...  1.64 us
    pallas_call x1, Pallas kernels, body(): pl.pallas_call(pack_kernel, out_shape=array(count, width + LANES), in_spe...  1.59 us
  transfers between devices with their start and end apart: 24, of which 16 were waited for; matrix products, arithmetic and copies ran while one was open for 0% of the time, Pallas kernels for 4%

profile of v7, /device:TPU:0, one launch (start us, length us, event | category | flops | bytes accessed | tf_op | source)
XLA Modules:
  0.0 47.8 jit_solution(17873884785551924536)
XLA Ops:
  0.0 1.6 %pack.1.refs_15_.refs_0_ = bf16[8,7296]{1,0:T(8,128)(2,1)} custom-call(bf16[8,7168]{1,0:T(8,128)(2,1)} %tokens.1, s32[2,8]{1,0:T(2,128)} %bitcast.8, f32[2,8]{1,0:T(2,128)} %bitcast.9), custom_call_target="tpu_custom_call" | custom-call | tf_op jit(solution)/shard_map/pack/pallas_call | solution.py:226
  1.6 3.1 %collective-permute-start.6 = (bf16[8,7296]{1,0:T(8,128)(2,1)}, bf16[8,7296]{1,0:T(8,128)(2,1)S(1)}, u32[]{:S(2)}, u32[]{:S(2)}) collective-permute-start(bf16[8,7296]{1,0:T(8,128)(2,1)} %pack.1.refs_15_.refs_0_), channel_id=1, source_target_pairs={{0,1},{1,0},{2,3},{3,2},{4,5},{5,4},{6,7},{7,6},{8,9},{9,8},{10,11... | collective-permute-start | bytes 350216 | tf_op jit(solution)/shard_map/ppermute | solution.py:25
  4.7 2.6 %collective-permute-start.3 = (bf16[8,7296]{1,0:T(8,128)(2,1)}, bf16[8,7296]{1,0:T(8,128)(2,1)S(1)}, u32[]{:S(2)}, u32[]{:S(2)}) collective-permute-start(bf16[8,7296]{1,0:T(8,128)(2,1)} %pack.1.refs_15_.refs_0_), channel_id=1, source_target_pairs={{0,2},{1,3},{2,0},{3,1},{4,6},{5,7},{6,4},{7,5},{8,10},{9,11},{10,... | collective-permute-start | bytes 350216 | tf_op jit(solution)/shard_map/ppermute | solution.py:25
  7.3 1.5 %collective-permute-start = (bf16[8,7296]{1,0:T(8,128)(2,1)}, bf16[8,7296]{1,0:T(8,128)(2,1)S(1)}, u32[]{:S(2)}, u32[]{:S(2)}) collective-permute-start(bf16[8,7296]{1,0:T(8,128)(2,1)} %pack.1.refs_15_.refs_0_), channel_id=1, source_target_pairs={{0,8},{4,12},{8,0},{12,4},{1,9},{5,13},{9,1},{13,5},{2,10},{6,14},... | collective-permute-start | bytes 350216 | tf_op jit(solution)/shard_map/ppermute | solution.py:25
  8.8 0.5 %collective-permute-done.6.x = bf16[8,7296]{1,0:T(8,128)(2,1)S(1)} collective-permute-done((bf16[8,7296]{1,0:T(8,128)(2,1)}, bf16[8,7296]{1,0:T(8,128)(2,1)S(1)}, u32[]{:S(2)}, u32[]{:S(2)}) %collective-permute-start.6) | collective-permute-done | bytes 116768 | tf_op jit(solution)/shard_map/ppermute | solution.py:25
  9.3 0.0 copy-start
  9.3 0.0 slice-start.3
  9.3 0.0 slice-start.5
  9.3 1.9 %collective-permute-start.7 = (bf16[8,7296]{1,0:T(8,128)(2,1)S(1)}, bf16[8,7296]{1,0:T(8,128)(2,1)S(1)}, u32[]{:S(2)}, u32[]{:S(2)}) collective-permute-start(bf16[8,7296]{1,0:T(8,128)(2,1)S(1)} %hold.3.refs_14_.refs_1_), channel_id=1, source_target_pairs={{0,8},{4,12},{8,0},{12,4},{1,9},{5,13},{9,1},{13,5},{2,10},{6,14},... | collective-permute-start | bytes 350216 | tf_op jit(solution)/shard_map/ppermute | solution.py:25
  11.3 1.8 %collective-permute-done.3.refs_13_.refs_2_ = bf16[8,7296]{1,0:T(8,128)(2,1)S(1)} collective-permute-done((bf16[8,7296]{1,0:T(8,128)(2,1)}, bf16[8,7296]{1,0:T(8,128)(2,1)S(1)}, u32[]{:S(2)}, u32[]{:S(2)}) %collective-permute-start.3) | collective-permute-done | bytes 116768 | tf_op jit(solution)/shard_map/ppermute | solution.py:25
  13.0 0.4 collective-permute-start.10
  13.4 0.0 collective-permute-done.x
  13.5 0.0 slice-start.1
  13.5 2.1 %collective-permute-start.1 = (bf16[8,7296]{1,0:T(8,128)(2,1)S(1)}, bf16[8,7296]{1,0:T(8,128)(2,1)S(1)}, u32[]{:S(2)}, u32[]{:S(2)}) collective-permute-start(bf16[8,7296]{1,0:T(8,128)(2,1)S(1)} %hold.2.refs_7_), channel_id=1, source_target_pairs={{0,3},{1,2},{2,1},{3,0},{4,7},{5,6},{6,5},{7,4},{8,11},{9,10},{10,... | collective-permute-start | bytes 350216 | tf_op jit(solution)/shard_map/ppermute | solution.py:25
  15.6 1.6 %collective-permute-start.4 = (bf16[8,7296]{1,0:T(8,128)(2,1)S(1)}, bf16[8,7296]{1,0:T(8,128)(2,1)S(1)}, u32[]{:S(2)}, u32[]{:S(2)}) collective-permute-start(bf16[8,7296]{1,0:T(8,128)(2,1)S(1)} %collective-permute-done.3.refs_13_.refs_2_), channel_id=1, source_target_pairs={{0,8},{4,12},{8,0},{12,4},{1,9},{5,13},{9,1},{13,5},{2,10},{6,14},... | collective-permute-start | bytes 350216 | tf_op jit(solution)/shard_map/ppermute | solution.py:25
  17.1 0.0 collective-permute-done.7.refs_6_
  17.1 0.0 collective-permute-start.12
  17.1 0.5 %collective-permute-start.13 = (bf16[8,7296]{1,0:T(8,128)(2,1)S(1)}, bf16[8,7296]{1,0:T(8,128)(2,1)S(1)}, u32[]{:S(2)}, u32[]{:S(2)}) collective-permute-start(bf16[8,7296]{1,0:T(8,128)(2,1)S(1)} %hold.3.refs_14_.refs_1_), channel_id=1, source_target_pairs={{0,4},{4,0},{8,12},{12,8},{1,5},{5,1},{9,13},{13,9},{2,6},{6,2},{1... | collective-permute-start | bytes 350216 | tf_op jit(solution)/shard_map/ppermute | solution.py:25
  17.7 1.4 %collective-permute-done.10.refs_12_.refs_3_ = bf16[8,7296]{1,0:T(8,128)(2,1)S(1)} collective-permute-done((bf16[8,7296]{1,0:T(8,128)(2,1)S(1)}, bf16[8,7296]{1,0:T(8,128)(2,1)S(1)}, u32[]{:S(2)}, u32[]{:S(2)}) %collective-permute-start.10) | collective-permute-done | bytes 116768 | tf_op jit(solution)/shard_map/ppermute | solution.py:25
  19.0 0.0 collective-permute-start.9
  19.0 1.4 %collective-permute-done.4.refs_5_ = bf16[8,7296]{1,0:T(8,128)(2,1)S(1)} collective-permute-done((bf16[8,7296]{1,0:T(8,128)(2,1)S(1)}, bf16[8,7296]{1,0:T(8,128)(2,1)S(1)}, u32[]{:S(2)}, u32[]{:S(2)}) %collective-permute-start.4) | collective-permute-done | bytes 116768 | tf_op jit(solution)/shard_map/ppermute | solution.py:25
  20.4 0.0 copy-done
  20.4 0.0 collective-permute-start.14
  20.4 0.0 collective-permute-done.1.refs_4_
  20.4 0.5 %collective-permute-start.8 = (bf16[8,7296]{1,0:T(8,128)(2,1)S(1)}, bf16[8,7296]{1,0:T(8,128)(2,1)S(1)}, u32[]{:S(2)}, u32[]{:S(2)}) collective-permute-start(bf16[8,7296]{1,0:T(8,128)(2,1)S(1)} %collective-permute-done.7.refs_6_), channel_id=1, source_target_pairs={{0,4},{4,0},{8,12},{12,8},{1,5},{5,1},{9,13},{13,9},{2,6},{6,2},{1... | collective-permute-start | bytes 350216 | tf_op jit(solution)/shard_map/ppermute | solution.py:25
  20.9 0.0 collective-permute-done.12.refs_9_
  20.9 0.1 collective-permute-start.11
  21.0 0.0 collective-permute-done.13.refs_10_
  21.0 0.4 collective-permute-start.5
  21.4 0.0 collective-permute-done.9.refs_3_
  21.4 0.1 collective-permute-start.2
  21.5 0.2 collective-permute-done.14.refs_11_
  21.7 0.2 collective-permute-done.8.refs_2_
  21.9 0.4 collective-permute-done.11.refs_8_
  22.2 0.2 collective-permute-done.5.refs_1_
  22.4 0.4 collective-permute-done.2.refs_0_
  22.8 0.0 slice-done.2
  22.8 0.0 slice-done.4
  22.8 0.0 slice-done.5
  22.8 2.3 %gate_up.1.refs_0_ = bf16[64,512]{1,0:T(8,128)(2,1)S(1)} custom-call(bf16[8,7296]{1,0:T(8,128)(2,1)S(1)} %collective-permute-done.2.refs_0_, bf16[8,7296]{1,0:T(8,128)(2,1)S(1)} %collective-permute-done.5.refs_1_, bf16[8,7296]{1,0:T(8,128)(2,1)S(1)} %collective-permute-done.8.refs_2_, bf16[8,7296]{1,0:T(8,128)(2,1)S(1)} %collective-permute-done.9.refs_3_, ...), custom_call_target="tpu_custom_call" | custom-call | tf_op jit(solution)/shard_map/gate_up/pallas_call | solution.py:280
  25.1 1.8 %collective-permute-start.16 = (bf16[64,512]{1,0:T(8,128)(2,1)S(1)}, bf16[64,512]{1,0:T(8,128)(2,1)S(1)}, u32[]{:S(2)}, u32[]{:S(2)}) collective-permute-start(bf16[64,512]{1,0:T(8,128)(2,1)S(1)} %gate_up.1.refs_0_), channel_id=1, source_target_pairs={{0,3},{1,2},{2,1},{3,0},{4,7},{5,6},{6,5},{7,4},{8,11},{9,10},{10,... | collective-permute-start | bytes 196616 | tf_op jit(solution)/shard_map/ppermute | solution.py:25
  26.9 0.2 collective-permute-start.17
  27.1 2.4 %collective-permute-start.15 = (bf16[64,512]{1,0:T(8,128)(2,1)S(1)}, bf16[64,512]{1,0:T(8,128)(2,1)S(1)}, u32[]{:S(2)}, u32[]{:S(2)}) collective-permute-start(bf16[64,512]{1,0:T(8,128)(2,1)S(1)} %gate_up.1.refs_0_), channel_id=1, source_target_pairs={{0,2},{1,3},{2,0},{3,1},{4,6},{5,7},{6,4},{7,5},{8,10},{9,11},{10,... | collective-permute-start | bytes 196616 | tf_op jit(solution)/shard_map/ppermute | solution.py:25
  29.5 0.6 %shares.1 = (bf16[32,64]{1,0:T(8,128)(2,1)S(1)}, bf16[32,64]{1,0:T(8,128)(2,1)S(1)}, bf16[32,64]{1,0:T(8,128)(2,1)S(1)}) custom-call(bf16[8,7296]{1,0:T(8,128)(2,1)S(1)} %copy-done, bf16[8,7296]{1,0:T(8,128)(2,1)S(1)} %hold.3.refs_14_.refs_1_, bf16[8,7296]{1,0:T(8,128)(2,1)S(1)} %collective-permute-done.3.refs_13_.refs_2_, ...), custom_call_target="tpu_custom_call" | custom-call | tf_op jit(solution)/shard_map/shares/pallas_call | solution.py:294
  30.2 0.5 down_0.1.refs_3_
  30.6 1.2 %collective-permute-done.16.refs_0_ = bf16[64,512]{1,0:T(8,128)(2,1)S(1)} collective-permute-done((bf16[64,512]{1,0:T(8,128)(2,1)S(1)}, bf16[64,512]{1,0:T(8,128)(2,1)S(1)}, u32[]{:S(2)}, u32[]{:S(2)}) %collective-permute-start.16) | collective-permute-done | bytes 65568 | tf_op jit(solution)/shard_map/ppermute | solution.py:25
  31.9 1.5 %collective-permute-done.17.refs_1_ = bf16[64,512]{1,0:T(8,128)(2,1)S(1)} collective-permute-done((bf16[64,512]{1,0:T(8,128)(2,1)S(1)}, bf16[64,512]{1,0:T(8,128)(2,1)S(1)}, u32[]{:S(2)}, u32[]{:S(2)}) %collective-permute-start.17) | collective-permute-done | bytes 65568 | tf_op jit(solution)/shard_map/ppermute | solution.py:25
  33.3 0.7 %down_3.1.refs_2_ = f32[64,1792]{1,0:T(8,128)S(1)} custom-call(bf16[64,512]{1,0:T(8,128)(2,1)S(1)} %collective-permute-done.16.refs_0_, bf16[64,512]{1,0:T(8,128)(2,1)S(1)} %collective-permute-done.17.refs_1_, bf16[1,2048,1792]{2,1,0:T(8,128)(2,1)S(1)} %bitcast.3, f32[64,1792]{1,0:T(8,128)S(1)} %down_0.1.refs_3_), custom_call_target="tpu_custom_call" | custom-call | tf_op jit(solution)/shard_map/down_3/pallas_call | solution.py:308
  34.1 0.1 collective-permute-done.15.refs_0_
  34.2 0.4 down_2.1
  34.6 0.1 collective-permute-start.18
  34.7 1.6 %collective-permute-start.19 = (bf16[16,1792]{1,0:T(8,128)(2,1)S(1)}, bf16[16,1792]{1,0:T(8,128)(2,1)S(1)}, u32[]{:S(2)}, u32[]{:S(2)}) collective-permute-start(bf16[16,1792]{1,0:T(8,128)(2,1)S(1)} %get-tuple-element.37), channel_id=1, source_target_pairs={{0,8},{4,12},{8,0},{12,4},{1,9},{5,13},{9,1},{13,5},{2,10},{6,14},... | collective-permute-start | bytes 172040 | tf_op jit(solution)/shard_map/ppermute | solution.py:25
  36.3 0.2 collective-permute-start.20
  36.5 0.0 collective-permute-done.18.refs_4_
  36.5 2.5 %collective-permute-done.19.refs_5_ = bf16[16,1792]{1,0:T(8,128)(2,1)S(1)} collective-permute-done((bf16[16,1792]{1,0:T(8,128)(2,1)S(1)}, bf16[16,1792]{1,0:T(8,128)(2,1)S(1)}, u32[]{:S(2)}, u32[]{:S(2)}) %collective-permute-start.19) | collective-permute-done | bytes 57376 | tf_op jit(solution)/shard_map/ppermute | solution.py:25
  39.0 1.2 %collective-permute-done.20.refs_6_ = bf16[16,1792]{1,0:T(8,128)(2,1)S(1)} collective-permute-done((bf16[16,1792]{1,0:T(8,128)(2,1)S(1)}, bf16[16,1792]{1,0:T(8,128)(2,1)S(1)}, u32[]{:S(2)}, u32[]{:S(2)}) %collective-permute-start.20) | collective-permute-done | bytes 57376 | tf_op jit(solution)/shard_map/ppermute | solution.py:25
  40.2 0.2 combine.1
  40.4 1.9 %collective-permute-start.21 = (bf16[8,1792]{1,0:T(8,128)(2,1)S(1)}, bf16[8,1792]{1,0:T(8,128)(2,1)S(1)}, u32[]{:S(2)}, u32[]{:S(2)}) collective-permute-start(bf16[8,1792]{1,0:T(8,128)(2,1)S(1)} %get-tuple-element.39), channel_id=1, source_target_pairs={{0,3},{1,2},{2,1},{3,0},{4,7},{5,6},{6,5},{7,4},{8,11},{9,10},{10,... | collective-permute-start | bytes 86024 | tf_op jit(solution)/shard_map/ppermute | solution.py:25
  42.3 0.0 collective-permute-start.22
  42.3 2.5 %collective-permute-start.23 = (bf16[8,1792]{1,0:T(8,128)(2,1)S(1)}, bf16[8,1792]{1,0:T(8,128)(2,1)S(1)}, u32[]{:S(2)}, u32[]{:S(2)}) collective-permute-start(bf16[8,1792]{1,0:T(8,128)(2,1)S(1)} %get-tuple-element.41), channel_id=1, source_target_pairs={{0,1},{1,0},{2,3},{3,2},{4,5},{5,4},{6,7},{7,6},{8,9},{9,8},{10,11... | collective-permute-start | bytes 86024 | tf_op jit(solution)/shard_map/ppermute | solution.py:25
  44.9 1.4 %collective-permute-done.21.refs_0_ = bf16[8,1792]{1,0:T(8,128)(2,1)S(1)} collective-permute-done((bf16[8,1792]{1,0:T(8,128)(2,1)S(1)}, bf16[8,1792]{1,0:T(8,128)(2,1)S(1)}, u32[]{:S(2)}, u32[]{:S(2)}) %collective-permute-start.21) | collective-permute-done | bytes 28704 | tf_op jit(solution)/shard_map/ppermute | solution.py:25
  46.2 0.9 %collective-permute-done.22.refs_1_ = bf16[8,1792]{1,0:T(8,128)(2,1)S(1)} collective-permute-done((bf16[8,1792]{1,0:T(8,128)(2,1)S(1)}, bf16[8,1792]{1,0:T(8,128)(2,1)S(1)}, u32[]{:S(2)}, u32[]{:S(2)}) %collective-permute-start.22) | collective-permute-done | bytes 28704 | tf_op jit(solution)/shard_map/ppermute | solution.py:25
  47.1 0.0 collective-permute-done.23.refs_2_
  47.1 0.7 %place.1 = bf16[8,7168]{1,0:T(8,128)(2,1)} custom-call(bf16[8,1792]{1,0:T(8,128)(2,1)S(1)} %collective-permute-done.21.refs_0_, bf16[8,1792]{1,0:T(8,128)(2,1)S(1)} %collective-permute-done.22.refs_1_, bf16[8,1792]{1,0:T(8,128)(2,1)S(1)} %collective-permute-done.23.refs_2_, bf16[8,1792]{1,0:T(8,128)(2,1)S(1)} %get-tuple-element.42.refs_3_), custom_call_target="tpu_custom_call" | custom-call | tf_op jit(solution)/shard_map/place/pallas_call | solution.py:335
  (11 shorter events, 0.0 us)
Async XLA Ops:
  1.6 7.7 %collective-permute-start.6 = (bf16[8,7296]{1,0:T(8,128)(2,1)}, bf16[8,7296]{1,0:T(8,128)(2,1)S(1)}, u32[]{:S(2)}, u32[]{:S(2)}) collective-permute-start(bf16[8,7296]{1,0:T(8,128)(2,1)} %pack.1.refs_15_.refs_0_), channel_id=1, source_target_pairs={{0,1},{1,0},{2,3},{3,2},{4,5},{5,4},{6,7},{7,6},{8,9},{9,8},{10,11... | collective-permute-start | bytes 350216 | tf_op jit(solution)/shard_map/ppermute | solution.py:25
  4.7 8.3 %collective-permute-start.3 = (bf16[8,7296]{1,0:T(8,128)(2,1)}, bf16[8,7296]{1,0:T(8,128)(2,1)S(1)}, u32[]{:S(2)}, u32[]{:S(2)}) collective-permute-start(bf16[8,7296]{1,0:T(8,128)(2,1)} %pack.1.refs_15_.refs_0_), channel_id=1, source_target_pairs={{0,2},{1,3},{2,0},{3,1},{4,6},{5,7},{6,4},{7,5},{8,10},{9,11},{10,... | collective-permute-start | bytes 350216 | tf_op jit(solution)/shard_map/ppermute | solution.py:25
  7.3 6.2 %collective-permute-start = (bf16[8,7296]{1,0:T(8,128)(2,1)}, bf16[8,7296]{1,0:T(8,128)(2,1)S(1)}, u32[]{:S(2)}, u32[]{:S(2)}) collective-permute-start(bf16[8,7296]{1,0:T(8,128)(2,1)} %pack.1.refs_15_.refs_0_), channel_id=1, source_target_pairs={{0,8},{4,12},{8,0},{12,4},{1,9},{5,13},{9,1},{13,5},{2,10},{6,14},... | collective-permute-start | bytes 350216 | tf_op jit(solution)/shard_map/ppermute | solution.py:25
  9.3 13.5 %slice-start.2 = ((s8[7340032]{0:T(1024)(128)(4,1)}), s8[4194304]{0:T(1024)(128)(4,1)S(1)}, s32[]{:S(2)}) async-start(s8[7340032]{0:T(1024)(128)(4,1)} %bitcast.4), calls=%async_computation.2 | async-start | bytes 8388608
  9.3 13.5 %slice-start.4 = ((s8[7340032]{0:T(1024)(128)(4,1)}), s8[4194304]{0:T(1024)(128)(4,1)S(1)}, s32[]{:S(2)}) async-start(s8[7340032]{0:T(1024)(128)(4,1)} %bitcast.6), calls=%async_computation.4 | async-start | bytes 8388608
  9.3 11.1 %copy-start = (bf16[8,7296]{1,0:T(8,128)(2,1)S(1)}, bf16[8,7296]{1,0:T(8,128)(2,1)}, u32[]{:S(2)}) copy-start(bf16[8,7296]{1,0:T(8,128)(2,1)} %pack.1.refs_15_.refs_0_) | copy-start | bytes 350212
  9.3 13.5 %slice-start.3 = ((s8[7340032]{0:T(1024)(128)(4,1)}), s8[3145728]{0:T(1024)(128)(4,1)S(1)}, s32[]{:S(2)}) async-start(s8[7340032]{0:T(1024)(128)(4,1)} %bitcast.4), calls=%async_computation.3 | async-start | bytes 6291456
  9.3 13.4 %slice-start.5 = ((s8[7340032]{0:T(1024)(128)(4,1)}), s8[3145728]{0:T(1024)(128)(4,1)S(1)}, s32[]{:S(2)}) async-start(s8[7340032]{0:T(1024)(128)(4,1)} %bitcast.6), calls=%async_computation.5 | async-start | bytes 6291456
  9.3 7.8 %collective-permute-start.7 = (bf16[8,7296]{1,0:T(8,128)(2,1)S(1)}, bf16[8,7296]{1,0:T(8,128)(2,1)S(1)}, u32[]{:S(2)}, u32[]{:S(2)}) collective-permute-start(bf16[8,7296]{1,0:T(8,128)(2,1)S(1)} %hold.3.refs_14_.refs_1_), channel_id=1, source_target_pairs={{0,8},{4,12},{8,0},{12,4},{1,9},{5,13},{9,1},{13,5},{2,10},{6,14},... | collective-permute-start | bytes 350216 | tf_op jit(solution)/shard_map/ppermute | solution.py:25
  13.0 6.0 %collective-permute-start.10 = (bf16[8,7296]{1,0:T(8,128)(2,1)S(1)}, bf16[8,7296]{1,0:T(8,128)(2,1)S(1)}, u32[]{:S(2)}, u32[]{:S(2)}) collective-permute-start(bf16[8,7296]{1,0:T(8,128)(2,1)S(1)} %collective-permute-done.3.refs_13_.refs_2_), channel_id=1, source_target_pairs={{0,1},{1,0},{2,3},{3,2},{4,5},{5,4},{6,7},{7,6},{8,9},{9,8},{10,11... | collective-permute-start | bytes 350216 | tf_op jit(solution)/shard_map/ppermute | solution.py:25
  13.4 16.7 %slice-start = ((s8[7340032]{0:T(1024)(128)(4,1)}), s8[4194304]{0:T(1024)(128)(4,1)S(1)}, s32[]{:S(2)}) async-start(s8[7340032]{0:T(1024)(128)(4,1)} %bitcast.2), calls=%async_computation | async-start | bytes 8388608
  13.5 16.7 %slice-start.1 = ((s8[7340032]{0:T(1024)(128)(4,1)}), s8[3145728]{0:T(1024)(128)(4,1)S(1)}, s32[]{:S(2)}) async-start(s8[7340032]{0:T(1024)(128)(4,1)} %bitcast.2), calls=%async_computation.1 | async-start | bytes 6291456
  13.5 6.9 %collective-permute-start.1 = (bf16[8,7296]{1,0:T(8,128)(2,1)S(1)}, bf16[8,7296]{1,0:T(8,128)(2,1)S(1)}, u32[]{:S(2)}, u32[]{:S(2)}) collective-permute-start(bf16[8,7296]{1,0:T(8,128)(2,1)S(1)} %hold.2.refs_7_), channel_id=1, source_target_pairs={{0,3},{1,2},{2,1},{3,0},{4,7},{5,6},{6,5},{7,4},{8,11},{9,10},{10,... | collective-permute-start | bytes 350216 | tf_op jit(solution)/shard_map/ppermute | solution.py:25
  15.6 4.8 %collective-permute-start.4 = (bf16[8,7296]{1,0:T(8,128)(2,1)S(1)}, bf16[8,7296]{1,0:T(8,128)(2,1)S(1)}, u32[]{:S(2)}, u32[]{:S(2)}) collective-permute-start(bf16[8,7296]{1,0:T(8,128)(2,1)S(1)} %collective-permute-done.3.refs_13_.refs_2_), channel_id=1, source_target_pairs={{0,8},{4,12},{8,0},{12,4},{1,9},{5,13},{9,1},{13,5},{2,10},{6,14},... | collective-permute-start | bytes 350216 | tf_op jit(solution)/shard_map/ppermute | solution.py:25
  17.1 3.8 %collective-permute-start.12 = (bf16[8,7296]{1,0:T(8,128)(2,1)S(1)}, bf16[8,7296]{1,0:T(8,128)(2,1)S(1)}, u32[]{:S(2)}, u32[]{:S(2)}) collective-permute-start(bf16[8,7296]{1,0:T(8,128)(2,1)S(1)} %collective-permute-done.3.refs_13_.refs_2_), channel_id=1, source_target_pairs={{0,4},{4,0},{8,12},{12,8},{1,5},{5,1},{9,13},{13,9},{2,6},{6,2},{1... | collective-permute-start | bytes 350216 | tf_op jit(solution)/shard_map/ppermute | solution.py:25
  17.1 3.8 %collective-permute-start.13 = (bf16[8,7296]{1,0:T(8,128)(2,1)S(1)}, bf16[8,7296]{1,0:T(8,128)(2,1)S(1)}, u32[]{:S(2)}, u32[]{:S(2)}) collective-permute-start(bf16[8,7296]{1,0:T(8,128)(2,1)S(1)} %hold.3.refs_14_.refs_1_), channel_id=1, source_target_pairs={{0,4},{4,0},{8,12},{12,8},{1,5},{5,1},{9,13},{13,9},{2,6},{6,2},{1... | collective-permute-start | bytes 350216 | tf_op jit(solution)/shard_map/ppermute | solution.py:25
  19.0 2.4 %collective-permute-start.9 = (bf16[8,7296]{1,0:T(8,128)(2,1)S(1)}, bf16[8,7296]{1,0:T(8,128)(2,1)S(1)}, u32[]{:S(2)}, u32[]{:S(2)}) collective-permute-start(bf16[8,7296]{1,0:T(8,128)(2,1)S(1)} %hold.2.refs_7_), channel_id=1, source_target_pairs={{0,4},{4,0},{8,12},{12,8},{1,5},{5,1},{9,13},{13,9},{2,6},{6,2},{1... | collective-permute-start | bytes 350216 | tf_op jit(solution)/shard_map/ppermute | solution.py:25
  20.4 1.3 %collective-permute-start.14 = (bf16[8,7296]{1,0:T(8,128)(2,1)S(1)}, bf16[8,7296]{1,0:T(8,128)(2,1)S(1)}, u32[]{:S(2)}, u32[]{:S(2)}) collective-permute-start(bf16[8,7296]{1,0:T(8,128)(2,1)S(1)} %copy-done), channel_id=1, source_target_pairs={{0,4},{4,0},{8,12},{12,8},{1,5},{5,1},{9,13},{13,9},{2,6},{6,2},{1... | collective-permute-start | bytes 350216 | tf_op jit(solution)/shard_map/ppermute | solution.py:25
  20.4 1.5 %collective-permute-start.8 = (bf16[8,7296]{1,0:T(8,128)(2,1)S(1)}, bf16[8,7296]{1,0:T(8,128)(2,1)S(1)}, u32[]{:S(2)}, u32[]{:S(2)}) collective-permute-start(bf16[8,7296]{1,0:T(8,128)(2,1)S(1)} %collective-permute-done.7.refs_6_), channel_id=1, source_target_pairs={{0,4},{4,0},{8,12},{12,8},{1,5},{5,1},{9,13},{13,9},{2,6},{6,2},{1... | collective-permute-start | bytes 350216 | tf_op jit(solution)/shard_map/ppermute | solution.py:25
  20.9 1.3 %collective-permute-start.11 = (bf16[8,7296]{1,0:T(8,128)(2,1)S(1)}, bf16[8,7296]{1,0:T(8,128)(2,1)S(1)}, u32[]{:S(2)}, u32[]{:S(2)}) collective-permute-start(bf16[8,7296]{1,0:T(8,128)(2,1)S(1)} %collective-permute-done.10.refs_12_.refs_3_), channel_id=1, source_target_pairs={{0,4},{4,0},{8,12},{12,8},{1,5},{5,1},{9,13},{13,9},{2,6},{6,2},{1... | collective-permute-start | bytes 350216 | tf_op jit(solution)/shard_map/ppermute | solution.py:25
  21.0 1.4 %collective-permute-start.5 = (bf16[8,7296]{1,0:T(8,128)(2,1)S(1)}, bf16[8,7296]{1,0:T(8,128)(2,1)S(1)}, u32[]{:S(2)}, u32[]{:S(2)}) collective-permute-start(bf16[8,7296]{1,0:T(8,128)(2,1)S(1)} %collective-permute-done.4.refs_5_), channel_id=1, source_target_pairs={{0,4},{4,0},{8,12},{12,8},{1,5},{5,1},{9,13},{13,9},{2,6},{6,2},{1... | collective-permute-start | bytes 350216 | tf_op jit(solution)/shard_map/ppermute | solution.py:25
  21.4 1.3 %collective-permute-start.2 = (bf16[8,7296]{1,0:T(8,128)(2,1)S(1)}, bf16[8,7296]{1,0:T(8,128)(2,1)S(1)}, u32[]{:S(2)}, u32[]{:S(2)}) collective-permute-start(bf16[8,7296]{1,0:T(8,128)(2,1)S(1)} %collective-permute-done.1.refs_4_), channel_id=1, source_target_pairs={{0,4},{4,0},{8,12},{12,8},{1,5},{5,1},{9,13},{13,9},{2,6},{6,2},{1... | collective-permute-start | bytes 350216 | tf_op jit(solution)/shard_map/ppermute | solution.py:25
  25.1 6.7 %collective-permute-start.16 = (bf16[64,512]{1,0:T(8,128)(2,1)S(1)}, bf16[64,512]{1,0:T(8,128)(2,1)S(1)}, u32[]{:S(2)}, u32[]{:S(2)}) collective-permute-start(bf16[64,512]{1,0:T(8,128)(2,1)S(1)} %gate_up.1.refs_0_), channel_id=1, source_target_pairs={{0,3},{1,2},{2,1},{3,0},{4,7},{5,6},{6,5},{7,4},{8,11},{9,10},{10,... | collective-permute-start | bytes 196616 | tf_op jit(solution)/shard_map/ppermute | solution.py:25
  26.9 6.4 %collective-permute-start.17 = (bf16[64,512]{1,0:T(8,128)(2,1)S(1)}, bf16[64,512]{1,0:T(8,128)(2,1)S(1)}, u32[]{:S(2)}, u32[]{:S(2)}) collective-permute-start(bf16[64,512]{1,0:T(8,128)(2,1)S(1)} %gate_up.1.refs_0_), channel_id=1, source_target_pairs={{0,1},{1,0},{2,3},{3,2},{4,5},{5,4},{6,7},{7,6},{8,9},{9,8},{10,11... | collective-permute-start | bytes 196616 | tf_op jit(solution)/shard_map/ppermute | solution.py:25
  27.1 7.0 %collective-permute-start.15 = (bf16[64,512]{1,0:T(8,128)(2,1)S(1)}, bf16[64,512]{1,0:T(8,128)(2,1)S(1)}, u32[]{:S(2)}, u32[]{:S(2)}) collective-permute-start(bf16[64,512]{1,0:T(8,128)(2,1)S(1)} %gate_up.1.refs_0_), channel_id=1, source_target_pairs={{0,2},{1,3},{2,0},{3,1},{4,6},{5,7},{6,4},{7,5},{8,10},{9,11},{10,... | collective-permute-start | bytes 196616 | tf_op jit(solution)/shard_map/ppermute | solution.py:25
  34.6 1.9 %collective-permute-start.18 = (bf16[16,1792]{1,0:T(8,128)(2,1)S(1)}, bf16[16,1792]{1,0:T(8,128)(2,1)S(1)}, u32[]{:S(2)}, u32[]{:S(2)}) collective-permute-start(bf16[16,1792]{1,0:T(8,128)(2,1)S(1)} %get-tuple-element.36), channel_id=1, source_target_pairs={{0,4},{4,0},{8,12},{12,8},{1,5},{5,1},{9,13},{13,9},{2,6},{6,2},{1... | collective-permute-start | bytes 172040 | tf_op jit(solution)/shard_map/ppermute | solution.py:25
  34.7 4.3 %collective-permute-start.19 = (bf16[16,1792]{1,0:T(8,128)(2,1)S(1)}, bf16[16,1792]{1,0:T(8,128)(2,1)S(1)}, u32[]{:S(2)}, u32[]{:S(2)}) collective-permute-start(bf16[16,1792]{1,0:T(8,128)(2,1)S(1)} %get-tuple-element.37), channel_id=1, source_target_pairs={{0,8},{4,12},{8,0},{12,4},{1,9},{5,13},{9,1},{13,5},{2,10},{6,14},... | collective-permute-start | bytes 172040 | tf_op jit(solution)/shard_map/ppermute | solution.py:25
  36.3 3.9 %collective-permute-start.20 = (bf16[16,1792]{1,0:T(8,128)(2,1)S(1)}, bf16[16,1792]{1,0:T(8,128)(2,1)S(1)}, u32[]{:S(2)}, u32[]{:S(2)}) collective-permute-start(bf16[16,1792]{1,0:T(8,128)(2,1)S(1)} %get-tuple-element.38), channel_id=1, source_target_pairs={{0,12},{4,8},{8,4},{12,0},{1,13},{5,9},{9,5},{13,1},{2,14},{6,10},... | collective-permute-start | bytes 172040 | tf_op jit(solution)/shard_map/ppermute | solution.py:25
  40.4 5.8 %collective-permute-start.21 = (bf16[8,1792]{1,0:T(8,128)(2,1)S(1)}, bf16[8,1792]{1,0:T(8,128)(2,1)S(1)}, u32[]{:S(2)}, u32[]{:S(2)}) collective-permute-start(bf16[8,1792]{1,0:T(8,128)(2,1)S(1)} %get-tuple-element.39), channel_id=1, source_target_pairs={{0,3},{1,2},{2,1},{3,0},{4,7},{5,6},{6,5},{7,4},{8,11},{9,10},{10,... | collective-permute-start | bytes 86024 | tf_op jit(solution)/shard_map/ppermute | solution.py:25
  42.3 4.8 %collective-permute-start.22 = (bf16[8,1792]{1,0:T(8,128)(2,1)S(1)}, bf16[8,1792]{1,0:T(8,128)(2,1)S(1)}, u32[]{:S(2)}, u32[]{:S(2)}) collective-permute-start(bf16[8,1792]{1,0:T(8,128)(2,1)S(1)} %get-tuple-element.40), channel_id=1, source_target_pairs={{0,2},{1,3},{2,0},{3,1},{4,6},{5,7},{6,4},{7,5},{8,10},{9,11},{10,... | collective-permute-start | bytes 86024 | tf_op jit(solution)/shard_map/ppermute | solution.py:25
  42.3 4.8 %collective-permute-start.23 = (bf16[8,1792]{1,0:T(8,128)(2,1)S(1)}, bf16[8,1792]{1,0:T(8,128)(2,1)S(1)}, u32[]{:S(2)}, u32[]{:S(2)}) collective-permute-start(bf16[8,1792]{1,0:T(8,128)(2,1)S(1)} %get-tuple-element.41), channel_id=1, source_target_pairs={{0,1},{1,0},{2,3},{3,2},{4,5},{5,4},{6,7},{7,6},{8,9},{9,8},{10,11... | collective-permute-start | bytes 86024 | tf_op jit(solution)/shard_map/ppermute | solution.py:25
